TPU v7x, 128 devices: a whole 4x4x4 slice. The times are simulated.
128 devices in a mesh: lat: 16 (over y, z_hi, core), lev: 8 (over x, z_lo).
Axes of the slice: x: 4, y: 4, z: 4 (z_hi: 2, z_lo: 2; z = z_hi * 2 + z_lo), core: 2. Of those that a mesh axis runs over, the one named last changes fastest.
Arguments:
- tracers: float32 [4, 72, 64, 1440], P(None, 'lev', 'lat'), may hold values from -6 to 6
- zonal: float32 [72, 64, 1440], P('lev', 'lat'), may hold values from -0.6 to 0.6
- meridional: float32 [72, 64, 1440], P('lev', 'lat'), may hold values from -0.5 to 0.5
- vertical: float32 [72, 64, 1440], P(None, 'lat', 'lev'), may hold values from -0.5 to 0.5
- route: int32 [64, 1440, 1], P('lat', 'lev'), may hold values from 0 to 127; in each aligned block of 180 rows (0 to 179, 180 to 359, ..., all dimensions but the last counted through in order) at most 3 rows name the same one
- inverse: float32 [16, 8, 288, 288], P('lat', 'lev'), may hold values from -0.5 to 1
Outputs:
- tendency: float32 [4, 72, 64, 1440], P(None, 'lev', 'lat')
Inputs may be any that keep to these rules, and one draw needn't show every extreme that they name: `route`: in each latitude row and each group of 180 longitudes with equal b // 180, at most 3 columns name one span.
All inputs are finite; a program needn't handle non-finite values.
Results may differ from a plain program's by a relative error of at most 0.0003.
Values sent between devices are 32-bit elements; how exact they have to be, the bound alone decides.
A program may use at most 64 MiB of HBM per device.

v0:
```python
import jax
import jax.numpy as jnp
from jax import lax
from jax.sharding import PartitionSpec as P


def padded_2(cells, sides, width):
    for axis, dim in sides:
        count = lax.axis_size(axis)
        ends = count - 1
        head = lax.slice_in_dim(cells, 0, width, axis=dim)
        tail = lax.slice_in_dim(cells, cells.shape[dim] - width, cells.shape[dim], axis=dim)
        cells = jnp.concatenate(
            [
                lax.ppermute(tail, axis, [(i, (i + 1) % count) for i in range(ends)]),
                cells,
                lax.ppermute(head, axis, [((i + 1) % count, i) for i in range(ends)]),
            ],
            axis=dim,
        )
    return cells


def take_range(values, start, finish, axis):
    return lax.slice_in_dim(values, start, finish, axis=axis)


def edge_change(padded, courant, axis, cells):
    faces = (
        7.0
        / 12.0
        * (take_range(padded, 1, cells + 4, axis) + take_range(padded, 2, cells + 5, axis))
    )
    faces = faces - 1.0 / 12.0 * (
        take_range(padded, 0, cells + 3, axis) + take_range(padded, 3, cells + 6, axis)
    )
    left_face = take_range(faces, 0, cells + 2, axis)
    right_face = take_range(faces, 1, cells + 3, axis)
    centre = take_range(padded, 2, cells + 4, axis)
    slope_term = right_face - left_face
    curvature = 6.0 * (centre - 0.5 * (left_face + right_face))
    from_low = courant * (
        take_range(right_face, 0, cells + 1, axis)
        - 0.5
        * courant
        * (
            take_range(slope_term, 0, cells + 1, axis)
            - (1.0 - 2.0 * courant / 3.0) * take_range(curvature, 0, cells + 1, axis)
        )
    )
    reverse = -courant
    from_high = courant * (
        take_range(left_face, 1, cells + 2, axis)
        + 0.5
        * reverse
        * (
            take_range(slope_term, 1, cells + 2, axis)
            + (1.0 - 2.0 * reverse / 3.0) * take_range(curvature, 1, cells + 2, axis)
        )
    )
    edge_flux = jnp.where(courant >= 0.0, from_low, from_high)
    return take_range(edge_flux, 0, cells, axis) - take_range(edge_flux, 1, cells + 1, axis)


def apply_matrix(matrix, received):
    return jnp.einsum("abo,po->abp", received, matrix, precision=lax.Precision.HIGHEST)


def body(tracers, zonal, meridional, vertical, route, inverse):
    tracer_count, level_block, row_count, lon_count = tracers.shape
    rim_tracers = jnp.concatenate([tracers[:, :, :3], tracers[:, :, -3:]], axis=2)
    rim_courant = jnp.concatenate([meridional[:, :3], meridional[:, -3:]], axis=1)[None]
    rim_rows = jnp.concatenate([rim_tracers, rim_courant], axis=0)
    extended = padded_2(rim_rows, (("lat", 2),), 3)
    lon_padded = jnp.concatenate([tracers[..., -3:], tracers, tracers[..., :3]], axis=3)
    lon_courant = jnp.concatenate([zonal, zonal[:, :, :1]], axis=2)
    lon_change = edge_change(lon_padded, lon_courant, 3, lon_count)
    below_rows = extended[:tracer_count, :, 0:3]
    above_rows = extended[:tracer_count, :, 9:12]
    north_face = extended[tracer_count, :, 9:10]
    lat_padded = jnp.concatenate([below_rows, tracers, above_rows], axis=2)
    row_index = jnp.arange(row_count, dtype=jnp.int32)[None, :, None]
    at_pole = jnp.logical_and(lax.axis_index("lat") == 0, row_index == 0)
    south_faces = jnp.where(at_pole, 0.0, meridional)
    lat_courant = jnp.concatenate([south_faces, north_face], axis=1)
    lat_change = edge_change(lat_padded, lat_courant, 2, row_count)
    horizontal = tracers + lon_change + lat_change
    columns = lax.all_to_all(horizontal, "lev", split_axis=3, concat_axis=1, tiled=True)
    level_count = columns.shape[1]
    lon_local = columns.shape[3]
    vert_padded = jnp.pad(columns, ((0, 0), (3, 3), (0, 0), (0, 0)))
    zero_level = jnp.zeros_like(vertical[:1])
    vert_courant = jnp.concatenate([zero_level, vertical[1:], zero_level], axis=0)
    advected = columns + edge_change(vert_padded, vert_courant, 1, level_count)
    targets = route[:, :, 0]
    band_count = lax.axis_size("lat")
    group_count = lax.axis_size("lev")
    span_count = band_count * group_count
    capacity = max(2, (2 * lon_local + span_count - 1) // span_count)
    order_size = tracer_count * level_count
    span_ids = jnp.arange(span_count, dtype=jnp.int32)
    member = (targets[:, :, None] == span_ids[None, None, :]).astype(jnp.int32)
    ranking = jnp.sum((jnp.cumsum(member, axis=1) - 1) * member, axis=2)
    slot_of = targets * capacity + ranking
    slot_ids = jnp.arange(span_count * capacity, dtype=jnp.int32)
    selector = (slot_of[:, :, None] == slot_ids[None, None, :]).astype(jnp.float32)
    packed = jnp.einsum("tkrl,rls->srtk", advected, selector, precision=lax.Precision.HIGHEST)
    packed = packed.reshape(span_count, capacity * row_count, order_size)
    matrix = inverse[0, 0]
    mixed = apply_matrix(
        matrix, lax.all_to_all(packed, ("lat", "lev"), split_axis=0, concat_axis=0, tiled=True)
    )
    returned = lax.all_to_all(mixed, ("lat", "lev"), split_axis=0, concat_axis=0, tiled=True)
    flat_slots = returned.reshape(span_count * capacity, row_count, tracer_count, level_count)
    diffused = jnp.einsum("srtk,rls->tkrl", flat_slots, selector, precision=lax.Precision.HIGHEST)
    level_form = lax.all_to_all(diffused, "lev", split_axis=1, concat_axis=3, tiled=True)
    return level_form - tracers


def solution(mesh):
    in_specs = (
        P(None, "lev", "lat", None),
        P("lev", "lat", None),
        P("lev", "lat", None),
        P(None, "lat", "lev"),
        P("lat", "lev", None),
        P("lat", "lev", None, None),
    )
    out_specs = P(None, "lev", "lat", None)
    return jax.shard_map(body, mesh=mesh, in_specs=in_specs, out_specs=out_specs, check_vma=False)
```

profile of v0, /device:TPU:24, one launch (start us, length us, event | category | flops | bytes accessed | tf_op | source)
XLA Modules:
  0.0 276.9 jit_solution(17675126299534039594)
XLA Ops:
  0.0 1.6 copy.308
  2.5 0.8 copy.311
  3.8 1.8 pad_maximum_fusion.1
  5.6 5.4 %collective-permute-start = (f32[5,9,3,1440]{3,1,2,0:T(8,128)}, f32[5,9,3,1440]{3,1,2,0:T(8,128)}, u32[]{:S(2)}, u32[]{:S(2)}) collective-permute-start(f32[5,9,3,1440]{3,1,2,0:T(8,128)} %get-tuple-element.8), channel_id=1, source_target_pairs={{8,0},{16,8},{24,16},{32,24},{40,32},{48,40},{56,48},{64,56},{72,6... | collective-permute-start | bytes 2332808 | tf_op jit(solution)/shard_map/ppermute | solution.py:17
  11.0 1.9 collective-permute-start.1
  13.8 1.6 concatenate.82
  15.3 2.4 fusion.40
  17.8 2.2 slice_subtract_fusion.7
  20.1 1.1 broadcast_multiply_fusion.2
  21.8 0.8 copy-done.5
  22.6 0.6 slice_bitcast_fusion.1
  23.2 1.3 reduce-window.9
  24.5 3.2 %fusion.33 = f32[4,9,4,1441]{3,2,1,0:T(4,128)S(1)} fusion(f32[4,9,4,1442]{3,2,1,0:T(4,128)} %get-tuple-element.14, f32[4,9,4,1442]{3,2,1,0:T(4,128)S(1)} %copy-done.4, f32[4,9,4,1443]{3,2,1,0:T(4,128)S(1)} %fusion.40, f32[9,4,1441]{2,1,0:T(4,128)} %get-tuple-element.32, f32[9,4,1441]{2,1,0:T(4,128)} %get-tuple-element.30, ...), kind=kLoop, calls=%fused_computation.55 | loop fusion | flops 2282544 | bytes 6069492 | tf_op jit(solution)/shard_map/jit(_where)/select_n | solution.py:61
  27.6 0.6 collective-permute-done
  28.3 1.4 slice.254
  30.5 4.0 %collective-permute-done.1 = f32[5,9,3,1440]{3,1,2,0:T(8,128)} collective-permute-done((f32[5,9,3,1440]{3,1,2,0:T(8,128)}, f32[5,9,3,1440]{3,1,2,0:T(8,128)}, u32[]{:S(2)}, u32[]{:S(2)}) %collective-permute-start.1) | collective-permute-done | bytes 777632 | tf_op jit(solution)/shard_map/ppermute | solution.py:15
  34.6 1.4 slice.253
  36.8 0.9 slice_bitcast_fusion
  38.1 0.8 copy-done.3
  39.4 0.9 pad_maximum_fusion
  40.2 1.0 fusion.13
  41.2 0.6 slice_subtract_fusion.1
  42.8 1.2 fusion.6
  44.0 0.6 fusion.27
  44.6 8.8 %copy.329 = f32[4,9,4,1440]{1,2,0,3:T(4,128)} copy(f32[4,9,4,1440]{3,2,1,0:T(4,128)S(1)} %fusion.27) | data formatting | bytes 1658880 | tf_op jit(solution)/shard_map/add | solution.py:87
  53.4 14.4 %reshape.216 = f32[8,1,25920]{2,1,0:T(1,128)} reshape(f32[1440,4,4,9]{3,2,1,0:T(4,128)} %bitcast.47) | data formatting | bytes 1658880
  67.8 4.9 %all-to-all-start = ((f32[8,1,25920]{2,1,0:T(1,128)}), f32[8,1,25920]{2,1,0:T(1,128)S(1)}, u32[]{:S(2)}, u32[]{:S(2)}) async-start(f32[8,1,25920]{2,1,0:T(1,128)} %reshape.216), calls=%async_computation | async-start | bytes 1662976 | tf_op jit(solution)/shard_map/all_to_all | solution.py:88
  73.5 1.3 pad_maximum_fusion.5
  74.8 7.8 %all-to-all-done = f32[8,1,25920]{2,1,0:T(1,128)S(1)} async-done(((f32[8,1,25920]{2,1,0:T(1,128)}), f32[8,1,25920]{2,1,0:T(1,128)S(1)}, u32[]{:S(2)}, u32[]{:S(2)}) %all-to-all-start) | async-done | bytes 829472 | tf_op jit(solution)/shard_map/all_to_all | solution.py:88
  83.1 2.6 reduce
  85.7 20.0 %reshape.217 = f32[1440,4,4,9]{3,2,1,0:T(4,128)} reshape(f32[8,25920]{1,0:T(8,128)S(1)} %reduce) | data formatting | bytes 1658880
  105.8 11.5 %copy.330 = f32[4,9,4,8,180]{4,2,1,3,0:T(4,128)S(1)} copy(f32[4,9,4,8,180]{1,2,0,4,3:T(4,128)} %bitcast.48) | data formatting | bytes 1658880 | tf_op jit(solution)/shard_map/all_to_all | solution.py:88
  117.7 0.6 slice_subtract_fusion.3
  118.9 1.2 fusion.19
  120.8 1.2 fusion.26
  122.1 2.9 %copy.332 = f32[384,4,4,72]{3,2,1,0:T(4,128)} copy(f32[384,4,4,72]{0,3,2,1:T(8,128)S(1)} %bitcast.53) | data formatting | bytes 3538944 | tf_op jit(solution)/shard_map/tkrl,rls->srtk/transpose | solution.py:107
  125.0 5.1 %reshape.208 = f32[128,12,288]{2,1,0:T(8,128)} reshape(f32[384,4,4,72]{3,2,1,0:T(4,128)} %copy.332) | data formatting | bytes 3538944 | tf_op jit(solution)/shard_map/reshape | solution.py:108
  130.1 59.4 %all_to_all.46 = f32[128,12,288]{2,1,0:T(8,128)S(1)} all-to-all(f32[128,12,288]{2,1,0:T(8,128)} %reshape.208), channel_id=1, replica_groups=mesh['lat'=16,'lev'=8] {'lat','lev'}, dimensions={0} | all-to-all | bytes 3538944 | tf_op jit(solution)/shard_map/all_to_all | solution.py:111
  189.5 3.7 %fusion = f32[128,12,288]{0,2,1:T(8,128)S(1)} fusion(f32[128,12,288]{2,1,0:T(8,128)S(1)} %all_to_all.46, f32[1,1,288,288]{3,2,1,0:T(8,128)S(1)} %copy-done), kind=kOutput, calls=%fused_computation.3 | convolution fusion | flops 1528823808 | bytes 3870720 | tf_op jit(solution)/shard_map/abo,po->abp/dot_general | solution.py:66
  193.3 2.6 copy.334
  195.9 47.3 %all_to_all.47 = f32[128,12,288]{2,1,0:T(8,128)} all-to-all(f32[128,12,288]{2,1,0:T(8,128)} %copy.334), channel_id=1, replica_groups=mesh['lat'=16,'lev'=8] {'lat','lev'}, dimensions={0} | all-to-all | bytes 3538944 | tf_op jit(solution)/shard_map/all_to_all | solution.py:113
  243.2 5.1 %reshape.209 = f32[384,4,4,72]{3,2,1,0:T(4,128)} reshape(f32[128,12,288]{2,1,0:T(8,128)} %all_to_all.47) | data formatting | bytes 3538944 | tf_op jit(solution)/shard_map/reshape | solution.py:114
  248.3 3.2 %copy.335 = f32[384,4,4,72]{0,3,2,1:T(8,128)S(1)} copy(f32[384,4,4,72]{3,2,1,0:T(4,128)} %reshape.209) | data formatting | bytes 3538944 | tf_op jit(solution)/shard_map/reshape | solution.py:114
  251.5 1.3 fusion.25
  253.3 20.6 %all_to_all.48 = f32[4,72,4,180]{3,0,2,1:T(4,128)S(1)} all-to-all(f32[4,72,4,180]{3,0,2,1:T(4,128)S(1)} %copy.336), channel_id=1, replica_groups=mesh['lat'=16,'lev'=8] {'lev'}, dimensions={1} | all-to-all | bytes 1658880 | tf_op jit(solution)/shard_map/all_to_all | solution.py:116
  273.9 0.7 copy.338
  274.6 0.9 all_to_all.41
  275.5 1.1 sub.128
  (77 shorter events, 9.8 us)
Async XLA Ops:
  0.0 189.5 %copy-start = (f32[1,1,288,288]{3,2,1,0:T(8,128)S(1)}, f32[1,1,288,288]{3,2,1,0:T(8,128)}, u32[]{:S(2)}) copy-start(f32[1,1,288,288]{3,2,1,0:T(8,128)} %param.11) | copy-start | bytes 995332
  1.6 0.9 copy-start.2
  2.5 0.9 copy-start.7
  3.8 9.2 %copy-start.1 = (f32[4,9,4,1440]{3,2,1,0:T(4,128)S(1)}, f32[4,9,4,1440]{3,2,1,0:T(4,128)}, u32[]{:S(2)}) copy-start(f32[4,9,4,1440]{3,2,1,0:T(4,128)} %param.6) | copy-start | bytes 2488324
  5.6 22.6 %collective-permute-start = (f32[5,9,3,1440]{3,1,2,0:T(8,128)}, f32[5,9,3,1440]{3,1,2,0:T(8,128)}, u32[]{:S(2)}, u32[]{:S(2)}) collective-permute-start(f32[5,9,3,1440]{3,1,2,0:T(8,128)} %get-tuple-element.8), channel_id=1, source_target_pairs={{8,0},{16,8},{24,16},{32,24},{40,32},{48,40},{56,48},{64,56},{72,6... | collective-permute-start | bytes 2332808 | tf_op jit(solution)/shard_map/ppermute | solution.py:17
  11.0 23.5 %collective-permute-start.1 = (f32[5,9,3,1440]{3,1,2,0:T(8,128)}, f32[5,9,3,1440]{3,1,2,0:T(8,128)}, u32[]{:S(2)}, u32[]{:S(2)}) collective-permute-start(f32[5,9,3,1440]{3,1,2,0:T(8,128)} %get-tuple-element.7), channel_id=1, source_target_pairs={{0,8},{8,16},{16,24},{24,32},{32,40},{40,48},{48,56},{56,64},{64,7... | collective-permute-start | bytes 2332808 | tf_op jit(solution)/shard_map/ppermute | solution.py:15
  13.1 0.6 copy-start.13
  13.1 0.6 copy-start.14
  17.7 2.2 copy-start.16
  17.8 2.2 slice-start
  19.9 1.2 copy-start.17
  20.0 1.3 copy-start.8
  20.1 4.4 %copy-start.4 = (f32[4,9,4,1442]{3,2,1,0:T(4,128)S(1)}, f32[4,9,4,1442]{3,2,1,0:T(4,128)}, u32[]{:S(2)}) copy-start(f32[4,9,4,1442]{3,2,1,0:T(4,128)} %get-tuple-element.13) | copy-start | bytes 2491780
  21.8 0.8 copy-start.5
  37.7 1.2 copy-start.3
  67.8 4.9 %copy-start.6 = (s32[4,128,2,128]{1,2,3,0:T(2,128)S(1)}, s32[4,128,2,128]{1,2,3,0:T(2,128)}, u32[]{:S(2)}) copy-start(s32[4,128,2,128]{1,2,3,0:T(2,128)} %copy-done.5) | copy-start | bytes 1572868
  67.8 4.9 %slice-start.1 = ((s32[4,128,3]{1,2,0:T(4,128)}), s32[4,128,2]{1,2,0:T(2,128)S(1)}, s32[]{:S(2)}) async-start(s32[4,128,3]{1,2,0:T(4,128)} %reduce-window.9), calls=%async_computation.5 | async-start | bytes 8192 | tf_op jit(solution)/shard_map/slice.1
  67.8 5.1 %copy-start.15 = (f32[72,4,180]{2,1,0:T(4,128)S(1)}, f32[72,4,180]{2,1,0:T(4,128)}, u32[]{:S(2)}) copy-start(f32[72,4,180]{2,1,0:T(4,128)} %param.9) | copy-start | bytes 622084
  67.8 14.8 %all-to-all-start = ((f32[8,1,25920]{2,1,0:T(1,128)}), f32[8,1,25920]{2,1,0:T(1,128)S(1)}, u32[]{:S(2)}, u32[]{:S(2)}) async-start(f32[8,1,25920]{2,1,0:T(1,128)} %reshape.216), calls=%async_computation | async-start | bytes 1662976 | tf_op jit(solution)/shard_map/all_to_all | solution.py:88
  117.7 1.0 copy-start.9
  117.7 1.0 copy-start.10
  117.7 1.1 copy-start.11
  117.7 1.2 copy-start.12
where the time goes:
time: 282 us; the launch traced here: 277 us
  blocking collectives  127 us (45%)
  local copies, waits for them, and re-layouts  91.3 us (32%)
  other arithmetic  26.5 us (9%)
  waiting for transfers between devices  12.4 us (4%)
  starting transfers between devices  12.2 us (4%)
  matrix products  6.31 us (2%)
    all_to_all x1, blocking collectives, body(): lax.all_to_all(packed, ('lat', 'lev'), split_axis=0, concat_axis=0, tiled...  59.4 us
    all_to_all x1, blocking collectives, body(): lax.all_to_all(mixed, ('lat', 'lev'), split_axis=0, concat_axis=0, tiled=...  47.3 us
    unnamed x43, local copies, waits for them, and re-layouts  40.2 us
    all_to_all x1, blocking collectives, body(): lax.all_to_all(diffused, 'lev', split_axis=1, concat_axis=3, tiled=True)  20.6 us
    all_to_all x2, local copies, waits for them, and re-layouts, body(): lax.all_to_all(horizontal, 'lev', split_axis=3, concat_axis=1, tiled=True)  12 us
    add x1, local copies, waits for them, and re-layouts, body(): horizontal = tracers + lon_change + lat_change  8.8 us
    reshape x2, local copies, waits for them, and re-layouts, body(): returned.reshape(span_count * capacity, row_count, tracer_count, level_co...  8.37 us
    all_to_all x1, waiting for transfers between devices, body(): lax.all_to_all(horizontal, 'lev', split_axis=3, concat_axis=1, tiled=True)  7.8 us
  transfers between devices with their start and end apart: 3, of which 3 were waited for; matrix products, arithmetic and copies ran while one was open for 6% of the time, Pallas kernels for 0%

commit v1 on v0

v1 whole, which is shorter than its diff:
```python
import functools
import jax
import jax.numpy as jnp
from jax import lax
from jax.experimental import pallas as pl
from jax.experimental.pallas import tpu as pltpu
from jax.sharding import PartitionSpec as P

MESH = pl.DeviceIdType.MESH
F32 = jnp.float32
BF16 = jnp.bfloat16
VMEM = pl.BlockSpec(memory_space=pltpu.VMEM)
NT = (((1,), (1,)), ((), ()))
NN = (((1,), (0,)), ((), ()))


def dot(a, b, dims=NN):
    return lax.dot_general(a, b, dims, preferred_element_type=F32)


def split(x):
    hi = x.astype(BF16)
    lo = (x - hi.astype(F32)).astype(BF16)
    return hi, lo


def flux(c, e, s_low, s_here, k_low, k_here):
    up = c >= 0.0
    a = jnp.abs(c)
    s = jnp.where(up, -s_low, s_here)
    k = jnp.where(up, k_low, k_here)
    return c * (e + (0.5 * a) * (s + (1.0 - (2.0 / 3.0) * a) * k))


def face(q_m2, q_m1, q_0, q_p1):
    return (7.0 / 12.0) * (q_m1 + q_0) - (1.0 / 12.0) * (q_m2 + q_p1)


def horizontal_kernel(tr_ref, south_ref, north_ref, zon_ref, mer_ref, mern_ref, g_ref):
    lat = lax.axis_index("lat")
    last = lax.axis_size("lat") - 1
    width = tr_ref.shape[3]
    groups = g_ref.shape[0]
    lon = width // groups
    sub = lax.broadcasted_iota(jnp.int32, (8, width), 0) < 4
    ext = -(-width // 128) * 128
    spare = ext - width
    half = spare // 3
    ksouth = (lat > 0).astype(F32)
    knorth = (lat < last).astype(F32)

    def swap(x):
        return pltpu.roll(x, 4, 0)

    def extend(x):
        return jnp.concatenate([x, x[:, :half], x[:, width - (spare - half):]], axis=1)

    def rolled(x, n):
        return pltpu.roll(x, n % ext, 1)

    def level(k, carry):
        row = [tr_ref[r, k] for r in range(4)]
        low = [south_ref[r, k] * ksouth for r in range(3)]
        high = [north_ref[r, k] * knorth for r in range(3)]
        pair = lambda a, b: jnp.concatenate([a, b], axis=0)
        q = [
            pair(low[0], low[0]),
            pair(low[1], low[2]),
            pair(row[0], row[1]),
            pair(row[2], row[3]),
            pair(high[0], high[1]),
            pair(high[2], high[2]),
        ]
        sq = [swap(x) for x in q]
        e = [face(q[p - 1], jnp.where(sub, sq[p - 1], sq[p]), q[p], jnp.where(sub, sq[p], sq[p + 1])) for p in range(1, 5)]
        se = [swap(x) for x in e]
        s, kk = [], []
        for p in range(4):
            right = jnp.where(sub, se[p], se[min(p + 1, 3)])
            s.append(right - e[p])
            kk.append(6.0 * q[p + 1] - 3.0 * (e[p] + right))
        ss = [swap(x) for x in s]
        sk = [swap(x) for x in kk]
        m = mer_ref[k]
        zero = jnp.zeros((8, width), F32)
        m0 = jnp.where(sub, m[0:1] * ksouth, m[1:2])
        m1 = jnp.where(sub, m[2:3], m[3:4])
        m2 = mern_ref[k] * knorth + zero
        f = []
        for i, c in enumerate((m0, m1, m2)):
            p = i + 1
            f.append(
                flux(c, e[p], jnp.where(sub, ss[p - 1], ss[p]), s[p], jnp.where(sub, sk[p - 1], sk[p]), kk[p])
            )
        sf = [swap(x) for x in f]
        z = zon_ref[k]
        out = []
        for p in range(2):
            lat_change = f[p] - jnp.where(sub, sf[p], sf[p + 1])
            x = extend(q[p + 2])
            c = extend(jnp.where(sub, z[2 * p : 2 * p + 1], z[2 * p + 1 : 2 * p + 2]))
            le = face(rolled(x, 2), rolled(x, 1), x, rolled(x, -1))
            right = rolled(le, -1)
            ls = right - le
            lk = 6.0 * x - 3.0 * (le + right)
            lf = flux(c, le, rolled(ls, 1), ls, rolled(lk, 1), lk)
            lon_change = lf - rolled(lf, -1)
            out.append(q[p + 2] + lon_change[:, :width] + lat_change)
        rest = lon - 128
        pad = jnp.zeros((8, 128 - 2 * rest), F32)
        for g in range(groups):
            o = g * lon
            g_ref[g, k] = jnp.concatenate(
                [
                    out[0][:, o : o + 128],
                    out[1][:, o : o + 128],
                    out[0][:, o + 128 : o + lon],
                    out[1][:, o + 128 : o + lon],
                    pad,
                ],
                axis=1,
            )
        return carry

    lax.fori_loop(0, tr_ref.shape[1], level, 0)


def selector(slot_ref, r):
    ids = lax.broadcasted_iota(jnp.int32, (512, 256), 0)
    return (ids == slot_ref[r : r + 1, :]).astype(F32).astype(BF16)


def select_kernel(rest, g_ref, c_ref, slot_ref, p_ref, a_ref):
    levels = g_ref.shape[0]
    sub = lax.broadcasted_iota(jnp.int32, (8, 384), 0) < 4
    half = lax.broadcasted_iota(jnp.int32, (8, 256), 0) < 4
    zero = jnp.zeros((8, 384), F32)
    for r in range(4):
        if r > 0:
            a_ref[r, 0 : 32 * r, :] = jnp.zeros((32 * r, 512), BF16)
        if r < 3:
            a_ref[r, 32 * r + 288 : 384, :] = jnp.zeros((96 - 32 * r, 512), BF16)

    def q(k):
        return g_ref[k] if 0 <= k < levels else zero

    def e_at(k):
        return face(q(k - 2), q(k - 1), q(k), q(k + 1))

    left = e_at(0)
    f_here = zero
    held = []
    right = e_at(1)
    s, kk = right - left, 6.0 * q(0) - 3.0 * (left + right)
    for k in range(levels):
        if k + 1 < levels:
            nxt = e_at(k + 2)
            s1, k1 = nxt - right, 6.0 * q(k + 1) - 3.0 * (right + nxt)
            c = jnp.where(sub, c_ref[k + 1, 0:1, :], c_ref[k + 1, 1:2, :])
            f_next = flux(c, right, s, s1, kk, k1)
            right, s, kk = nxt, s1, k1
        else:
            f_next = zero
        held.append(q(k) + f_here - f_next)
        f_here = f_next
        if k % 4 == 3:
            for rp in range(2):
                x = []
                for h in held:
                    third = h[:, 256:384]
                    if rp == 1:
                        third = pltpu.roll(third, 128 - rest, 1)
                    x.append(jnp.concatenate([h[:, 128 * rp : 128 * rp + 128], third], axis=1))
                t = [pltpu.roll(v, 4, 0) for v in x]
                first = [jnp.where(half, x[0], t[1]), jnp.where(half, x[2], t[3])]
                second = [jnp.where(half, t[0], x[1]), jnp.where(half, t[2], x[3])]
                for r2, rows in enumerate((first, second)):
                    r = 2 * rp + r2
                    hi, lo = split(jnp.concatenate(rows, axis=0))
                    at = 32 * r + 4 * (k - 3)
                    a_ref[r, at : at + 16, 0:256] = hi
                    a_ref[r, at : at + 16, 256:512] = lo
            held = []
    carried = None
    for r in range(4):
        one = selector(slot_ref, r)
        out = dot(jnp.concatenate([one, one], axis=1), a_ref[r], NT)
        for t in range(3):
            part = out[:, 128 * t : 128 * t + 128]
            if t == 0 and r > 0:
                part = part + carried
            if t == 2 and r < 3:
                carried = part
                continue
            p_ref[2 * r + t] = part.reshape(p_ref.shape[1:])


def reorder_kernel(m_ref, o_ref):
    order = m_ref.shape[0]
    levels = order // 4
    x = lax.broadcasted_iota(jnp.int32, (order, order), 0)
    o = lax.broadcasted_iota(jnp.int32, (order, order), 1)
    pick = ((x & 3) * levels + (x >> 2) == o).astype(F32)
    exact = dict(precision=lax.Precision.HIGHEST, preferred_element_type=F32)
    o_ref[...] = lax.dot_general(lax.dot_general(pick, m_ref[...], NN, **exact), pick, NT, **exact)


def route_kernel(lats, levs, p_ref, m_ref, v_ref, r_ref, y_ref, w_ref, ssem, rsem, lsem):
    lat, lev = lax.axis_index("lat"), lax.axis_index("lev")
    order = m_ref.shape[1]
    spans = m_ref.shape[0]
    barrier = pltpu.get_barrier_semaphore()
    for i in range(1, levs):
        pl.semaphore_signal(barrier, inc=1, device_id=(lat, lax.rem(lev + i, levs)), device_id_type=MESH)
    pl.semaphore_wait(barrier, levs - 1)

    def out_copy(i):
        to = lax.rem(lev + i, levs)
        return pltpu.make_async_remote_copy(
            src_ref=p_ref.at[:, to, :, 0:3],
            dst_ref=r_ref.at[:, :, lev, 0:3],
            send_sem=ssem.at[0, i],
            recv_sem=rsem.at[0, i],
            device_id=(lat, to),
            device_id_type=MESH,
        )

    def back_copy(i):
        to = lax.rem(lev + i, levs)
        return pltpu.make_async_remote_copy(
            src_ref=y_ref.at[:, :, to, 0:3],
            dst_ref=v_ref.at[:, lev, :, 0:3],
            send_sem=ssem.at[1, i],
            recv_sem=rsem.at[1, i],
            device_id=(lat, to),
            device_id_type=MESH,
        )

    own_out = pltpu.make_async_copy(p_ref.at[:, lev, :, 0:3], r_ref.at[:, :, lev, 0:3], lsem.at[0])
    own_back = pltpu.make_async_copy(y_ref.at[:, :, lev, 0:3], v_ref.at[:, lev, :, 0:3], lsem.at[1])
    own_out.start()
    for i in range(1, levs):
        out_copy(i).start()

    @pl.loop(0, spans)
    def _(n):
        hi, lo = split(m_ref[n])
        w_ref[0, n] = hi
        w_ref[1, n] = lo

    own_out.wait()
    for i in range(1, levs):
        out_copy(i).wait()

    @pl.loop(0, spans)
    def _(n):
        tiles = [r_ref[j, n].reshape(4 * levs, 128) for j in range(9)]
        rows = []
        for r in range(4):
            x = jnp.concatenate(tiles[2 * r : 2 * r + 3], axis=1)
            if r > 0:
                x = pltpu.roll(x, 384 - 32 * r, 1)
            rows.append(x[:, :order])
        hi, lo = split(jnp.concatenate(rows, axis=0))
        y = dot(hi, w_ref[0, n], NT) + dot(lo, w_ref[0, n], NT) + dot(hi, w_ref[1, n], NT)
        size = 4 * levs
        carried = None
        for r in range(4):
            x = jnp.concatenate([y[r * size : (r + 1) * size], jnp.zeros((size, 384 - order), F32)], axis=1)
            if r > 0:
                x = pltpu.roll(x, 32 * r, 1)
            for t in range(3):
                part = x[:, 128 * t : 128 * t + 128]
                if t == 0 and r > 0:
                    part = part + carried
                if t == 2 and r < 3:
                    carried = part
                    continue
                y_ref[2 * r + t, n] = part.reshape(levs, 4, 128)

    own_back.start()
    for i in range(1, levs):
        back_copy(i).start()
    own_back.wait()
    for i in range(1, levs):
        back_copy(i).wait()


def unselect_kernel(rest, v_ref, slot_ref, d_ref):
    lane = lax.broadcasted_iota(jnp.int32, (128, 512), 1)
    live = (lane & 3) < 3
    turned = [jnp.where(live, v_ref[j].reshape(512, 128).T, 0.0) for j in range(9)]
    turned = jnp.concatenate(turned, axis=0)
    whole = []
    for r in range(4):
        hi, lo = split(turned[288 * r : 288 * r + 288])
        one = selector(slot_ref, r)
        whole.append(dot(jnp.concatenate([hi, lo], axis=1), jnp.concatenate([one, one], axis=0)))
    sub = lax.broadcasted_iota(jnp.int32, (8, 256), 0) < 4
    lane = lax.broadcasted_iota(jnp.int32, (8, 128), 1)
    for n in range(d_ref.shape[0] // 2):
        even, odd = [], []
        for rp in range(2):
            x = whole[2 * rp][8 * n : 8 * n + 8]
            y = whole[2 * rp + 1][8 * n : 8 * n + 8]
            even.append(jnp.where(sub, x, pltpu.roll(y, 4, 0)))
            odd.append(jnp.where(sub, pltpu.roll(x, 4, 0), y))
        for i, (a, b) in enumerate((even, odd)):
            third = jnp.where(lane < rest, a[:, 128:], pltpu.roll(b[:, 128:], rest, 1))
            d_ref[2 * n + i] = jnp.concatenate([a[:, :128], b[:, :128], third], axis=1)


def assemble_kernel(lon, d_ref, o_ref):
    groups = d_ref.shape[0]
    rest = lon - 128

    def level(k, carry):
        for rp in range(2):
            parts = []
            for g in range(groups):
                x = d_ref[g, k]
                parts.append(x[:, 128 * rp : 128 * rp + 128])
                parts.append(x[:, 256 + rest * rp : 256 + rest * rp + rest])
            o_ref[rp, k] = jnp.concatenate(parts, axis=1)
        return carry

    lax.fori_loop(0, d_ref.shape[1], level, 0)


def call(kernel, shape, count, scratch=(), limit=48, **params):
    return pl.pallas_call(
        kernel,
        out_shape=jax.ShapeDtypeStruct(shape, F32),
        in_specs=[VMEM] * count,
        out_specs=VMEM,
        scratch_shapes=list(scratch),
        compiler_params=pltpu.CompilerParams(vmem_limit_bytes=limit << 20, **params),
    )


def body(tracers, zonal, meridional, vertical, route, inverse):
    trac, levs_here, rows, width = tracers.shape
    lats, groups = lax.axis_size("lat"), lax.axis_size("lev")
    levels, _, lon = vertical.shape
    rest = lon - 128
    matrix = call(reorder_kernel, inverse.shape[2:], 1)(inverse[0, 0])
    matrices = lax.all_gather(matrix, "lat")
    turned = jnp.transpose(tracers, (2, 1, 0, 3))
    up = [(i, i + 1) for i in range(lats - 1)]
    down = [(i + 1, i) for i in range(lats - 1)]
    south = lax.ppermute(turned[rows - 3 :], "lat", up)
    north = lax.ppermute(turned[:3], "lat", down)
    mer_north = lax.ppermute(meridional[:, :1], "lat", down)
    targets = route[:, :, 0]
    before = jnp.arange(lon)[:, None] < jnp.arange(lon)[None, :]
    same = jnp.logical_and(targets[:, :, None] == targets[:, None, :], before[None])
    place = (targets % groups) * lats + targets // groups
    slots = place * 4 + jnp.sum(same.astype(jnp.int32), axis=1)
    slots = jnp.pad(slots, ((0, 0), (0, 256 - lon)), constant_values=-1)
    v = vertical.reshape(levels, 2, 2, lon)
    courant = jnp.concatenate(
        [v[:, 0, :, :128], v[:, 1, :, :128], v[:, 0, :, 128:], v[:, 1, :, 128:], jnp.zeros((levels, 2, 128 - 2 * rest), F32)],
        axis=-1,
    )
    sent = call(horizontal_kernel, (groups, levs_here, 8, 384), 6)(turned, south, north, zonal, meridional, mer_north)
    columns = lax.all_to_all(sent, "lev", split_axis=0, concat_axis=0, tiled=True)
    columns = columns.reshape(levels, 8, 384)
    packed = call(
        functools.partial(select_kernel, rest), (9, groups, lats, 4, 128), 3, [pltpu.VMEM((4, 384, 512), BF16)]
    )(columns, courant, slots)
    order = matrix.shape[0]
    back = call(
        functools.partial(route_kernel, lats, groups),
        (9, groups, lats, 4, 128),
        2,
        [
            pltpu.VMEM((9, lats, groups, 4, 128), F32),
            pltpu.VMEM((9, lats, groups, 4, 128), F32),
            pltpu.VMEM((2, lats, order, order), BF16),
            pltpu.SemaphoreType.DMA((2, groups)),
            pltpu.SemaphoreType.DMA((2, groups)),
            pltpu.SemaphoreType.DMA((2,)),
        ],
        collective_id=0,
        has_side_effects=True,
    )(packed, matrices)
    diffused = call(functools.partial(unselect_kernel, rest), (levels, 8, 384), 2)(back, slots)
    owned = lax.all_to_all(diffused.reshape(groups, levs_here, 8, 384), "lev", split_axis=0, concat_axis=0, tiled=True)
    whole = call(functools.partial(assemble_kernel, lon), (2, levs_here, 8, width), 1)(owned)
    whole = whole.reshape(2, levs_here, 2, trac, width)
    return jnp.transpose(whole, (3, 1, 0, 2, 4)).reshape(tracers.shape) - tracers


def solution(mesh):
    in_specs = (
        P(None, "lev", "lat", None),
        P("lev", "lat", None),
        P("lev", "lat", None),
        P(None, "lat", "lev"),
        P("lat", "lev", None),
        P("lat", "lev", None, None),
    )
    out_specs = P(None, "lev", "lat", None)
    return jax.shard_map(body, mesh=mesh, in_specs=in_specs, out_specs=out_specs, check_vma=False)
```

time: 282 us -> 189 us (0.67); the launches traced: 277 us -> 188 us
  blocking collectives: 127 us -> 18.5 us
  local copies, waits for them, and re-layouts: 91.3 us -> 6.32 us
  Pallas kernels: 0 us -> 76.1 us
  waiting for transfers between devices: 12.4 us -> 53.7 us
  other arithmetic: 26.5 us -> 1.57 us
  between operations: 0.83 us -> 13.6 us
  matrix products: 6.31 us -> 0 us
  starting transfers between devices: 12.2 us -> 18.1 us
    all_to_all x3 -> x1, blocking collectives: 127 us -> 18.5 us  [body(): lax.all_to_all(diffused.reshape(groups, levs_here, 8, 384), 'lev', split_...]
    pallas_call x0 -> x6, Pallas kernels: none -> 76.1 us  [the longest x1 63.2 us: body(): call(functools.partial(route_kernel, lats, groups), (9, groups, lats, 4,...]
    unnamed x43 -> x15, local copies, waits for them, and re-layouts: 40.2 us -> 2.7 us
    all_gather x0 -> x1, waiting for transfers between devices: none -> 34.8 us  [body(): matrices = lax.all_gather(matrix, 'lat')]
    all_to_all x4 -> x0, local copies, waits for them, and re-layouts: 13.6 us -> none  [the longest x2 12 us: body(): lax.all_to_all(horizontal, 'lev', split_axis=3, concat_axis=1, tiled=True)]
    reshape x3 -> x2, local copies, waits for them, and re-layouts: 13.5 us -> 1.02 us  [the longest x1 0.76 us: body(): jnp.transpose(whole, (3, 1, 0, 2, 4)).reshape(tracers.shape) - tracers]
    add x2 -> x0, local copies, waits for them, and re-layouts: 9.03 us -> none  [the longest x1 8.8 us: body(): horizontal = tracers + lon_change + lat_change]
    sub x7 -> x1, other arithmetic: 8.3 us -> 1.14 us  [body(): jnp.transpose(whole, (3, 1, 0, 2, 4)).reshape(tracers.shape) - tracers]
  transfers between devices with their start and end apart: 3 -> 5, of which waited for: 3 -> 4; matrix products, arithmetic and copies ran while one was open for 6% -> 2% of each run, Pallas kernels for 0% -> 4%
where the time goes in v1:
time: 189 us; the launch traced here: 188 us
  Pallas kernels  76.1 us (40%)
  waiting for transfers between devices  53.7 us (28%)
  blocking collectives  18.5 us (10%)
  starting transfers between devices  18.1 us (10%)
  between operations  13.6 us (7%)
  local copies, waits for them, and re-layouts  6.32 us (3%)
    pallas_call x1, Pallas kernels, body(): call(functools.partial(route_kernel, lats, groups), (9, groups, lats, 4,...  63.2 us
    all_gather x1, waiting for transfers between devices, body(): matrices = lax.all_gather(matrix, 'lat')  34.8 us
    all_to_all x1, blocking collectives, body(): lax.all_to_all(diffused.reshape(groups, levs_here, 8, 384), 'lev', split_...  18.5 us
    all_to_all x1, waiting for transfers between devices, body(): lax.all_to_all(sent, 'lev', split_axis=0, concat_axis=0, tiled=True)  9.48 us
    ppermute x1, waiting for transfers between devices, body(): south = lax.ppermute(turned[rows - 3:], 'lat', up)  6.23 us
    ppermute x1, starting transfers between devices, body(): mer_north = lax.ppermute(meridional[:, :1], 'lat', down)  6.05 us
    pallas_call x1, Pallas kernels, body(): call(horizontal_kernel, (groups, levs_here, 8, 384), 6)  5.92 us
    ppermute x1, starting transfers between devices, body(): north = lax.ppermute(turned[:3], 'lat', down)  5.39 us
  transfers between devices with their start and end apart: 5, of which 4 were waited for; matrix products, arithmetic and copies ran while one was open for 2% of the time, Pallas kernels for 4%

profile of v1, /device:TPU:24, one launch (start us, length us, event | category | flops | bytes accessed | tf_op | source)
XLA Modules:
  0.0 187.9 jit_solution(9006203658082914601)
XLA Ops:
  6.5 0.0 all-gather.3.cloned.1.call-start
  6.5 0.0 copy-start
  6.5 1.0 copy-done
  7.6 2.9 %shard_map.66 = f32[288,288]{1,0:T(8,128)} custom-call(f32[288,288]{1,0:T(8,128)S(1)} %bitcast.28), custom_call_target="tpu_custom_call" | custom-call | tf_op jit(solution)/shard_map/pallas_call | solution.py:346
  10.4 0.0 copy-start.1
  10.4 0.0 all-gather.3.cloned.1.call-update
  10.5 0.0 copy-start.5
  10.5 0.0 copy-start.4
  10.5 1.6 copy.37
  12.1 0.0 copy-start.2
  12.1 1.3 fusion.6
  13.3 5.4 %collective-permute-start.1 = (f32[3,9,4,1440]{3,2,1,0:T(4,128)}, f32[3,9,4,1440]{3,2,1,0:T(4,128)S(1)}, u32[]{:S(2)}, u32[]{:S(2)}) collective-permute-start(f32[3,9,4,1440]{3,2,1,0:T(4,128)} %get-tuple-element.5), channel_id=1, source_target_pairs={{8,0},{16,8},{24,16},{32,24},{40,32},{48,40},{56,48},{64,56},{72,6... | collective-permute-start | bytes 1866248 | tf_op jit(solution)/shard_map/ppermute | solution.py:352
  18.7 1.9 %collective-permute-start = (f32[3,9,4,1440]{3,2,1,0:T(4,128)}, f32[3,9,4,1440]{3,2,1,0:T(4,128)S(1)}, u32[]{:S(2)}, u32[]{:S(2)}) collective-permute-start(f32[3,9,4,1440]{3,2,1,0:T(4,128)} %get-tuple-element.6), channel_id=1, source_target_pairs={{0,8},{8,16},{16,24},{24,32},{32,40},{40,48},{48,56},{56,64},{64,7... | collective-permute-start | bytes 1866248 | tf_op jit(solution)/shard_map/ppermute | solution.py:351
  20.7 0.0 copy-done.1
  20.7 6.0 %collective-permute-start.2 = (f32[9,1,1440]{2,1,0:T(1,128)S(1)}, f32[9,1,1440]{2,1,0:T(1,128)S(1)}, u32[]{:S(2)}, u32[]{:S(2)}) collective-permute-start(f32[9,1,1440]{2,1,0:T(1,128)S(1)} %slice.23), channel_id=1, source_target_pairs={{8,0},{16,8},{24,16},{32,24},{40,32},{48,40},{56,48},{64,56},{72,6... | collective-permute-start | bytes 155528 | tf_op jit(solution)/shard_map/ppermute | solution.py:353
  26.8 0.0 copy-done.5
  26.8 0.1 copy.22
  26.9 0.0 copy-done.4
  26.9 0.1 copy.17
  27.1 0.4 convert_reduce_fusion
  27.5 3.3 %collective-permute-done.2.mern_ref = f32[9,1,1440]{2,1,0:T(1,128)S(1)} collective-permute-done((f32[9,1,1440]{2,1,0:T(1,128)S(1)}, f32[9,1,1440]{2,1,0:T(1,128)S(1)}, u32[]{:S(2)}, u32[]{:S(2)}) %collective-permute-start.2) | collective-permute-done | bytes 51872 | tf_op jit(solution)/shard_map/ppermute | solution.py:353
  30.7 0.0 collective-permute-done.1.north_ref
  30.7 6.2 %collective-permute-done.south_ref = f32[3,9,4,1440]{3,2,1,0:T(4,128)S(1)} collective-permute-done((f32[3,9,4,1440]{3,2,1,0:T(4,128)}, f32[3,9,4,1440]{3,2,1,0:T(4,128)S(1)}, u32[]{:S(2)}, u32[]{:S(2)}) %collective-permute-start) | collective-permute-done | bytes 622112 | tf_op jit(solution)/shard_map/ppermute | solution.py:351
  37.0 0.0 copy-done.2
  37.0 5.9 %shard_map.64 = f32[8,9,8,384]{3,2,1,0:T(8,128)} custom-call(f32[4,9,4,1440]{3,2,1,0:T(4,128)S(1)} %bitcast.25, f32[3,9,4,1440]{3,2,1,0:T(4,128)S(1)} %collective-permute-done.south_ref, f32[3,9,4,1440]{3,2,1,0:T(4,128)S(1)} %collective-permute-done.1.north_ref, f32[9,4,1440]{2,1,0:T(4,128)S(1)} %copy-done.2, f32[9,4,1440]{2,1,0:T(4,128)S(1)} %copy-done.1, ...), custom_call_target="tpu_custom_call" | custom-call | tf_op jit(solution)/shard_map/pallas_call | solution.py:365
  42.9 4.7 %all-to-all-start = ((f32[8,9,8,384]{3,2,1,0:T(8,128)}), f32[8,9,8,384]{3,2,1,0:T(8,128)S(1)}, u32[]{:S(2)}, u32[]{:S(2)}) async-start(f32[8,9,8,384]{3,2,1,0:T(8,128)} %shard_map.64), calls=%async_computation | async-start | bytes 1769472 | tf_op jit(solution)/shard_map/all_to_all | solution.py:366
  47.6 0.1 copy_bitcast_fusion.3
  47.7 0.1 copy_bitcast_fusion.1
  47.8 0.5 concatenate.3.c_ref
  48.4 9.5 %all-to-all-done = f32[8,9,8,384]{3,2,1,0:T(8,128)S(1)} async-done(((f32[8,9,8,384]{3,2,1,0:T(8,128)}), f32[8,9,8,384]{3,2,1,0:T(8,128)S(1)}, u32[]{:S(2)}, u32[]{:S(2)}) %all-to-all-start) | async-done | bytes 884768 | tf_op jit(solution)/shard_map/all_to_all | solution.py:366
  57.9 1.9 %shard_map.65.p_ref = f32[9,8,16,4,128]{4,3,2,1,0:T(4,128)S(1)} custom-call(f32[72,8,384]{2,1,0:T(8,128)S(1)} %bitcast.27, f32[72,2,384]{2,1,0:T(2,128)S(1)} %concatenate.3.c_ref, s32[4,256]{1,0:T(4,128)S(1)} %pad.4.slot_ref), custom_call_target="tpu_custom_call" | custom-call | tf_op jit(solution)/shard_map/pallas_call | solution.py:368
  59.8 34.8 %all-gather.3.cloned.1.call-done = f32[4608,288]{1,0:T(8,128)} async-done(((f32[288,288]{1,0:T(8,128)}), f32[4608,288]{1,0:T(8,128)}) %all-gather.3.cloned.1.call-update) | async-done | bytes 5308432 | tf_op jit(solution)/shard_map/all_gather | solution.py:347
  94.5 63.2 %shard_map.67.v_ref = f32[9,8,16,4,128]{4,3,2,1,0:T(4,128)S(1)} custom-call(f32[9,8,16,4,128]{4,3,2,1,0:T(4,128)S(1)} %shard_map.65.p_ref, f32[16,288,288]{2,1,0:T(8,128)} %bitcast.29), custom_call_target="tpu_custom_call" | custom-call | tf_op jit(solution)/shard_map/pallas_call | solution.py:372
  157.8 1.3 shard_map.68
  159.0 18.5 %all_to_all.10.d_ref = f32[8,9,8,384]{3,2,1,0:T(8,128)S(1)} all-to-all(f32[8,9,8,384]{3,2,1,0:T(8,128)S(1)} %bitcast.26), channel_id=1, replica_groups=mesh['lat'=16,'lev'=8] {'lev'}, dimensions={0} | all-to-all | bytes 1769472 | tf_op jit(solution)/shard_map/all_to_all | solution.py:388
  177.5 0.9 shard_map.69
  178.4 0.0 copy-start.3
  178.4 0.3 reshape.31
  178.7 0.5 copy.23
  179.1 0.8 reshape.32
  179.9 0.0 copy-done.3
  179.9 1.1 sub.10
  (8 shorter events, 0.1 us)
Async XLA Ops:
  6.5 88.0 %all-gather.3.cloned.1.call-start = ((), (), s32[]{:S(2)}) async-start(), calls=%async_computation.2 | async-start | bytes 7520256 | tf_op jit(solution)/shard_map/all_gather | solution.py:347
  6.5 1.0 copy-start
  10.4 10.2 %copy-start.1 = (f32[9,4,1440]{2,1,0:T(4,128)S(1)}, f32[9,4,1440]{2,1,0:T(4,128)}, u32[]{:S(2)}) copy-start(f32[9,4,1440]{2,1,0:T(4,128)} %mer_ref.1) | copy-start | bytes 622084
  10.5 16.3 %copy-start.5 = (s32[4,180,1]{1,2,0:T(1,128)S(1)}, s32[4,180,1]{1,2,0:T(1,128)}, u32[]{:S(2)}) copy-start(s32[4,180,1]{1,2,0:T(1,128)} %param.10) | copy-start | bytes 8644
  10.5 16.5 %copy-start.4 = (f32[72,4,180]{2,1,0:T(4,128)S(1)}, f32[72,4,180]{2,1,0:T(4,128)}, u32[]{:S(2)}) copy-start(f32[72,4,180]{2,1,0:T(4,128)} %param.9) | copy-start | bytes 622084
  12.1 24.9 %copy-start.2 = (f32[9,4,1440]{2,1,0:T(4,128)S(1)}, f32[9,4,1440]{2,1,0:T(4,128)}, u32[]{:S(2)}) copy-start(f32[9,4,1440]{2,1,0:T(4,128)} %zon_ref.1) | copy-start | bytes 622084
  13.3 17.4 %collective-permute-start.1 = (f32[3,9,4,1440]{3,2,1,0:T(4,128)}, f32[3,9,4,1440]{3,2,1,0:T(4,128)S(1)}, u32[]{:S(2)}, u32[]{:S(2)}) collective-permute-start(f32[3,9,4,1440]{3,2,1,0:T(4,128)} %get-tuple-element.5), channel_id=1, source_target_pairs={{8,0},{16,8},{24,16},{32,24},{40,32},{48,40},{56,48},{64,56},{72,6... | collective-permute-start | bytes 1866248 | tf_op jit(solution)/shard_map/ppermute | solution.py:352
  18.7 18.2 %collective-permute-start = (f32[3,9,4,1440]{3,2,1,0:T(4,128)}, f32[3,9,4,1440]{3,2,1,0:T(4,128)S(1)}, u32[]{:S(2)}, u32[]{:S(2)}) collective-permute-start(f32[3,9,4,1440]{3,2,1,0:T(4,128)} %get-tuple-element.6), channel_id=1, source_target_pairs={{0,8},{8,16},{16,24},{24,32},{32,40},{40,48},{48,56},{56,64},{64,7... | collective-permute-start | bytes 1866248 | tf_op jit(solution)/shard_map/ppermute | solution.py:351
  20.7 10.0 %collective-permute-start.2 = (f32[9,1,1440]{2,1,0:T(1,128)S(1)}, f32[9,1,1440]{2,1,0:T(1,128)S(1)}, u32[]{:S(2)}, u32[]{:S(2)}) collective-permute-start(f32[9,1,1440]{2,1,0:T(1,128)S(1)} %slice.23), channel_id=1, source_target_pairs={{8,0},{16,8},{24,16},{32,24},{40,32},{48,40},{56,48},{64,56},{72,6... | collective-permute-start | bytes 155528 | tf_op jit(solution)/shard_map/ppermute | solution.py:353
  42.9 15.0 %all-to-all-start = ((f32[8,9,8,384]{3,2,1,0:T(8,128)}), f32[8,9,8,384]{3,2,1,0:T(8,128)S(1)}, u32[]{:S(2)}, u32[]{:S(2)}) async-start(f32[8,9,8,384]{3,2,1,0:T(8,128)} %shard_map.64), calls=%async_computation | async-start | bytes 1769472 | tf_op jit(solution)/shard_map/all_to_all | solution.py:366
  178.4 1.5 copy-start.3
Sparse Core Ops, SparseCore 0:
  10.6 83.9 all-gather.2

commit v2 on v1

--- a/solution.py
+++ b/solution.py
@@ -36,7 +36,7 @@
     return (7.0 / 12.0) * (q_m1 + q_0) - (1.0 / 12.0) * (q_m2 + q_p1)
 
 
-def horizontal_kernel(tr_ref, south_ref, north_ref, zon_ref, mer_ref, mern_ref, g_ref):
+def horizontal(tr_ref, south_ref, north_ref, zon_ref, mer_ref, mern_ref, g_ref, ready):
     lat = lax.axis_index("lat")
     last = lax.axis_size("lat") - 1
     width = tr_ref.shape[3]
@@ -120,6 +120,7 @@
                 ],
                 axis=1,
             )
+        ready(k)
         return carry
 
     lax.fori_loop(0, tr_ref.shape[1], level, 0)
@@ -130,8 +131,9 @@
     return (ids == slot_ref[r : r + 1, :]).astype(F32).astype(BF16)
 
 
-def select_kernel(rest, g_ref, c_ref, slot_ref, p_ref, a_ref):
-    levels = g_ref.shape[0]
+def select(rest, g_ref, c_ref, slot_ref, p_ref, a_ref, ready):
+    block = g_ref.shape[1]
+    levels = g_ref.shape[0] * block
     sub = lax.broadcasted_iota(jnp.int32, (8, 384), 0) < 4
     half = lax.broadcasted_iota(jnp.int32, (8, 256), 0) < 4
     zero = jnp.zeros((8, 384), F32)
@@ -142,7 +144,7 @@
             a_ref[r, 32 * r + 288 : 384, :] = jnp.zeros((96 - 32 * r, 512), BF16)
 
     def q(k):
-        return g_ref[k] if 0 <= k < levels else zero
+        return g_ref[k // block, k % block] if 0 <= k < levels else zero
 
     def e_at(k):
         return face(q(k - 2), q(k - 1), q(k), q(k + 1))
@@ -193,6 +195,7 @@
                 carried = part
                 continue
             p_ref[2 * r + t] = part.reshape(p_ref.shape[1:])
+        ready(r)
 
 
 def reorder_kernel(m_ref, o_ref):
@@ -202,91 +205,22 @@
     o = lax.broadcasted_iota(jnp.int32, (order, order), 1)
     pick = ((x & 3) * levels + (x >> 2) == o).astype(F32)
     exact = dict(precision=lax.Precision.HIGHEST, preferred_element_type=F32)
-    o_ref[...] = lax.dot_general(lax.dot_general(pick, m_ref[...], NN, **exact), pick, NT, **exact)
-
-
-def route_kernel(lats, levs, p_ref, m_ref, v_ref, r_ref, y_ref, w_ref, ssem, rsem, lsem):
-    lat, lev = lax.axis_index("lat"), lax.axis_index("lev")
-    order = m_ref.shape[1]
-    spans = m_ref.shape[0]
-    barrier = pltpu.get_barrier_semaphore()
-    for i in range(1, levs):
-        pl.semaphore_signal(barrier, inc=1, device_id=(lat, lax.rem(lev + i, levs)), device_id_type=MESH)
-    pl.semaphore_wait(barrier, levs - 1)
-
-    def out_copy(i):
-        to = lax.rem(lev + i, levs)
-        return pltpu.make_async_remote_copy(
-            src_ref=p_ref.at[:, to, :, 0:3],
-            dst_ref=r_ref.at[:, :, lev, 0:3],
-            send_sem=ssem.at[0, i],
-            recv_sem=rsem.at[0, i],
-            device_id=(lat, to),
-            device_id_type=MESH,
-        )
-
-    def back_copy(i):
-        to = lax.rem(lev + i, levs)
-        return pltpu.make_async_remote_copy(
-            src_ref=y_ref.at[:, :, to, 0:3],
-            dst_ref=v_ref.at[:, lev, :, 0:3],
-            send_sem=ssem.at[1, i],
-            recv_sem=rsem.at[1, i],
-            device_id=(lat, to),
-            device_id_type=MESH,
-        )
-
-    own_out = pltpu.make_async_copy(p_ref.at[:, lev, :, 0:3], r_ref.at[:, :, lev, 0:3], lsem.at[0])
-    own_back = pltpu.make_async_copy(y_ref.at[:, :, lev, 0:3], v_ref.at[:, lev, :, 0:3], lsem.at[1])
-    own_out.start()
-    for i in range(1, levs):
-        out_copy(i).start()
-
-    @pl.loop(0, spans)
-    def _(n):
-        hi, lo = split(m_ref[n])
-        w_ref[0, n] = hi
-        w_ref[1, n] = lo
-
-    own_out.wait()
-    for i in range(1, levs):
-        out_copy(i).wait()
-
-    @pl.loop(0, spans)
-    def _(n):
-        tiles = [r_ref[j, n].reshape(4 * levs, 128) for j in range(9)]
-        rows = []
-        for r in range(4):
-            x = jnp.concatenate(tiles[2 * r : 2 * r + 3], axis=1)
-            if r > 0:
-                x = pltpu.roll(x, 384 - 32 * r, 1)
-            rows.append(x[:, :order])
-        hi, lo = split(jnp.concatenate(rows, axis=0))
-        y = dot(hi, w_ref[0, n], NT) + dot(lo, w_ref[0, n], NT) + dot(hi, w_ref[1, n], NT)
-        size = 4 * levs
-        carried = None
-        for r in range(4):
-            x = jnp.concatenate([y[r * size : (r + 1) * size], jnp.zeros((size, 384 - order), F32)], axis=1)
-            if r > 0:
-                x = pltpu.roll(x, 32 * r, 1)
-            for t in range(3):
-                part = x[:, 128 * t : 128 * t + 128]
-                if t == 0 and r > 0:
-                    part = part + carried
-                if t == 2 and r < 3:
-                    carried = part
-                    continue
-                y_ref[2 * r + t, n] = part.reshape(levs, 4, 128)
-
-    own_back.start()
-    for i in range(1, levs):
-        back_copy(i).start()
-    own_back.wait()
-    for i in range(1, levs):
-        back_copy(i).wait()
-
-
-def unselect_kernel(rest, v_ref, slot_ref, d_ref):
+    out = lax.dot_general(lax.dot_general(pick, m_ref[...], NN, **exact), pick, NT, **exact)
+    part = order // 4
+    o_ref[0:order] = out[:, 0:128]
+    o_ref[order : 2 * order] = out[:, 128:256]
+    o_ref[2 * order :] = jnp.concatenate([out[part * i : part * i + part, 256:] for i in range(4)], axis=1)
+
+
+def unpacked(packed):
+    part = packed.shape[0] // 9
+    third = packed[8 * part :]
+    lanes = third.shape[1] // 4
+    third = jnp.concatenate([third[:, lanes * i : lanes * i + lanes] for i in range(4)], axis=0)
+    return jnp.concatenate([packed[: 4 * part], packed[4 * part : 8 * part], third], axis=1)
+
+
+def unselect(rest, v_ref, slot_ref, d_ref):
     lane = lax.broadcasted_iota(jnp.int32, (128, 512), 1)
     live = (lane & 3) < 3
     turned = [jnp.where(live, v_ref[j].reshape(512, 128).T, 0.0) for j in range(9)]
@@ -298,7 +232,8 @@
         whole.append(dot(jnp.concatenate([hi, lo], axis=1), jnp.concatenate([one, one], axis=0)))
     sub = lax.broadcasted_iota(jnp.int32, (8, 256), 0) < 4
     lane = lax.broadcasted_iota(jnp.int32, (8, 128), 1)
-    for n in range(d_ref.shape[0] // 2):
+    block = d_ref.shape[1]
+    for n in range(d_ref.shape[0] * block // 2):
         even, odd = [], []
         for rp in range(2):
             x = whole[2 * rp][8 * n : 8 * n + 8]
@@ -307,10 +242,10 @@
             odd.append(jnp.where(sub, pltpu.roll(x, 4, 0), y))
         for i, (a, b) in enumerate((even, odd)):
             third = jnp.where(lane < rest, a[:, 128:], pltpu.roll(b[:, 128:], rest, 1))
-            d_ref[2 * n + i] = jnp.concatenate([a[:, :128], b[:, :128], third], axis=1)
-
-
-def assemble_kernel(lon, d_ref, o_ref):
+            d_ref[(2 * n + i) // block, (2 * n + i) % block] = jnp.concatenate([a[:, :128], b[:, :128], third], axis=1)
+
+
+def assemble(lon, d_ref, o_ref):
     groups = d_ref.shape[0]
     rest = lon - 128
 
@@ -327,6 +262,143 @@
     lax.fori_loop(0, d_ref.shape[1], level, 0)
 
 
+CHUNKS = 4
+
+
+def greet(lat, lev, levs):
+    barrier = pltpu.get_barrier_semaphore()
+    for i in range(1, levs):
+        pl.semaphore_signal(barrier, inc=1, device_id=(lat, lax.rem(lev + i, levs)), device_id_type=MESH)
+    pl.semaphore_wait(barrier, levs - 1)
+
+
+def send(src, dst, ssem, rsem, lat, to):
+    return pltpu.make_async_remote_copy(
+        src_ref=src, dst_ref=dst, send_sem=ssem, recv_sem=rsem, device_id=(lat, to), device_id_type=MESH
+    )
+
+
+def forth_kernel(
+    rest, levs, tr_ref, south_ref, north_ref, zon_ref, mer_ref, mern_ref, c_ref, slot_ref,
+    r_ref, g_ref, col_ref, p_ref, a_ref, s1, r1, s2, r2, lsem,
+):
+    lat, lev = lax.axis_index("lat"), lax.axis_index("lev")
+    block = tr_ref.shape[1]
+    greet(lat, lev, levs)
+
+    def level_copy(k, i):
+        to = lax.rem(lev + i, levs)
+        return send(g_ref.at[to, k], col_ref.at[lev, k], s1.at[k, i], r1.at[k, i], lat, to)
+
+    def level_ready(k):
+        for i in range(1, levs):
+            level_copy(k, i).start()
+
+    horizontal(tr_ref, south_ref, north_ref, zon_ref, mer_ref, mern_ref, g_ref, level_ready)
+    own = pltpu.make_async_copy(g_ref.at[lev], col_ref.at[lev], lsem.at[0])
+    own.start()
+    own.wait()
+
+    @pl.loop(0, block)
+    def _(k):
+        for i in range(1, levs):
+            level_copy(k, i).wait()
+
+    def tiles(r):
+        return slice(2 * r, 2 * r + (3 if r == 3 else 2))
+
+    def row_copy(r, i):
+        to = lax.rem(lev + i, levs)
+        return send(p_ref.at[tiles(r), to, :, 0:3], r_ref.at[tiles(r), :, lev, 0:3], s2.at[r, i], r2.at[r, i], lat, to)
+
+    def row_ready(r):
+        for i in range(1, levs):
+            row_copy(r, i).start()
+
+    select(rest, col_ref, c_ref, slot_ref, p_ref, a_ref, row_ready)
+    own = pltpu.make_async_copy(p_ref.at[:, lev, :, 0:3], r_ref.at[:, :, lev, 0:3], lsem.at[1])
+    own.start()
+    own.wait()
+    for r in range(4):
+        for i in range(1, levs):
+            row_copy(r, i).wait()
+
+
+def back_kernel(
+    rest, levs, order, r_ref, near_ref, far_ref, slot_ref,
+    o_ref, y_ref, v_ref, w_ref, d_ref, own_ref, s1, r1, s2, r2, lsem,
+):
+    lat, lev = lax.axis_index("lat"), lax.axis_index("lev")
+    lats = r_ref.shape[1]
+    size = lats // CHUNKS
+    greet(lat, lev, levs)
+
+    def back_copy(q, i):
+        to = lax.rem(lev + i, levs)
+        part = slice(q * size, q * size + size)
+        return send(y_ref.at[:, part, to, 0:3], v_ref.at[:, lev, part, 0:3], s1.at[q, i], r1.at[q, i], lat, to)
+
+    @pl.loop(0, lats // 2)
+    def _(n):
+        steps, turn = n // 2, lax.rem(n, 2)
+        chip = lax.rem(lat // 4 - steps + 4, 4) * 4 + lax.rem(lat // 2 + turn, 2) * 2
+        for ref, core in ((near_ref, lax.rem(lat, 2)), (far_ref, lax.rem(lat + 1, 2))):
+            hi, lo = split(unpacked(ref[n]))
+            w_ref[0, chip + core] = hi
+            w_ref[1, chip + core] = lo
+
+    def mix(n):
+        tiles = [r_ref[j, n].reshape(4 * levs, 128) for j in range(9)]
+        rows = []
+        for r in range(4):
+            x = jnp.concatenate(tiles[2 * r : 2 * r + 3], axis=1)
+            if r > 0:
+                x = pltpu.roll(x, 384 - 32 * r, 1)
+            rows.append(x[:, :order])
+        hi, lo = split(jnp.concatenate(rows, axis=0))
+        y = dot(hi, w_ref[0, n], NT) + dot(lo, w_ref[0, n], NT) + dot(hi, w_ref[1, n], NT)
+        many = 4 * levs
+        carried = None
+        for r in range(4):
+            x = jnp.concatenate([y[r * many : (r + 1) * many], jnp.zeros((many, 384 - order), F32)], axis=1)
+            if r > 0:
+                x = pltpu.roll(x, 32 * r, 1)
+            for t in range(3):
+                part = x[:, 128 * t : 128 * t + 128]
+                if t == 0 and r > 0:
+                    part = part + carried
+                if t == 2 and r < 3:
+                    carried = part
+                    continue
+                y_ref[2 * r + t, n] = part.reshape(levs, 4, 128)
+
+    for q in range(CHUNKS):
+        pl.loop(q * size, q * size + size)(mix)
+        for i in range(1, levs):
+            back_copy(q, i).start()
+    own = pltpu.make_async_copy(y_ref.at[:, :, lev, 0:3], v_ref.at[:, lev, :, 0:3], lsem.at[0])
+    own.start()
+    own.wait()
+    for q in range(CHUNKS):
+        for i in range(1, levs):
+            back_copy(q, i).wait()
+
+    unselect(rest, v_ref, slot_ref, d_ref)
+
+    def level_copy(i):
+        to = lax.rem(lev + i, levs)
+        return send(d_ref.at[to], own_ref.at[lev], s2.at[i], r2.at[i], lat, to)
+
+    for i in range(1, levs):
+        level_copy(i).start()
+    own = pltpu.make_async_copy(d_ref.at[lev], own_ref.at[lev], lsem.at[1])
+    own.start()
+    own.wait()
+    for i in range(1, levs):
+        level_copy(i).wait()
+    assemble(128 + rest, own_ref, o_ref)
+
+
 def call(kernel, shape, count, scratch=(), limit=48, **params):
     return pl.pallas_call(
         kernel,
@@ -343,8 +415,10 @@
     lats, groups = lax.axis_size("lat"), lax.axis_size("lev")
     levels, _, lon = vertical.shape
     rest = lon - 128
-    matrix = call(reorder_kernel, inverse.shape[2:], 1)(inverse[0, 0])
-    matrices = lax.all_gather(matrix, "lat")
+    order = inverse.shape[2]
+    matrix = call(reorder_kernel, (order * order // 128, 128), 1)(inverse[0, 0])
+    across = lax.ppermute(matrix, "lat", [(i, i ^ 2) for i in range(lats)])
+    pair = jnp.stack([matrix, across])
     turned = jnp.transpose(tracers, (2, 1, 0, 3))
     up = [(i, i + 1) for i in range(lats - 1)]
     down = [(i + 1, i) for i in range(lats - 1)]
@@ -362,31 +436,50 @@
         [v[:, 0, :, :128], v[:, 1, :, :128], v[:, 0, :, 128:], v[:, 1, :, 128:], jnp.zeros((levels, 2, 128 - 2 * rest), F32)],
         axis=-1,
     )
-    sent = call(horizontal_kernel, (groups, levs_here, 8, 384), 6)(turned, south, north, zonal, meridional, mer_north)
-    columns = lax.all_to_all(sent, "lev", split_axis=0, concat_axis=0, tiled=True)
-    columns = columns.reshape(levels, 8, 384)
-    packed = call(
-        functools.partial(select_kernel, rest), (9, groups, lats, 4, 128), 3, [pltpu.VMEM((4, 384, 512), BF16)]
-    )(columns, courant, slots)
-    order = matrix.shape[0]
-    back = call(
-        functools.partial(route_kernel, lats, groups),
-        (9, groups, lats, 4, 128),
-        2,
+    south, north, mer_north, pair = lax.optimization_barrier((south, north, mer_north, pair))
+    shifted = [lax.ppermute(pair, "lat", [(i, (i + 4 * d) % lats) for i in range(lats)]) for d in range(1, 4)]
+    dma = pltpu.SemaphoreType.DMA
+    levels_of = pltpu.VMEM((groups, levs_here, 8, 384), F32)
+    received = call(
+        functools.partial(forth_kernel, rest, groups),
+        (9, lats, groups, 4, 128),
+        8,
         [
-            pltpu.VMEM((9, lats, groups, 4, 128), F32),
-            pltpu.VMEM((9, lats, groups, 4, 128), F32),
-            pltpu.VMEM((2, lats, order, order), BF16),
-            pltpu.SemaphoreType.DMA((2, groups)),
-            pltpu.SemaphoreType.DMA((2, groups)),
-            pltpu.SemaphoreType.DMA((2,)),
+            levels_of,
+            levels_of,
+            pltpu.VMEM((9, groups, lats, 4, 128), F32),
+            pltpu.VMEM((4, 384, 512), BF16),
+            dma((levs_here, groups)),
+            dma((levs_here, groups)),
+            dma((4, groups)),
+            dma((4, groups)),
+            dma((2,)),
         ],
         collective_id=0,
         has_side_effects=True,
-    )(packed, matrices)
-    diffused = call(functools.partial(unselect_kernel, rest), (levels, 8, 384), 2)(back, slots)
-    owned = lax.all_to_all(diffused.reshape(groups, levs_here, 8, 384), "lev", split_axis=0, concat_axis=0, tiled=True)
-    whole = call(functools.partial(assemble_kernel, lon), (2, levs_here, 8, width), 1)(owned)
+    )(turned, south, north, zonal, meridional, mer_north, courant, slots)
+    received, shifted = lax.optimization_barrier((received, shifted))
+    near = jnp.concatenate([pair] + shifted, axis=0)
+    far = lax.ppermute(near, "lat", [(i, i ^ 1) for i in range(lats)])
+    whole = call(
+        functools.partial(back_kernel, rest, groups, order),
+        (2, levs_here, 8, width),
+        4,
+        [
+            pltpu.VMEM((9, lats, groups, 4, 128), F32),
+            pltpu.VMEM((9, groups, lats, 4, 128), F32),
+            pltpu.VMEM((2, lats, order, order), BF16),
+            levels_of,
+            levels_of,
+            dma((CHUNKS, groups)),
+            dma((CHUNKS, groups)),
+            dma((groups,)),
+            dma((groups,)),
+            dma((2,)),
+        ],
+        collective_id=1,
+        has_side_effects=True,
+    )(received, near, far, slots)
     whole = whole.reshape(2, levs_here, 2, trac, width)
     return jnp.transpose(whole, (3, 1, 0, 2, 4)).reshape(tracers.shape) - tracers
 

time: 189 us -> 135 us (0.71)
  waiting for transfers between devices: 53.7 us -> 14.6 us
  blocking collectives: 18.5 us -> 0 us
  between operations: 13.6 us -> 0.26 us
  Pallas kernels: 76.1 us -> 84.9 us
  local copies, waits for them, and re-layouts: 6.32 us -> 14.2 us
  starting transfers between devices: 18.1 us -> 16.2 us
    all_gather x1 -> x0, waiting for transfers between devices: 34.8 us -> none  [body(): matrices = lax.all_gather(matrix, 'lat')]
    all_to_all x1 -> x0, blocking collectives: 18.5 us -> none  [body(): lax.all_to_all(diffused.reshape(groups, levs_here, 8, 384), 'lev', split_...]
    all_to_all x1 -> x0, waiting for transfers between devices: 9.48 us -> none  [body(): lax.all_to_all(sent, 'lev', split_axis=0, concat_axis=0, tiled=True)]
    pallas_call x6 -> x3, Pallas kernels: 76.1 us -> 84.9 us  [the longest x1 44.1 us: body(): call(functools.partial(back_kernel, rest, groups, order), (2, levs_here,...]
    ppermute x0 -> x5, starting transfers between devices: none -> 6.34 us  [the longest x3 3.58 us: body(): lax.ppermute(pair, 'lat', [(i, (i + 4 * d) % lats) for i in range(lats)])]
    unnamed x15 -> x18, local copies, waits for them, and re-layouts: 2.7 us -> 8.48 us
    all_to_all x1 -> x0, starting transfers between devices: 4.71 us -> none  [body(): lax.all_to_all(sent, 'lev', split_axis=0, concat_axis=0, tiled=True)]
    ppermute x0 -> x5, waiting for transfers between devices: none -> 4.59 us  [the longest x1 4.58 us: body(): far = lax.ppermute(near, 'lat', [(i, i ^ 1) for i in range(lats)])]
  transfers between devices with their start and end apart: 5 -> 8, of which waited for: 4 -> 3; matrix products, arithmetic and copies ran while one was open for 2% -> 5% of each run, Pallas kernels for 4% -> 31%
where the time goes in v2:
time: 135 us; the launch traced here: 133 us
  Pallas kernels  84.9 us (63%)
  starting transfers between devices  16.2 us (12%)
  waiting for transfers between devices  14.6 us (11%)
  local copies, waits for them, and re-layouts  14.2 us (11%)
  other arithmetic  2.47 us (2%)
    pallas_call x1, Pallas kernels, body(): call(functools.partial(back_kernel, rest, groups, order), (2, levs_here,...  44.1 us
    pallas_call x1, Pallas kernels, body(): call(functools.partial(forth_kernel, rest, groups), (9, lats, groups, 4,...  38.6 us
    unnamed x18, local copies, waits for them, and re-layouts  8.48 us
    ppermute x1, waiting for transfers between devices, body(): south = lax.ppermute(turned[rows - 3:], 'lat', up)  6.17 us
    ppermute x1, starting transfers between devices, body(): mer_north = lax.ppermute(meridional[:, :1], 'lat', down)  5.4 us
    ppermute x1, waiting for transfers between devices, body(): far = lax.ppermute(near, 'lat', [(i, i ^ 1) for i in range(lats)])  4.58 us
    ppermute x1, waiting for transfers between devices, body(): north = lax.ppermute(turned[:3], 'lat', down)  3.85 us
    ppermute x3, starting transfers between devices, body(): lax.ppermute(pair, 'lat', [(i, (i + 4 * d) % lats) for i in range(lats)])  3.58 us
  transfers between devices with their start and end apart: 8, of which 3 were waited for; matrix products, arithmetic and copies ran while one was open for 5% of the time, Pallas kernels for 31%

profile of v2, /device:TPU:24, one launch (start us, length us, event | category | flops | bytes accessed | tf_op | source)
XLA Modules:
  0.0 132.6 jit_solution(7859397421038347262)
XLA Ops:
  0.0 0.0 copy-start.5
  0.0 1.0 slice.23
  1.0 5.4 %collective-permute-start.2 = (f32[9,1,1440]{2,1,0:T(1,128)S(1)}, f32[9,1,1440]{2,1,0:T(1,128)S(1)}, u32[]{:S(2)}, u32[]{:S(2)}) collective-permute-start(f32[9,1,1440]{2,1,0:T(1,128)S(1)} %slice.23), channel_id=1, source_target_pairs={{8,0},{16,8},{24,16},{32,24},{40,32},{48,40},{56,48},{64,56},{72,6... | collective-permute-start | bytes 155528 | tf_op jit(solution)/shard_map/ppermute | solution.py:427
  6.4 0.0 copy-start
  6.4 1.0 copy-done
  7.4 2.1 %shard_map.64 = f32[648,128]{1,0:T(8,128)S(1)} custom-call(f32[288,288]{1,0:T(8,128)S(1)} %bitcast.26), custom_call_target="tpu_custom_call" | custom-call | tf_op jit(solution)/shard_map/pallas_call | solution.py:419
  9.6 0.5 collective-permute-start.3
  10.0 1.5 %copy.37 = f32[4,9,4,1440]{3,0,1,2:T(4,128)S(1)} copy(f32[4,9,4,1440]{3,2,1,0:T(4,128)} %param.6) | data formatting | bytes 1658880 | tf_op args[0]
  11.5 1.2 fusion.6
  12.8 0.0 copy-start.1
  12.8 0.0 copy-start.2
  12.8 2.3 %collective-permute-start.1 = (f32[3,9,4,1440]{3,2,1,0:T(4,128)}, f32[3,9,4,1440]{3,2,1,0:T(4,128)S(1)}, u32[]{:S(2)}, u32[]{:S(2)}) collective-permute-start(f32[3,9,4,1440]{3,2,1,0:T(4,128)} %get-tuple-element.21), channel_id=1, source_target_pairs={{8,0},{16,8},{24,16},{32,24},{40,32},{48,40},{56,48},{64,56},{72,6... | collective-permute-start | bytes 1866248 | tf_op jit(solution)/shard_map/ppermute | solution.py:426
  15.1 2.1 %collective-permute-start = (f32[3,9,4,1440]{3,2,1,0:T(4,128)}, f32[3,9,4,1440]{3,2,1,0:T(4,128)S(1)}, u32[]{:S(2)}, u32[]{:S(2)}) collective-permute-start(f32[3,9,4,1440]{3,2,1,0:T(4,128)} %get-tuple-element.22), channel_id=1, source_target_pairs={{0,8},{8,16},{16,24},{24,32},{32,40},{40,48},{48,56},{56,64},{64,7... | collective-permute-start | bytes 1866248 | tf_op jit(solution)/shard_map/ppermute | solution.py:425
  17.2 0.0 copy-done.5
  17.2 0.1 copy.22
  17.4 1.0 copy.17
  18.4 0.4 convert_reduce_fusion
  18.9 0.0 collective-permute-done.3
  18.9 0.9 pad_maximum_fusion
  19.8 0.0 collective-permute-done.2.mern_ref
  19.8 3.9 %collective-permute-done.1.north_ref = f32[3,9,4,1440]{3,2,1,0:T(4,128)S(1)} collective-permute-done((f32[3,9,4,1440]{3,2,1,0:T(4,128)}, f32[3,9,4,1440]{3,2,1,0:T(4,128)S(1)}, u32[]{:S(2)}, u32[]{:S(2)}) %collective-permute-start.1) | collective-permute-done | bytes 622112 | tf_op jit(solution)/shard_map/ppermute | solution.py:426
  23.6 6.2 %collective-permute-done.south_ref = f32[3,9,4,1440]{3,2,1,0:T(4,128)S(1)} collective-permute-done((f32[3,9,4,1440]{3,2,1,0:T(4,128)}, f32[3,9,4,1440]{3,2,1,0:T(4,128)S(1)}, u32[]{:S(2)}, u32[]{:S(2)}) %collective-permute-start) | collective-permute-done | bytes 622112 | tf_op jit(solution)/shard_map/ppermute | solution.py:425
  29.8 0.5 collective-permute-start.6
  30.3 0.5 collective-permute-start.5
  30.8 2.6 %collective-permute-start.4 = (f32[2,648,128]{2,1,0:T(8,128)}, f32[2,648,128]{2,1,0:T(8,128)}, u32[]{:S(2)}, u32[]{:S(2)}) collective-permute-start(f32[2,648,128]{2,1,0:T(8,128)} %pad_maximum_fusion), channel_id=1, source_target_pairs={{0,32},{8,40},{16,48},{24,56},{32,64},{40,72},{48,80},{56,88},{64,... | collective-permute-start | bytes 1990664 | tf_op jit(solution)/shard_map/ppermute | solution.py:440
  33.4 0.1 copy_bitcast_fusion.3
  33.5 0.1 copy_bitcast_fusion.1
  33.6 0.5 concatenate.6.c_ref
  34.2 0.0 copy-done.1
  34.2 0.0 copy-done.2
  34.2 38.6 %shard_map.65.r_ref = f32[9,16,8,4,128]{4,3,2,1,0:T(4,128)S(1)} custom-call(f32[4,9,4,1440]{3,2,1,0:T(4,128)S(1)} %bitcast.24, f32[3,9,4,1440]{3,2,1,0:T(4,128)S(1)} %collective-permute-done.south_ref, f32[3,9,4,1440]{3,2,1,0:T(4,128)S(1)} %collective-permute-done.1.north_ref, f32[9,4,1440]{2,1,0:T(4,128)S(1)} %copy-done.2, f32[9,4,1440]{2,1,0:T(4,128)S(1)} %copy-done.1, ...), custom_call_target="tpu_custom_call" | custom-call | tf_op jit(solution)/shard_map/pallas_call | solution.py:443
  72.8 1.1 constant_dynamic-update-slice_fusion.3
  73.9 0.0 collective-permute-done.6
  73.9 0.0 collective-permute-done.5
  74.0 0.0 collective-permute-done.4
  74.0 1.1 constant_dynamic-update-slice_fusion.2
  75.1 1.1 constant_dynamic-update-slice_fusion.1
  76.2 1.1 constant_dynamic-update-slice_fusion.near_ref
  77.4 2.3 %collective-permute-start.7 = (f32[8,648,128]{2,1,0:T(8,128)S(1)}, f32[8,648,128]{2,1,0:T(8,128)S(1)}, u32[]{:S(2)}, u32[]{:S(2)}) collective-permute-start(f32[8,648,128]{2,1,0:T(8,128)S(1)} %constant_dynamic-update-slice_fusion.near_ref), channel_id=1, source_target_pairs={{0,8},{8,0},{16,24},{24,16},{32,40},{40,32},{48,56},{56,48},{64,72... | collective-permute-start | bytes 7962632 | tf_op jit(solution)/shard_map/ppermute | solution.py:463
  79.7 4.6 %collective-permute-done.7.far_ref = f32[8,648,128]{2,1,0:T(8,128)S(1)} collective-permute-done((f32[8,648,128]{2,1,0:T(8,128)S(1)}, f32[8,648,128]{2,1,0:T(8,128)S(1)}, u32[]{:S(2)}, u32[]{:S(2)}) %collective-permute-start.7) | collective-permute-done | bytes 2654240 | tf_op jit(solution)/shard_map/ppermute | solution.py:463
  84.3 1.5 %copy-done.4 = f32[8,648,128]{2,1,0:T(8,128)} copy-done((f32[8,648,128]{2,1,0:T(8,128)}, f32[8,648,128]{2,1,0:T(8,128)S(1)}, u32[]{:S(2)}) %copy-start.4) | copy-done | bytes 2654232
  85.8 44.1 %shard_map.66 = f32[2,9,8,1440]{3,2,1,0:T(8,128)S(1)} custom-call(f32[9,16,8,4,128]{4,3,2,1,0:T(4,128)S(1)} %shard_map.65.r_ref, f32[8,648,128]{2,1,0:T(8,128)S(1)} %constant_dynamic-update-slice_fusion.near_ref, f32[8,648,128]{2,1,0:T(8,128)} %copy-done.4, s32[4,256]{1,0:T(4,128)S(1)} %pad.4.slot_ref), custom_call_target="tpu_custom_call" | custom-call | tf_op jit(solution)/shard_map/pallas_call | solution.py:464
  129.9 0.0 copy-start.3
  129.9 0.3 reshape.23
  130.2 0.5 copy.23
  130.7 0.8 reshape.24
  131.4 0.0 copy-done.3
  131.4 1.1 sub.10
  (8 shorter events, 0.1 us)
Async XLA Ops:
  0.0 17.2 %copy-start.5 = (s32[4,180,1]{1,2,0:T(1,128)S(1)}, s32[4,180,1]{1,2,0:T(1,128)}, u32[]{:S(2)}) copy-start(s32[4,180,1]{1,2,0:T(1,128)} %param.10) | copy-start | bytes 8644
  1.0 18.8 %collective-permute-start.2 = (f32[9,1,1440]{2,1,0:T(1,128)S(1)}, f32[9,1,1440]{2,1,0:T(1,128)S(1)}, u32[]{:S(2)}, u32[]{:S(2)}) collective-permute-start(f32[9,1,1440]{2,1,0:T(1,128)S(1)} %slice.23), channel_id=1, source_target_pairs={{8,0},{16,8},{24,16},{32,24},{40,32},{48,40},{56,48},{64,56},{72,6... | collective-permute-start | bytes 155528 | tf_op jit(solution)/shard_map/ppermute | solution.py:427
  6.4 1.0 copy-start
  9.6 9.3 %collective-permute-start.3 = (f32[648,128]{1,0:T(8,128)S(1)}, f32[648,128]{1,0:T(8,128)S(1)}, u32[]{:S(2)}, u32[]{:S(2)}) collective-permute-start(f32[648,128]{1,0:T(8,128)S(1)} %shard_map.64), channel_id=1, source_target_pairs={{0,16},{8,24},{16,0},{24,8},{32,48},{40,56},{48,32},{56,40},{64,80... | collective-permute-start | bytes 995336 | tf_op jit(solution)/shard_map/ppermute | solution.py:420
  12.8 21.4 %copy-start.1 = (f32[9,4,1440]{2,1,0:T(4,128)S(1)}, f32[9,4,1440]{2,1,0:T(4,128)}, u32[]{:S(2)}) copy-start(f32[9,4,1440]{2,1,0:T(4,128)} %mer_ref.1) | copy-start | bytes 622084
  12.8 21.4 %copy-start.2 = (f32[9,4,1440]{2,1,0:T(4,128)S(1)}, f32[9,4,1440]{2,1,0:T(4,128)}, u32[]{:S(2)}) copy-start(f32[9,4,1440]{2,1,0:T(4,128)} %zon_ref.1) | copy-start | bytes 622084
  12.8 10.9 %collective-permute-start.1 = (f32[3,9,4,1440]{3,2,1,0:T(4,128)}, f32[3,9,4,1440]{3,2,1,0:T(4,128)S(1)}, u32[]{:S(2)}, u32[]{:S(2)}) collective-permute-start(f32[3,9,4,1440]{3,2,1,0:T(4,128)} %get-tuple-element.21), channel_id=1, source_target_pairs={{8,0},{16,8},{24,16},{32,24},{40,32},{48,40},{56,48},{64,56},{72,6... | collective-permute-start | bytes 1866248 | tf_op jit(solution)/shard_map/ppermute | solution.py:426
  15.1 14.7 %collective-permute-start = (f32[3,9,4,1440]{3,2,1,0:T(4,128)}, f32[3,9,4,1440]{3,2,1,0:T(4,128)S(1)}, u32[]{:S(2)}, u32[]{:S(2)}) collective-permute-start(f32[3,9,4,1440]{3,2,1,0:T(4,128)} %get-tuple-element.22), channel_id=1, source_target_pairs={{0,8},{8,16},{16,24},{24,32},{32,40},{40,48},{48,56},{56,64},{64,7... | collective-permute-start | bytes 1866248 | tf_op jit(solution)/shard_map/ppermute | solution.py:425
  29.8 44.1 %collective-permute-start.6 = (f32[2,648,128]{2,1,0:T(8,128)}, f32[2,648,128]{2,1,0:T(8,128)}, u32[]{:S(2)}, u32[]{:S(2)}) collective-permute-start(f32[2,648,128]{2,1,0:T(8,128)} %pad_maximum_fusion), channel_id=1, source_target_pairs={{0,96},{8,104},{16,112},{24,120},{32,0},{40,8},{48,16},{56,24},{64... | collective-permute-start | bytes 1990664 | tf_op jit(solution)/shard_map/ppermute | solution.py:440
  30.3 43.7 %collective-permute-start.5 = (f32[2,648,128]{2,1,0:T(8,128)}, f32[2,648,128]{2,1,0:T(8,128)}, u32[]{:S(2)}, u32[]{:S(2)}) collective-permute-start(f32[2,648,128]{2,1,0:T(8,128)} %pad_maximum_fusion), channel_id=1, source_target_pairs={{0,64},{8,72},{16,80},{24,88},{32,96},{40,104},{48,112},{56,120},{... | collective-permute-start | bytes 1990664 | tf_op jit(solution)/shard_map/ppermute | solution.py:440
  30.8 43.2 %collective-permute-start.4 = (f32[2,648,128]{2,1,0:T(8,128)}, f32[2,648,128]{2,1,0:T(8,128)}, u32[]{:S(2)}, u32[]{:S(2)}) collective-permute-start(f32[2,648,128]{2,1,0:T(8,128)} %pad_maximum_fusion), channel_id=1, source_target_pairs={{0,32},{8,40},{16,48},{24,56},{32,64},{40,72},{48,80},{56,88},{64,... | collective-permute-start | bytes 1990664 | tf_op jit(solution)/shard_map/ppermute | solution.py:440
  77.4 6.9 %collective-permute-start.7 = (f32[8,648,128]{2,1,0:T(8,128)S(1)}, f32[8,648,128]{2,1,0:T(8,128)S(1)}, u32[]{:S(2)}, u32[]{:S(2)}) collective-permute-start(f32[8,648,128]{2,1,0:T(8,128)S(1)} %constant_dynamic-update-slice_fusion.near_ref), channel_id=1, source_target_pairs={{0,8},{8,0},{16,24},{24,16},{32,40},{40,32},{48,56},{56,48},{64,72... | collective-permute-start | bytes 7962632 | tf_op jit(solution)/shard_map/ppermute | solution.py:463
  84.3 1.5 %copy-start.4 = (f32[8,648,128]{2,1,0:T(8,128)}, f32[8,648,128]{2,1,0:T(8,128)S(1)}, u32[]{:S(2)}) copy-start(f32[8,648,128]{2,1,0:T(8,128)S(1)} %collective-permute-done.7.far_ref) | copy-start | bytes 7962628
  129.9 1.5 %copy-start.3 = (f32[4,9,4,1440]{3,2,1,0:T(4,128)S(1)}, f32[4,9,4,1440]{3,2,1,0:T(4,128)}, u32[]{:S(2)}) copy-start(f32[4,9,4,1440]{3,2,1,0:T(4,128)} %param.6) | copy-start | bytes 2488324

commit v3 on v2

--- a/solution.py
+++ b/solution.py
@@ -36,7 +36,7 @@
     return (7.0 / 12.0) * (q_m1 + q_0) - (1.0 / 12.0) * (q_m2 + q_p1)
 
 
-def horizontal(tr_ref, south_ref, north_ref, zon_ref, mer_ref, mern_ref, g_ref, ready):
+def horizontal(tr_ref, south_ref, north_ref, zon_ref, mer_ref, g_ref, ready):
     lat = lax.axis_index("lat")
     last = lax.axis_size("lat") - 1
     width = tr_ref.shape[3]
@@ -61,7 +61,7 @@
     def level(k, carry):
         row = [tr_ref[r, k] for r in range(4)]
         low = [south_ref[r, k] * ksouth for r in range(3)]
-        high = [north_ref[r, k] * knorth for r in range(3)]
+        high = [north_ref[r * tr_ref.shape[1] + k] * knorth for r in range(3)]
         pair = lambda a, b: jnp.concatenate([a, b], axis=0)
         q = [
             pair(low[0], low[0]),
@@ -85,7 +85,7 @@
         zero = jnp.zeros((8, width), F32)
         m0 = jnp.where(sub, m[0:1] * ksouth, m[1:2])
         m1 = jnp.where(sub, m[2:3], m[3:4])
-        m2 = mern_ref[k] * knorth + zero
+        m2 = north_ref[3 * tr_ref.shape[1] + k // 4, pl.ds(k % 4, 1), :] * knorth + zero
         f = []
         for i, c in enumerate((m0, m1, m2)):
             p = i + 1
@@ -198,18 +198,23 @@
         ready(r)
 
 
-def reorder_kernel(m_ref, o_ref):
+def reorder_kernel(m_ref, n_ref, o_ref):
     order = m_ref.shape[0]
     levels = order // 4
     x = lax.broadcasted_iota(jnp.int32, (order, order), 0)
     o = lax.broadcasted_iota(jnp.int32, (order, order), 1)
-    pick = ((x & 3) * levels + (x >> 2) == o).astype(F32)
-    exact = dict(precision=lax.Precision.HIGHEST, preferred_element_type=F32)
-    out = lax.dot_general(lax.dot_general(pick, m_ref[...], NN, **exact), pick, NT, **exact)
+    pick = ((x & 3) * levels + (x >> 2) == o).astype(F32).astype(BF16)
     part = order // 4
-    o_ref[0:order] = out[:, 0:128]
-    o_ref[order : 2 * order] = out[:, 128:256]
-    o_ref[2 * order :] = jnp.concatenate([out[part * i : part * i + part, 256:] for i in range(4)], axis=1)
+    for n, ref in enumerate((m_ref, n_ref)):
+        hi, lo = split(ref[...])
+        rest = (ref[...] - hi.astype(F32) - lo.astype(F32)).astype(BF16)
+        out = None
+        for piece in (hi, lo, rest):
+            term = dot(dot(pick, piece).astype(BF16), pick, NT)
+            out = term if out is None else out + term
+        o_ref[n, 0:order] = out[:, 0:128]
+        o_ref[n, order : 2 * order] = out[:, 128:256]
+        o_ref[n, 2 * order :] = jnp.concatenate([out[part * i : part * i + part, 256:] for i in range(4)], axis=1)
 
 
 def unpacked(packed):
@@ -266,10 +271,14 @@
 
 
 def greet(lat, lev, levs):
-    barrier = pltpu.get_barrier_semaphore()
     for i in range(1, levs):
-        pl.semaphore_signal(barrier, inc=1, device_id=(lat, lax.rem(lev + i, levs)), device_id_type=MESH)
-    pl.semaphore_wait(barrier, levs - 1)
+        pl.semaphore_signal(
+            pltpu.get_barrier_semaphore(), inc=1, device_id=(lat, lax.rem(lev + i, levs)), device_id_type=MESH
+        )
+
+
+def greeted(levs):
+    pl.semaphore_wait(pltpu.get_barrier_semaphore(), levs - 1)
 
 
 def send(src, dst, ssem, rsem, lat, to):
@@ -279,12 +288,13 @@
 
 
 def forth_kernel(
-    rest, levs, tr_ref, south_ref, north_ref, zon_ref, mer_ref, mern_ref, c_ref, slot_ref,
+    rest, levs, tr_ref, south_ref, north_ref, zon_ref, mer_ref, c_ref, slot_ref,
     r_ref, g_ref, col_ref, p_ref, a_ref, s1, r1, s2, r2, lsem,
 ):
     lat, lev = lax.axis_index("lat"), lax.axis_index("lev")
     block = tr_ref.shape[1]
     greet(lat, lev, levs)
+    greeted(levs)
 
     def level_copy(k, i):
         to = lax.rem(lev + i, levs)
@@ -294,7 +304,7 @@
         for i in range(1, levs):
             level_copy(k, i).start()
 
-    horizontal(tr_ref, south_ref, north_ref, zon_ref, mer_ref, mern_ref, g_ref, level_ready)
+    horizontal(tr_ref, south_ref, north_ref, zon_ref, mer_ref, g_ref, level_ready)
     own = pltpu.make_async_copy(g_ref.at[lev], col_ref.at[lev], lsem.at[0])
     own.start()
     own.wait()
@@ -325,29 +335,19 @@
 
 
 def back_kernel(
-    rest, levs, order, r_ref, near_ref, far_ref, slot_ref,
+    rest, levs, order, r_ref, n0, n1, n2, n3, f0, f1, f2, f3, slot_ref,
     o_ref, y_ref, v_ref, w_ref, d_ref, own_ref, s1, r1, s2, r2, lsem,
 ):
     lat, lev = lax.axis_index("lat"), lax.axis_index("lev")
-    lats = r_ref.shape[1]
-    size = lats // CHUNKS
+    size = r_ref.shape[1] // CHUNKS
     greet(lat, lev, levs)
 
-    def back_copy(q, i):
+    def back_copy(d, i):
         to = lax.rem(lev + i, levs)
-        part = slice(q * size, q * size + size)
-        return send(y_ref.at[:, part, to, 0:3], v_ref.at[:, lev, part, 0:3], s1.at[q, i], r1.at[q, i], lat, to)
-
-    @pl.loop(0, lats // 2)
-    def _(n):
-        steps, turn = n // 2, lax.rem(n, 2)
-        chip = lax.rem(lat // 4 - steps + 4, 4) * 4 + lax.rem(lat // 2 + turn, 2) * 2
-        for ref, core in ((near_ref, lax.rem(lat, 2)), (far_ref, lax.rem(lat + 1, 2))):
-            hi, lo = split(unpacked(ref[n]))
-            w_ref[0, chip + core] = hi
-            w_ref[1, chip + core] = lo
-
-    def mix(n):
+        part = pl.ds(lax.rem(lat // 4 - d + 4, 4) * size, size)
+        return send(y_ref.at[:, part, to, 0:3], v_ref.at[:, lev, part, 0:3], s1.at[d, i], r1.at[d, i], lat, to)
+
+    def mix(n, at):
         tiles = [r_ref[j, n].reshape(4 * levs, 128) for j in range(9)]
         rows = []
         for r in range(4):
@@ -356,7 +356,7 @@
                 x = pltpu.roll(x, 384 - 32 * r, 1)
             rows.append(x[:, :order])
         hi, lo = split(jnp.concatenate(rows, axis=0))
-        y = dot(hi, w_ref[0, n], NT) + dot(lo, w_ref[0, n], NT) + dot(hi, w_ref[1, n], NT)
+        y = dot(hi, w_ref[0, at], NT) + dot(lo, w_ref[0, at], NT) + dot(hi, w_ref[1, at], NT)
         many = 4 * levs
         carried = None
         for r in range(4):
@@ -372,10 +372,21 @@
                     continue
                 y_ref[2 * r + t, n] = part.reshape(levs, 4, 128)
 
-    for q in range(CHUNKS):
-        pl.loop(q * size, q * size + size)(mix)
+    for d, refs in enumerate(((n0, f0), (n1, f1), (n2, f2), (n3, f3))):
+        base = lax.rem(lat // 4 - d + 4, 4) * size
+        for at in range(4):
+            hi, lo = split(unpacked(refs[at % 2][at // 2]))
+            w_ref[0, at] = hi
+            w_ref[1, at] = lo
+
+        @pl.loop(0, size)
+        def _(at):
+            mix(base + lax.rem(lat // 2 + at // 2, 2) * 2 + lax.rem(lat + at, 2), at)
+
+        if d == 0:
+            greeted(levs)
         for i in range(1, levs):
-            back_copy(q, i).start()
+            back_copy(d, i).start()
     own = pltpu.make_async_copy(y_ref.at[:, :, lev, 0:3], v_ref.at[:, lev, :, 0:3], lsem.at[0])
     own.start()
     own.wait()
@@ -416,15 +427,17 @@
     levels, _, lon = vertical.shape
     rest = lon - 128
     order = inverse.shape[2]
-    matrix = call(reorder_kernel, (order * order // 128, 128), 1)(inverse[0, 0])
-    across = lax.ppermute(matrix, "lat", [(i, i ^ 2) for i in range(lats)])
-    pair = jnp.stack([matrix, across])
+    own = inverse[0, 0]
+    across = lax.ppermute(own, "lat", [(i, i ^ 2) for i in range(lats)])
     turned = jnp.transpose(tracers, (2, 1, 0, 3))
     up = [(i, i + 1) for i in range(lats - 1)]
     down = [(i + 1, i) for i in range(lats - 1)]
     south = lax.ppermute(turned[rows - 3 :], "lat", up)
-    north = lax.ppermute(turned[:3], "lat", down)
-    mer_north = lax.ppermute(meridional[:, :1], "lat", down)
+    edge = jnp.pad(meridional[:, 0], ((0, -levs_here % 4), (0, 0))).reshape(-1, 4, width)
+    north = lax.ppermute(
+        jnp.concatenate([turned[:3].reshape(3 * levs_here, trac, width), edge], axis=0), "lat", down
+    )
+    pair = call(reorder_kernel, (2, order * order // 128, 128), 2)(own, across)
     targets = route[:, :, 0]
     before = jnp.arange(lon)[:, None] < jnp.arange(lon)[None, :]
     same = jnp.logical_and(targets[:, :, None] == targets[:, None, :], before[None])
@@ -436,14 +449,16 @@
         [v[:, 0, :, :128], v[:, 1, :, :128], v[:, 0, :, 128:], v[:, 1, :, 128:], jnp.zeros((levels, 2, 128 - 2 * rest), F32)],
         axis=-1,
     )
-    south, north, mer_north, pair = lax.optimization_barrier((south, north, mer_north, pair))
     shifted = [lax.ppermute(pair, "lat", [(i, (i + 4 * d) % lats) for i in range(lats)]) for d in range(1, 4)]
+    other = [(i, i ^ 1) for i in range(lats)]
+    far = [lax.ppermute(pair, "lat", other)]
+    south, north, pair = lax.optimization_barrier((south, north, pair))
     dma = pltpu.SemaphoreType.DMA
     levels_of = pltpu.VMEM((groups, levs_here, 8, 384), F32)
     received = call(
         functools.partial(forth_kernel, rest, groups),
         (9, lats, groups, 4, 128),
-        8,
+        7,
         [
             levels_of,
             levels_of,
@@ -457,18 +472,17 @@
         ],
         collective_id=0,
         has_side_effects=True,
-    )(turned, south, north, zonal, meridional, mer_north, courant, slots)
+    )(turned, south, north, zonal, meridional, courant, slots)
     received, shifted = lax.optimization_barrier((received, shifted))
-    near = jnp.concatenate([pair] + shifted, axis=0)
-    far = lax.ppermute(near, "lat", [(i, i ^ 1) for i in range(lats)])
+    far += [lax.ppermute(x, "lat", other) for x in shifted]
     whole = call(
         functools.partial(back_kernel, rest, groups, order),
         (2, levs_here, 8, width),
-        4,
+        10,
         [
             pltpu.VMEM((9, lats, groups, 4, 128), F32),
             pltpu.VMEM((9, groups, lats, 4, 128), F32),
-            pltpu.VMEM((2, lats, order, order), BF16),
+            pltpu.VMEM((2, lats // CHUNKS, order, order), BF16),
             levels_of,
             levels_of,
             dma((CHUNKS, groups)),
@@ -479,7 +493,7 @@
         ],
         collective_id=1,
         has_side_effects=True,
-    )(received, near, far, slots)
+    )(received, pair, *shifted, *far, slots)
     whole = whole.reshape(2, levs_here, 2, trac, width)
     return jnp.transpose(whole, (3, 1, 0, 2, 4)).reshape(tracers.shape) - tracers
 

time: 135 us -> 126 us (0.933)
  waiting for transfers between devices: 14.6 us -> 7.72 us
    ppermute x1, waiting for transfers between devices: 6.17 us -> 0.01 us  [body(): south = lax.ppermute(turned[rows - 3:], 'lat', up)]
    pallas_call x1, Pallas kernels: 44.1 us -> 40.8 us  [body(): call(functools.partial(back_kernel, rest, groups, order), (2, levs_here,...]
    pallas_call x1, Pallas kernels: 38.6 us -> 41 us  [body(): call(functools.partial(forth_kernel, rest, groups), (9, lats, groups, 4,...]
    unnamed x18 -> x20, local copies, waits for them, and re-layouts: 8.48 us -> 7.74 us
    ppermute x4 -> x6, waiting for transfers between devices: 8.44 us -> 7.71 us  [the longest x1 4.09 us: body(): across = lax.ppermute(own, 'lat', [(i, i ^ 2) for i in range(lats)])]
    ppermute x4 -> x6, starting transfers between devices: 10.5 us -> 10.8 us  [the longest x1 6.16 us: body(): lax.ppermute(jnp.concatenate([turned[:3].reshape(3 * levs_here, trac, wid...]
  transfers between devices with their start and end apart: 8 -> 10, of which waited for: 3 -> 4; matrix products, arithmetic and copies ran while one was open for 5% -> 6% of each run, Pallas kernels for 31% -> 35%
where the time goes in v3:
time: 126 us; the launch traced here: 124 us
  Pallas kernels  83.9 us (67%)
  starting transfers between devices  16.6 us (13%)
  local copies, waits for them, and re-layouts  13.2 us (10%)
  waiting for transfers between devices  7.72 us (6%)
  other arithmetic  2.61 us (2%)
    pallas_call x1, Pallas kernels, body(): call(functools.partial(forth_kernel, rest, groups), (9, lats, groups, 4,...  41 us
    pallas_call x1, Pallas kernels, body(): call(functools.partial(back_kernel, rest, groups, order), (2, levs_here,...  40.8 us
    unnamed x20, local copies, waits for them, and re-layouts  7.74 us
    ppermute x1, starting transfers between devices, body(): lax.ppermute(jnp.concatenate([turned[:3].reshape(3 * levs_here, trac, wid...  6.16 us
    ppermute x1, waiting for transfers between devices, body(): across = lax.ppermute(own, 'lat', [(i, i ^ 2) for i in range(lats)])  4.09 us
    ppermute x3, starting transfers between devices, body(): lax.ppermute(pair, 'lat', [(i, (i + 4 * d) % lats) for i in range(lats)])  3.93 us
    ppermute x1, starting transfers between devices, body(): across = lax.ppermute(own, 'lat', [(i, i ^ 2) for i in range(lats)])  3.88 us
    ppermute x3, waiting for transfers between devices, body(): far += [lax.ppermute(x, 'lat', other) for x in shifted]  3.61 us
  transfers between devices with their start and end apart: 10, of which 4 were waited for; matrix products, arithmetic and copies ran while one was open for 6% of the time, Pallas kernels for 35%

profile of v3, /device:TPU:24, one launch (start us, length us, event | category | flops | bytes accessed | tf_op | source)
XLA Modules:
  0.0 124.3 jit_solution(14026874199479037429)
XLA Ops:
  0.0 3.9 %collective-permute-start.2 = (f32[288,288]{1,0:T(8,128)}, f32[288,288]{1,0:T(8,128)S(1)}, u32[]{:S(2)}, u32[]{:S(2)}) collective-permute-start(f32[288,288]{1,0:T(8,128)} %bitcast.27), channel_id=1, source_target_pairs={{0,16},{8,24},{16,0},{24,8},{32,48},{40,56},{48,32},{56,40},{64,80... | collective-permute-start | bytes 995336 | tf_op jit(solution)/shard_map/ppermute | solution.py:431
  3.9 1.5 %copy.41 = f32[4,9,4,1440]{3,0,1,2:T(4,128)S(1)} copy(f32[4,9,4,1440]{3,2,1,0:T(4,128)} %param.6) | data formatting | bytes 1658880 | tf_op args[0]
  5.4 0.0 copy-start.7
  5.4 1.0 fusion.6
  6.4 1.9 %collective-permute-start = (f32[3,9,4,1440]{3,2,1,0:T(4,128)}, f32[3,9,4,1440]{3,2,1,0:T(4,128)S(1)}, u32[]{:S(2)}, u32[]{:S(2)}) collective-permute-start(f32[3,9,4,1440]{3,2,1,0:T(4,128)} %get-tuple-element.20), channel_id=1, source_target_pairs={{0,8},{8,16},{16,24},{24,32},{32,40},{40,48},{48,56},{56,64},{64,7... | collective-permute-start | bytes 1866248 | tf_op jit(solution)/shard_map/ppermute | solution.py:435
  8.3 0.0 slice-done
  8.4 1.0 pad_maximum_fusion
  9.4 6.2 %collective-permute-start.1 = (f32[30,4,1440]{2,1,0:T(4,128)}, f32[30,4,1440]{2,1,0:T(4,128)S(1)}, u32[]{:S(2)}, u32[]{:S(2)}) collective-permute-start(f32[30,4,1440]{2,1,0:T(4,128)} %pad_maximum_fusion), channel_id=1, source_target_pairs={{8,0},{16,8},{24,16},{32,24},{40,32},{48,40},{56,48},{64,56},{72,6... | collective-permute-start | bytes 2073608 | tf_op jit(solution)/shard_map/ppermute | solution.py:437
  15.6 0.0 copy-done.7
  15.7 0.1 copy.24
  15.8 0.4 convert_reduce_fusion
  16.2 1.0 copy.19
  17.3 4.1 %collective-permute-done.2.n_ref = f32[288,288]{1,0:T(8,128)S(1)} collective-permute-done((f32[288,288]{1,0:T(8,128)}, f32[288,288]{1,0:T(8,128)S(1)}, u32[]{:S(2)}, u32[]{:S(2)}) %collective-permute-start.2) | collective-permute-done | bytes 331808 | tf_op jit(solution)/shard_map/ppermute | solution.py:431
  21.4 0.8 copy-done.2
  22.1 1.0 copy-done.1
  23.2 1.0 copy-done.3
  24.2 2.0 %shard_map.64.n0 = f32[2,648,128]{2,1,0:T(8,128)S(1)} custom-call(f32[288,288]{1,0:T(8,128)S(1)} %bitcast.28, f32[288,288]{1,0:T(8,128)S(1)} %copy-done.3), custom_call_target="tpu_custom_call" | custom-call | tf_op jit(solution)/shard_map/pallas_call | solution.py:440
  26.2 0.8 collective-permute-start.5
  27.0 0.6 collective-permute-start.4
  27.6 2.5 %collective-permute-start.3 = (f32[2,648,128]{2,1,0:T(8,128)S(1)}, f32[2,648,128]{2,1,0:T(8,128)}, u32[]{:S(2)}, u32[]{:S(2)}) collective-permute-start(f32[2,648,128]{2,1,0:T(8,128)S(1)} %shard_map.64.n0), channel_id=1, source_target_pairs={{0,32},{8,40},{16,48},{24,56},{32,64},{40,72},{48,80},{56,88},{64,... | collective-permute-start | bytes 1990664 | tf_op jit(solution)/shard_map/ppermute | solution.py:452
  30.2 0.7 copy_bitcast_fusion.4
  30.9 0.7 copy_bitcast_fusion.2
  31.7 1.3 %concatenate.7.c_ref = f32[72,2,384]{2,1,0:T(2,128)S(1)} concatenate(f32[72,2,128]{2,1,0:T(2,128)} %get-tuple-element.26, f32[72,2,128]{2,1,0:T(2,128)S(1)} %get-tuple-element.25, f32[72,2,52]{2,1,0:T(2,128)} %get-tuple-element.28, f32[72,2,52]{2,1,0:T(2,128)} %get-tuple-element.27, f32[72,2,24]{2,1,0:T(2,128)S(1)} %broadcast_in_dim.2), dimensions={2} | concatenate | bytes 442368 | tf_op jit(solution)/shard_map/concatenate | solution.py:448
  33.0 0.0 collective-permute-done.south_ref
  33.0 0.1 collective-permute-start.6
  33.1 0.0 collective-permute-done.1.north_ref
  33.1 0.0 copy-done.4
  33.1 0.0 copy-start.5
  33.1 0.9 copy-done.5
  34.0 41.0 %shard_map.65.r_ref = f32[9,16,8,4,128]{4,3,2,1,0:T(4,128)S(1)} custom-call(f32[4,9,4,1440]{3,2,1,0:T(4,128)S(1)} %bitcast.26, f32[3,9,4,1440]{3,2,1,0:T(4,128)S(1)} %collective-permute-done.south_ref, f32[30,4,1440]{2,1,0:T(4,128)S(1)} %collective-permute-done.1.north_ref, f32[9,4,1440]{2,1,0:T(4,128)S(1)} %copy-done.5, f32[9,4,1440]{2,1,0:T(4,128)S(1)} %copy-done.4, ...), custom_call_target="tpu_custom_call" | custom-call | tf_op jit(solution)/shard_map/pallas_call | solution.py:458
  75.1 0.0 copy-start
  75.1 1.4 %copy-done = f32[9,16,8,4,128]{4,3,2,1,0:T(4,128)} copy-done((f32[9,16,8,4,128]{4,3,2,1,0:T(4,128)}, f32[9,16,8,4,128]{4,3,2,1,0:T(4,128)S(1)}, u32[]{:S(2)}) %copy-start) | copy-done | bytes 2359320
  76.5 0.0 collective-permute-done.5.n3
  76.5 0.0 collective-permute-done.4.n2
  76.5 0.0 collective-permute-done.3.n1
  76.5 0.1 collective-permute-start.7
  76.6 0.5 collective-permute-start.8
  77.1 0.1 collective-permute-start.9
  77.2 0.0 collective-permute-done.6.f0
  77.2 1.7 %collective-permute-done.7.f1 = f32[2,648,128]{2,1,0:T(8,128)S(1)} collective-permute-done((f32[2,648,128]{2,1,0:T(8,128)}, f32[2,648,128]{2,1,0:T(8,128)S(1)}, u32[]{:S(2)}, u32[]{:S(2)}) %collective-permute-start.7) | collective-permute-done | bytes 663584 | tf_op jit(solution)/shard_map/ppermute | solution.py:477
  78.9 0.9 collective-permute-done.8.f2
  79.9 0.9 collective-permute-done.9.f3
  80.8 40.8 %shard_map.66 = f32[2,9,8,1440]{3,2,1,0:T(8,128)S(1)} custom-call(f32[9,16,8,4,128]{4,3,2,1,0:T(4,128)} %copy-done, f32[2,648,128]{2,1,0:T(8,128)S(1)} %shard_map.64.n0, f32[2,648,128]{2,1,0:T(8,128)} %collective-permute-done.3.n1, f32[2,648,128]{2,1,0:T(8,128)} %collective-permute-done.4.n2, f32[2,648,128]{2,1,0:T(8,128)} %collective-permute-done.5.n3, ...), custom_call_target="tpu_custom_call" | custom-call | tf_op jit(solution)/shard_map/pallas_call | solution.py:478
  121.7 0.0 copy-start.6
  121.7 0.3 reshape.31
  121.9 0.5 copy.25
  122.4 0.8 reshape.32
  123.2 1.1 sub.10
  (16 shorter events, 0.1 us)
Async XLA Ops:
  0.0 8.3 %slice-start = ((f32[9,4,1440]{2,1,0:T(4,128)}), f32[9,1,1440]{2,1,0:T(1,128)S(1)}, s32[]{:S(2)}) async-start(f32[9,4,1440]{2,1,0:T(4,128)} %mer_ref.1), calls=%async_computation | async-start | bytes 110592 | tf_op jit(solution)/shard_map/slice | solution.py:436
  0.0 21.4 %collective-permute-start.2 = (f32[288,288]{1,0:T(8,128)}, f32[288,288]{1,0:T(8,128)S(1)}, u32[]{:S(2)}, u32[]{:S(2)}) collective-permute-start(f32[288,288]{1,0:T(8,128)} %bitcast.27), channel_id=1, source_target_pairs={{0,16},{8,24},{16,0},{24,8},{32,48},{40,56},{48,32},{56,40},{64,80... | collective-permute-start | bytes 995336 | tf_op jit(solution)/shard_map/ppermute | solution.py:431
  5.4 10.3 %copy-start.7 = (s32[4,180,1]{1,2,0:T(1,128)S(1)}, s32[4,180,1]{1,2,0:T(1,128)}, u32[]{:S(2)}) copy-start(s32[4,180,1]{1,2,0:T(1,128)} %param.10) | copy-start | bytes 8644
  6.4 26.5 %collective-permute-start = (f32[3,9,4,1440]{3,2,1,0:T(4,128)}, f32[3,9,4,1440]{3,2,1,0:T(4,128)S(1)}, u32[]{:S(2)}, u32[]{:S(2)}) collective-permute-start(f32[3,9,4,1440]{3,2,1,0:T(4,128)} %get-tuple-element.20), channel_id=1, source_target_pairs={{0,8},{8,16},{16,24},{24,32},{32,40},{40,48},{48,56},{56,64},{64,7... | collective-permute-start | bytes 1866248 | tf_op jit(solution)/shard_map/ppermute | solution.py:435
  9.4 23.6 %copy-start.4 = (f32[9,4,1440]{2,1,0:T(4,128)S(1)}, f32[9,4,1440]{2,1,0:T(4,128)}, u32[]{:S(2)}) copy-start(f32[9,4,1440]{2,1,0:T(4,128)} %mer_ref.1) | copy-start | bytes 622084
  9.4 23.6 %collective-permute-start.1 = (f32[30,4,1440]{2,1,0:T(4,128)}, f32[30,4,1440]{2,1,0:T(4,128)S(1)}, u32[]{:S(2)}, u32[]{:S(2)}) collective-permute-start(f32[30,4,1440]{2,1,0:T(4,128)} %pad_maximum_fusion), channel_id=1, source_target_pairs={{8,0},{16,8},{24,16},{32,24},{40,32},{48,40},{56,48},{64,56},{72,6... | collective-permute-start | bytes 2073608 | tf_op jit(solution)/shard_map/ppermute | solution.py:437
  21.4 0.8 copy-start.2
  22.1 1.0 copy-start.1
  23.2 1.0 copy-start.3
  26.2 50.3 %collective-permute-start.5 = (f32[2,648,128]{2,1,0:T(8,128)S(1)}, f32[2,648,128]{2,1,0:T(8,128)}, u32[]{:S(2)}, u32[]{:S(2)}) collective-permute-start(f32[2,648,128]{2,1,0:T(8,128)S(1)} %shard_map.64.n0), channel_id=1, source_target_pairs={{0,96},{8,104},{16,112},{24,120},{32,0},{40,8},{48,16},{56,24},{64... | collective-permute-start | bytes 1990664 | tf_op jit(solution)/shard_map/ppermute | solution.py:452
  27.0 49.5 %collective-permute-start.4 = (f32[2,648,128]{2,1,0:T(8,128)S(1)}, f32[2,648,128]{2,1,0:T(8,128)}, u32[]{:S(2)}, u32[]{:S(2)}) collective-permute-start(f32[2,648,128]{2,1,0:T(8,128)S(1)} %shard_map.64.n0), channel_id=1, source_target_pairs={{0,64},{8,72},{16,80},{24,88},{32,96},{40,104},{48,112},{56,120},{... | collective-permute-start | bytes 1990664 | tf_op jit(solution)/shard_map/ppermute | solution.py:452
  27.6 48.9 %collective-permute-start.3 = (f32[2,648,128]{2,1,0:T(8,128)S(1)}, f32[2,648,128]{2,1,0:T(8,128)}, u32[]{:S(2)}, u32[]{:S(2)}) collective-permute-start(f32[2,648,128]{2,1,0:T(8,128)S(1)} %shard_map.64.n0), channel_id=1, source_target_pairs={{0,32},{8,40},{16,48},{24,56},{32,64},{40,72},{48,80},{56,88},{64,... | collective-permute-start | bytes 1990664 | tf_op jit(solution)/shard_map/ppermute | solution.py:452
  33.0 44.2 %collective-permute-start.6 = (f32[2,648,128]{2,1,0:T(8,128)S(1)}, f32[2,648,128]{2,1,0:T(8,128)S(1)}, u32[]{:S(2)}, u32[]{:S(2)}) collective-permute-start(f32[2,648,128]{2,1,0:T(8,128)S(1)} %shard_map.64.n0), channel_id=1, source_target_pairs={{0,8},{8,0},{16,24},{24,16},{32,40},{40,32},{48,56},{56,48},{64,72... | collective-permute-start | bytes 1990664 | tf_op jit(solution)/shard_map/ppermute | solution.py:454
  33.1 0.9 copy-start.5
  75.1 1.4 %copy-start = (f32[9,16,8,4,128]{4,3,2,1,0:T(4,128)}, f32[9,16,8,4,128]{4,3,2,1,0:T(4,128)S(1)}, u32[]{:S(2)}) copy-start(f32[9,16,8,4,128]{4,3,2,1,0:T(4,128)S(1)} %shard_map.65.r_ref) | copy-start | bytes 7077892
  76.5 2.4 %collective-permute-start.7 = (f32[2,648,128]{2,1,0:T(8,128)}, f32[2,648,128]{2,1,0:T(8,128)S(1)}, u32[]{:S(2)}, u32[]{:S(2)}) collective-permute-start(f32[2,648,128]{2,1,0:T(8,128)} %collective-permute-done.3.n1), channel_id=1, source_target_pairs={{0,8},{8,0},{16,24},{24,16},{32,40},{40,32},{48,56},{56,48},{64,72... | collective-permute-start | bytes 1990664 | tf_op jit(solution)/shard_map/ppermute | solution.py:477
  76.6 3.3 %collective-permute-start.8 = (f32[2,648,128]{2,1,0:T(8,128)}, f32[2,648,128]{2,1,0:T(8,128)S(1)}, u32[]{:S(2)}, u32[]{:S(2)}) collective-permute-start(f32[2,648,128]{2,1,0:T(8,128)} %collective-permute-done.4.n2), channel_id=1, source_target_pairs={{0,8},{8,0},{16,24},{24,16},{32,40},{40,32},{48,56},{56,48},{64,72... | collective-permute-start | bytes 1990664 | tf_op jit(solution)/shard_map/ppermute | solution.py:477
  77.1 3.7 %collective-permute-start.9 = (f32[2,648,128]{2,1,0:T(8,128)}, f32[2,648,128]{2,1,0:T(8,128)S(1)}, u32[]{:S(2)}, u32[]{:S(2)}) collective-permute-start(f32[2,648,128]{2,1,0:T(8,128)} %collective-permute-done.5.n3), channel_id=1, source_target_pairs={{0,8},{8,0},{16,24},{24,16},{32,40},{40,32},{48,56},{56,48},{64,72... | collective-permute-start | bytes 1990664 | tf_op jit(solution)/shard_map/ppermute | solution.py:477
  121.7 1.5 %copy-start.6 = (f32[4,9,4,1440]{3,2,1,0:T(4,128)S(1)}, f32[4,9,4,1440]{3,2,1,0:T(4,128)}, u32[]{:S(2)}) copy-start(f32[4,9,4,1440]{3,2,1,0:T(4,128)} %param.6) | copy-start | bytes 2488324

commit v4 on v3

--- a/solution.py
+++ b/solution.py
@@ -126,9 +126,9 @@
     lax.fori_loop(0, tr_ref.shape[1], level, 0)
 
 
-def selector(slot_ref, r):
+def selector(slots):
     ids = lax.broadcasted_iota(jnp.int32, (512, 256), 0)
-    return (ids == slot_ref[r : r + 1, :]).astype(F32).astype(BF16)
+    return (ids == slots).astype(F32).astype(BF16)
 
 
 def select(rest, g_ref, c_ref, slot_ref, p_ref, a_ref, ready):
@@ -158,7 +158,12 @@
         if k + 1 < levels:
             nxt = e_at(k + 2)
             s1, k1 = nxt - right, 6.0 * q(k + 1) - 3.0 * (right + nxt)
-            c = jnp.where(sub, c_ref[k + 1, 0:1, :], c_ref[k + 1, 1:2, :])
+            v = c_ref[k + 1]
+            c0 = jnp.where(sub[:, : 128 + rest], v[0:1], v[1:2])
+            c1 = jnp.where(sub[:, : 128 + rest], v[2:3], v[3:4])
+            c = jnp.concatenate(
+                [c0[:, :128], c1[:, :128], c0[:, 128:], c1[:, 128:], zero[:, : 128 - 2 * rest]], axis=1
+            )
             f_next = flux(c, right, s, s1, kk, k1)
             right, s, kk = nxt, s1, k1
         else:
@@ -185,7 +190,7 @@
             held = []
     carried = None
     for r in range(4):
-        one = selector(slot_ref, r)
+        one = selector(slot_ref[r : r + 1, :])
         out = dot(jnp.concatenate([one, one], axis=1), a_ref[r], NT)
         for t in range(3):
             part = out[:, 128 * t : 128 * t + 128]
@@ -198,19 +203,23 @@
         ready(r)
 
 
-def reorder_kernel(m_ref, n_ref, o_ref):
+def reorder_kernel(levs, m_ref, n_ref, o_ref):
     order = m_ref.shape[0]
     levels = order // 4
+    block = levels // levs
     x = lax.broadcasted_iota(jnp.int32, (order, order), 0)
     o = lax.broadcasted_iota(jnp.int32, (order, order), 1)
     pick = ((x & 3) * levels + (x >> 2) == o).astype(F32).astype(BF16)
+    main = (x & 3) * levels + block * (x >> 5) + ((x >> 2) & 7)
+    last = (x & 3) * levels + block * ((x - 256) >> 2) + block - 1
+    put = (jnp.where(x < 256, main, last) == o).astype(F32).astype(BF16)
     part = order // 4
     for n, ref in enumerate((m_ref, n_ref)):
         hi, lo = split(ref[...])
         rest = (ref[...] - hi.astype(F32) - lo.astype(F32)).astype(BF16)
         out = None
         for piece in (hi, lo, rest):
-            term = dot(dot(pick, piece).astype(BF16), pick, NT)
+            term = dot(dot(put, piece).astype(BF16), pick, NT)
             out = term if out is None else out + term
         o_ref[n, 0:order] = out[:, 0:128]
         o_ref[n, order : 2 * order] = out[:, 128:256]
@@ -225,46 +234,20 @@
     return jnp.concatenate([packed[: 4 * part], packed[4 * part : 8 * part], third], axis=1)
 
 
-def unselect(rest, v_ref, slot_ref, d_ref):
-    lane = lax.broadcasted_iota(jnp.int32, (128, 512), 1)
-    live = (lane & 3) < 3
-    turned = [jnp.where(live, v_ref[j].reshape(512, 128).T, 0.0) for j in range(9)]
-    turned = jnp.concatenate(turned, axis=0)
-    whole = []
+def turned_tile(v_ref, j):
+    live = (lax.broadcasted_iota(jnp.int32, (128, 512), 1) & 3) < 3
+    return jnp.where(live, v_ref[j].reshape(512, 128).T, 0.0)
+
+
+def unselect(lon, g, tile, last, slot_ref, o_ref):
     for r in range(4):
-        hi, lo = split(turned[288 * r : 288 * r + 288])
-        one = selector(slot_ref, r)
-        whole.append(dot(jnp.concatenate([hi, lo], axis=1), jnp.concatenate([one, one], axis=0)))
-    sub = lax.broadcasted_iota(jnp.int32, (8, 256), 0) < 4
-    lane = lax.broadcasted_iota(jnp.int32, (8, 128), 1)
-    block = d_ref.shape[1]
-    for n in range(d_ref.shape[0] * block // 2):
-        even, odd = [], []
-        for rp in range(2):
-            x = whole[2 * rp][8 * n : 8 * n + 8]
-            y = whole[2 * rp + 1][8 * n : 8 * n + 8]
-            even.append(jnp.where(sub, x, pltpu.roll(y, 4, 0)))
-            odd.append(jnp.where(sub, pltpu.roll(x, 4, 0), y))
-        for i, (a, b) in enumerate((even, odd)):
-            third = jnp.where(lane < rest, a[:, 128:], pltpu.roll(b[:, 128:], rest, 1))
-            d_ref[(2 * n + i) // block, (2 * n + i) % block] = jnp.concatenate([a[:, :128], b[:, :128], third], axis=1)
-
-
-def assemble(lon, d_ref, o_ref):
-    groups = d_ref.shape[0]
-    rest = lon - 128
-
-    def level(k, carry):
-        for rp in range(2):
-            parts = []
-            for g in range(groups):
-                x = d_ref[g, k]
-                parts.append(x[:, 128 * rp : 128 * rp + 128])
-                parts.append(x[:, 256 + rest * rp : 256 + rest * rp + rest])
-            o_ref[rp, k] = jnp.concatenate(parts, axis=1)
-        return carry
-
-    lax.fori_loop(0, d_ref.shape[1], level, 0)
+        rows = jnp.concatenate([tile[32 * r : 32 * r + 32], last[16 * g : 16 * g + 16]], axis=0)
+        hi, lo = split(rows)
+        one = selector(slot_ref[g, r : r + 1, :])
+        out = dot(jnp.concatenate([hi, lo], axis=1), jnp.concatenate([one, one], axis=0))
+        at = slice(lon * g, lon * g + lon)
+        o_ref[r, 0:8, :, at] = out[0:32, :lon].reshape(8, 4, lon)
+        o_ref[r, 8, :, at] = out[32 + 4 * r : 36 + 4 * r, :lon]
 
 
 CHUNKS = 4
@@ -289,12 +272,21 @@
 
 def forth_kernel(
     rest, levs, tr_ref, south_ref, north_ref, zon_ref, mer_ref, c_ref, slot_ref,
-    r_ref, g_ref, col_ref, p_ref, a_ref, s1, r1, s2, r2, lsem,
+    r_ref, all_ref, g_ref, col_ref, p_ref, a_ref, s1, r1, s2, r2, s3, r3, lsem,
 ):
     lat, lev = lax.axis_index("lat"), lax.axis_index("lev")
     block = tr_ref.shape[1]
     greet(lat, lev, levs)
     greeted(levs)
+
+    def slot_copy(i):
+        to = lax.rem(lev + i, levs)
+        return send(slot_ref, all_ref.at[lev], s3.at[i], r3.at[i], lat, to)
+
+    for i in range(1, levs):
+        slot_copy(i).start()
+    own_slots = pltpu.make_async_copy(slot_ref, all_ref.at[lev], lsem.at[2])
+    own_slots.start()
 
     def level_copy(k, i):
         to = lax.rem(lev + i, levs)
@@ -332,20 +324,22 @@
     for r in range(4):
         for i in range(1, levs):
             row_copy(r, i).wait()
+    own_slots.wait()
+    for i in range(1, levs):
+        slot_copy(i).wait()
 
 
 def back_kernel(
     rest, levs, order, r_ref, n0, n1, n2, n3, f0, f1, f2, f3, slot_ref,
-    o_ref, y_ref, v_ref, w_ref, d_ref, own_ref, s1, r1, s2, r2, lsem,
+    o_ref, y_ref, v_ref, w_ref, z_ref, s1, r1, lsem,
 ):
     lat, lev = lax.axis_index("lat"), lax.axis_index("lev")
     size = r_ref.shape[1] // CHUNKS
     greet(lat, lev, levs)
 
-    def back_copy(d, i):
+    def back_copy(j, i):
         to = lax.rem(lev + i, levs)
-        part = pl.ds(lax.rem(lat // 4 - d + 4, 4) * size, size)
-        return send(y_ref.at[:, part, to, 0:3], v_ref.at[:, lev, part, 0:3], s1.at[d, i], r1.at[d, i], lat, to)
+        return send(y_ref.at[j, :, to, 0:3], v_ref.at[j, lev, :, 0:3], s1.at[j, i], r1.at[j, i], lat, to)
 
     def mix(n, at):
         tiles = [r_ref[j, n].reshape(4 * levs, 128) for j in range(9)]
@@ -358,19 +352,19 @@
         hi, lo = split(jnp.concatenate(rows, axis=0))
         y = dot(hi, w_ref[0, at], NT) + dot(lo, w_ref[0, at], NT) + dot(hi, w_ref[1, at], NT)
         many = 4 * levs
-        carried = None
-        for r in range(4):
-            x = jnp.concatenate([y[r * many : (r + 1) * many], jnp.zeros((many, 384 - order), F32)], axis=1)
-            if r > 0:
-                x = pltpu.roll(x, 32 * r, 1)
-            for t in range(3):
-                part = x[:, 128 * t : 128 * t + 128]
-                if t == 0 and r > 0:
-                    part = part + carried
-                if t == 2 and r < 3:
-                    carried = part
-                    continue
-                y_ref[2 * r + t, n] = part.reshape(levs, 4, 128)
+        quarter = lax.broadcasted_iota(jnp.int32, (many, 128), 1) >> 5
+        for half in range(2):
+            turns = []
+            for r in range(4):
+                tile = y[r * many : (r + 1) * many, 128 * half : 128 * half + 128]
+                turns.append([tile] + [pltpu.roll(tile, 32 * m, 1) for m in range(1, 4)])
+            for m in range(4):
+                x = turns[3][(3 - m) % 4]
+                for r in range(3):
+                    x = jnp.where(quarter == r, turns[r][(r - m) % 4], x)
+                y_ref[pl.ds(0, 8), n, 4 * half + m] = x.reshape(8, 4, 128)
+        z = jnp.concatenate([y[r * many : (r + 1) * many, 256:] for r in range(4)], axis=1)
+        z_ref[:, n] = z.reshape(8, 4, 128)
 
     for d, refs in enumerate(((n0, f0), (n1, f1), (n2, f2), (n3, f3))):
         base = lax.rem(lat // 4 - d + 4, 4) * size
@@ -383,39 +377,45 @@
         def _(at):
             mix(base + lax.rem(lat // 2 + at // 2, 2) * 2 + lax.rem(lat + at, 2), at)
 
-        if d == 0:
-            greeted(levs)
-        for i in range(1, levs):
-            back_copy(d, i).start()
+    lats = r_ref.shape[1]
+    to_lane = lax.broadcasted_iota(jnp.int32, (256, 1024), 1)
+    from_lane = lax.broadcasted_iota(jnp.int32, (256, 1024), 0) & 127
+    wanted = ((to_lane >> 2) & 3) * 32 + (to_lane >> 7) * 4 + (to_lane & 3)
+    move = (from_lane == wanted).astype(F32).astype(BF16)
+    hi, lo = split(z_ref[...].reshape(8 * 4 * lats, 128))
+    moved = dot(jnp.concatenate([hi, lo], axis=1), move)
+    group = (lax.broadcasted_iota(jnp.int32, (4 * lats, 1024), 1) >> 4) & 7
+    x = moved[: 4 * lats]
+    for g in range(1, 8):
+        x = jnp.where(group == g, moved[4 * lats * g : 4 * lats * (g + 1)], x)
+    for l in range(8):
+        y_ref[8, :, l] = x[:, 128 * l : 128 * l + 128].reshape(lats, 4, 128)
+
     own = pltpu.make_async_copy(y_ref.at[:, :, lev, 0:3], v_ref.at[:, lev, :, 0:3], lsem.at[0])
     own.start()
+    greeted(levs)
+    arrivals = [8] + list(range(8))
+    for j in arrivals:
+        for i in range(1, levs):
+            back_copy(j, i).start()
     own.wait()
-    for q in range(CHUNKS):
+    last = None
+    for j in arrivals:
         for i in range(1, levs):
-            back_copy(q, i).wait()
-
-    unselect(rest, v_ref, slot_ref, d_ref)
-
-    def level_copy(i):
-        to = lax.rem(lev + i, levs)
-        return send(d_ref.at[to], own_ref.at[lev], s2.at[i], r2.at[i], lat, to)
-
-    for i in range(1, levs):
-        level_copy(i).start()
-    own = pltpu.make_async_copy(d_ref.at[lev], own_ref.at[lev], lsem.at[1])
-    own.start()
-    own.wait()
-    for i in range(1, levs):
-        level_copy(i).wait()
-    assemble(128 + rest, own_ref, o_ref)
-
-
-def call(kernel, shape, count, scratch=(), limit=48, **params):
+            back_copy(j, i).wait()
+        tile = turned_tile(v_ref, j)
+        if j == 8:
+            last = tile
+        else:
+            unselect(128 + rest, j, tile, last, slot_ref, o_ref)
+
+
+def call(kernel, shape, count, scratch=(), limit=48, extra=None, **params):
     return pl.pallas_call(
         kernel,
-        out_shape=jax.ShapeDtypeStruct(shape, F32),
+        out_shape=jax.ShapeDtypeStruct(shape, F32) if extra is None else (jax.ShapeDtypeStruct(shape, F32), extra),
         in_specs=[VMEM] * count,
-        out_specs=VMEM,
+        out_specs=VMEM if extra is None else (VMEM, VMEM),
         scratch_shapes=list(scratch),
         compiler_params=pltpu.CompilerParams(vmem_limit_bytes=limit << 20, **params),
     )
@@ -437,25 +437,20 @@
     north = lax.ppermute(
         jnp.concatenate([turned[:3].reshape(3 * levs_here, trac, width), edge], axis=0), "lat", down
     )
-    pair = call(reorder_kernel, (2, order * order // 128, 128), 2)(own, across)
+    pair = call(functools.partial(reorder_kernel, groups), (2, order * order // 128, 128), 2)(own, across)
     targets = route[:, :, 0]
     before = jnp.arange(lon)[:, None] < jnp.arange(lon)[None, :]
     same = jnp.logical_and(targets[:, :, None] == targets[:, None, :], before[None])
     place = (targets % groups) * lats + targets // groups
     slots = place * 4 + jnp.sum(same.astype(jnp.int32), axis=1)
     slots = jnp.pad(slots, ((0, 0), (0, 256 - lon)), constant_values=-1)
-    v = vertical.reshape(levels, 2, 2, lon)
-    courant = jnp.concatenate(
-        [v[:, 0, :, :128], v[:, 1, :, :128], v[:, 0, :, 128:], v[:, 1, :, 128:], jnp.zeros((levels, 2, 128 - 2 * rest), F32)],
-        axis=-1,
-    )
     shifted = [lax.ppermute(pair, "lat", [(i, (i + 4 * d) % lats) for i in range(lats)]) for d in range(1, 4)]
     other = [(i, i ^ 1) for i in range(lats)]
     far = [lax.ppermute(pair, "lat", other)]
     south, north, pair = lax.optimization_barrier((south, north, pair))
     dma = pltpu.SemaphoreType.DMA
     levels_of = pltpu.VMEM((groups, levs_here, 8, 384), F32)
-    received = call(
+    received, all_slots = call(
         functools.partial(forth_kernel, rest, groups),
         (9, lats, groups, 4, 128),
         7,
@@ -468,34 +463,33 @@
             dma((levs_here, groups)),
             dma((4, groups)),
             dma((4, groups)),
-            dma((2,)),
+            dma((groups,)),
+            dma((groups,)),
+            dma((3,)),
         ],
+        extra=jax.ShapeDtypeStruct((groups, 4, 256), jnp.int32),
         collective_id=0,
         has_side_effects=True,
-    )(turned, south, north, zonal, meridional, courant, slots)
+    )(turned, south, north, zonal, meridional, vertical, slots)
     received, shifted = lax.optimization_barrier((received, shifted))
     far += [lax.ppermute(x, "lat", other) for x in shifted]
     whole = call(
         functools.partial(back_kernel, rest, groups, order),
-        (2, levs_here, 8, width),
+        (4, levs_here, trac, width),
         10,
         [
             pltpu.VMEM((9, lats, groups, 4, 128), F32),
             pltpu.VMEM((9, groups, lats, 4, 128), F32),
             pltpu.VMEM((2, lats // CHUNKS, order, order), BF16),
-            levels_of,
-            levels_of,
-            dma((CHUNKS, groups)),
-            dma((CHUNKS, groups)),
-            dma((groups,)),
-            dma((groups,)),
-            dma((2,)),
+            pltpu.VMEM((groups, lats, 4, 128), F32),
+            dma((9, groups)),
+            dma((9, groups)),
+            dma((1,)),
         ],
         collective_id=1,
         has_side_effects=True,
-    )(received, pair, *shifted, *far, slots)
-    whole = whole.reshape(2, levs_here, 2, trac, width)
-    return jnp.transpose(whole, (3, 1, 0, 2, 4)).reshape(tracers.shape) - tracers
+    )(received, pair, *shifted, *far, all_slots)
+    return jnp.transpose(whole, (2, 1, 0, 3)) - tracers
 
 
 def solution(mesh):

time: 126 us -> 155 us (1.23); the launches traced: 124 us -> 155 us
  waiting for transfers between devices: 7.72 us -> 46.4 us
  local copies, waits for them, and re-layouts: 13.2 us -> 7.27 us
  Pallas kernels: 83.9 us -> 80 us
  starting transfers between devices: 16.6 us -> 19.6 us
    ppermute x1, waiting for transfers between devices: 0.01 us -> 37.9 us  [body(): south = lax.ppermute(turned[rows - 3:], 'lat', up)]
    ppermute x3, starting transfers between devices: 3.93 us -> 11.2 us  [body(): lax.ppermute(pair, 'lat', [(i, (i + 4 * d) % lats) for i in range(lats)])]
    ppermute x1, starting transfers between devices: 6.16 us -> 1.91 us  [body(): lax.ppermute(jnp.concatenate([turned[:3].reshape(3 * levs_here, trac, wid...]
    unnamed x20 -> x17, local copies, waits for them, and re-layouts: 7.74 us -> 4.85 us
    pallas_call x2, Pallas kernels: 42.9 us -> 40.4 us  [the longest x1 38.3 us: body(): call(functools.partial(back_kernel, rest, groups, order), (4, levs_here,...]
  transfers between devices with their start and end apart: 10 -> 10, of which waited for: 4 -> 5; matrix products, arithmetic and copies ran while one was open for 6% -> 3% of each run, Pallas kernels for 35% -> 27%
where the time goes in v4:
time: 155 us
  Pallas kernels  80 us (52%)
  waiting for transfers between devices  46.4 us (30%)
  starting transfers between devices  19.6 us (13%)
  local copies, waits for them, and re-layouts  7.27 us (5%)
  other arithmetic  1.88 us (1%)
    pallas_call x1, Pallas kernels, body(): call(functools.partial(forth_kernel, rest, groups), (9, lats, groups, 4,...  39.6 us
    pallas_call x1, Pallas kernels, body(): call(functools.partial(back_kernel, rest, groups, order), (4, levs_here,...  38.3 us
    ppermute x1, waiting for transfers between devices, body(): south = lax.ppermute(turned[rows - 3:], 'lat', up)  37.9 us
    ppermute x3, starting transfers between devices, body(): lax.ppermute(pair, 'lat', [(i, (i + 4 * d) % lats) for i in range(lats)])  11.2 us
    unnamed x17, local copies, waits for them, and re-layouts  4.85 us
    ppermute x1, waiting for transfers between devices, body(): across = lax.ppermute(own, 'lat', [(i, i ^ 2) for i in range(lats)])  4.83 us
    ppermute x1, starting transfers between devices, body(): across = lax.ppermute(own, 'lat', [(i, i ^ 2) for i in range(lats)])  3.88 us
    ppermute x3, waiting for transfers between devices, body(): far += [lax.ppermute(x, 'lat', other) for x in shifted]  3.61 us
  transfers between devices with their start and end apart: 10, of which 5 were waited for; matrix products, arithmetic and copies ran while one was open for 3% of the time, Pallas kernels for 27%

profile of v4, /device:TPU:24, one launch (start us, length us, event | category | flops | bytes accessed | tf_op | source)
XLA Modules:
  0.0 155.2 jit_solution(13978816782446555839)
XLA Ops:
  0.0 0.0 slice-start
  0.0 3.9 %collective-permute-start.2 = (f32[288,288]{1,0:T(8,128)}, f32[288,288]{1,0:T(8,128)S(1)}, u32[]{:S(2)}, u32[]{:S(2)}) collective-permute-start(f32[288,288]{1,0:T(8,128)} %bitcast.17), channel_id=1, source_target_pairs={{0,16},{8,24},{16,0},{24,8},{32,48},{40,56},{48,32},{56,40},{64,80... | collective-permute-start | bytes 995336 | tf_op jit(solution)/shard_map/ppermute | solution.py:431
  3.9 1.5 copy.27
  5.4 0.0 copy-start.1
  5.4 1.0 fusion.6
  6.4 0.0 copy-start.6
  6.4 0.0 copy-start.2
  6.4 0.0 slice-done
  6.5 1.0 pad_maximum_fusion
  7.5 1.9 %collective-permute-start.1 = (f32[30,4,1440]{2,1,0:T(4,128)}, f32[30,4,1440]{2,1,0:T(4,128)S(1)}, u32[]{:S(2)}, u32[]{:S(2)}) collective-permute-start(f32[30,4,1440]{2,1,0:T(4,128)} %pad_maximum_fusion), channel_id=1, source_target_pairs={{8,0},{16,8},{24,16},{32,24},{40,32},{48,40},{56,48},{64,56},{72,6... | collective-permute-start | bytes 2073608 | tf_op jit(solution)/shard_map/ppermute | solution.py:437
  9.4 4.8 %collective-permute-done.2.n_ref = f32[288,288]{1,0:T(8,128)S(1)} collective-permute-done((f32[288,288]{1,0:T(8,128)}, f32[288,288]{1,0:T(8,128)S(1)}, u32[]{:S(2)}, u32[]{:S(2)}) %collective-permute-start.2) | collective-permute-done | bytes 331808 | tf_op jit(solution)/shard_map/ppermute | solution.py:431
  14.3 0.0 copy-done.1
  14.3 2.1 %shard_map.64.n0 = f32[2,648,128]{2,1,0:T(8,128)S(1)} custom-call(f32[288,288]{1,0:T(8,128)S(1)} %bitcast.18, f32[288,288]{1,0:T(8,128)S(1)} %collective-permute-done.2.n_ref), custom_call_target="tpu_custom_call" | custom-call | tf_op jit(solution)/shard_map/pallas_call | solution.py:440
  16.3 8.1 %collective-permute-start.5 = (f32[2,648,128]{2,1,0:T(8,128)S(1)}, f32[2,648,128]{2,1,0:T(8,128)}, u32[]{:S(2)}, u32[]{:S(2)}) collective-permute-start(f32[2,648,128]{2,1,0:T(8,128)S(1)} %shard_map.64.n0), channel_id=1, source_target_pairs={{0,96},{8,104},{16,112},{24,120},{32,0},{40,8},{48,16},{56,24},{64... | collective-permute-start | bytes 1990664 | tf_op jit(solution)/shard_map/ppermute | solution.py:447
  24.4 0.9 collective-permute-start.4
  25.4 2.2 %collective-permute-start.3 = (f32[2,648,128]{2,1,0:T(8,128)S(1)}, f32[2,648,128]{2,1,0:T(8,128)}, u32[]{:S(2)}, u32[]{:S(2)}) collective-permute-start(f32[2,648,128]{2,1,0:T(8,128)S(1)} %shard_map.64.n0), channel_id=1, source_target_pairs={{0,32},{8,40},{16,48},{24,56},{32,64},{40,72},{48,80},{56,88},{64,... | collective-permute-start | bytes 1990664 | tf_op jit(solution)/shard_map/ppermute | solution.py:447
  27.5 1.9 %collective-permute-start = (f32[3,9,4,1440]{3,2,1,0:T(4,128)}, f32[3,9,4,1440]{3,2,1,0:T(4,128)S(1)}, u32[]{:S(2)}, u32[]{:S(2)}) collective-permute-start(f32[3,9,4,1440]{3,2,1,0:T(4,128)} %get-tuple-element.24), channel_id=1, source_target_pairs={{0,8},{8,16},{16,24},{24,32},{32,40},{40,48},{48,56},{56,64},{64,7... | collective-permute-start | bytes 1866248 | tf_op jit(solution)/shard_map/ppermute | solution.py:435
  29.4 0.0 copy-done.6
  29.5 0.1 copy.16
  29.6 0.4 convert_reduce_fusion
  30.0 37.9 %collective-permute-done.south_ref = f32[3,9,4,1440]{3,2,1,0:T(4,128)S(1)} collective-permute-done((f32[3,9,4,1440]{3,2,1,0:T(4,128)}, f32[3,9,4,1440]{3,2,1,0:T(4,128)S(1)}, u32[]{:S(2)}, u32[]{:S(2)}) %collective-permute-start) | collective-permute-done | bytes 622112 | tf_op jit(solution)/shard_map/ppermute | solution.py:435
  67.9 0.0 collective-permute-start.6
  68.0 0.0 collective-permute-done.1.north_ref
  68.0 0.0 copy-done.2
  68.0 0.0 copy-start.3
  68.0 1.0 copy-done.3
  68.9 0.0 copy-start.4
  68.9 0.9 copy-done.4
  69.9 39.6 %shard_map.65 = (f32[9,16,8,4,128]{4,3,2,1,0:T(4,128)S(1)}, s32[8,4,256]{2,1,0:T(4,128)S(1)}) custom-call(f32[4,9,4,1440]{3,2,1,0:T(4,128)S(1)} %bitcast.16, f32[3,9,4,1440]{3,2,1,0:T(4,128)S(1)} %collective-permute-done.south_ref, f32[30,4,1440]{2,1,0:T(4,128)S(1)} %collective-permute-done.1.north_ref, f32[9,4,1440]{2,1,0:T(4,128)S(1)} %copy-done.4, ...), custom_call_target="tpu_custom_call" | custom-call | tf_op jit(solution)/shard_map/pallas_call | solution.py:453
  109.5 0.0 copy-start
  109.5 1.4 copy-done
  110.9 0.0 collective-permute-done.5.n3
  110.9 0.0 collective-permute-done.4.n2
  110.9 0.0 collective-permute-done.3.n1
  110.9 0.1 collective-permute-start.7
  111.0 0.5 collective-permute-start.8
  111.5 0.1 collective-permute-start.9
  111.6 0.0 collective-permute-done.6.f0
  111.6 1.7 %collective-permute-done.7.f1 = f32[2,648,128]{2,1,0:T(8,128)S(1)} collective-permute-done((f32[2,648,128]{2,1,0:T(8,128)}, f32[2,648,128]{2,1,0:T(8,128)S(1)}, u32[]{:S(2)}, u32[]{:S(2)}) %collective-permute-start.7) | collective-permute-done | bytes 663584 | tf_op jit(solution)/shard_map/ppermute | solution.py:475
  113.3 0.9 collective-permute-done.8.f2
  114.3 0.9 collective-permute-done.9.f3
  115.2 0.0 copy-start.5
  115.2 38.3 %shard_map.66 = f32[4,9,4,1440]{3,2,1,0:T(4,128)S(1)} custom-call(f32[9,16,8,4,128]{4,3,2,1,0:T(4,128)} %copy-done, f32[2,648,128]{2,1,0:T(8,128)S(1)} %shard_map.64.n0, f32[2,648,128]{2,1,0:T(8,128)} %collective-permute-done.3.n1, f32[2,648,128]{2,1,0:T(8,128)} %collective-permute-done.4.n2, f32[2,648,128]{2,1,0:T(8,128)} %collective-permute-done.5.n3, ...), custom_call_target="tpu_custom_call" | custom-call | tf_op jit(solution)/shard_map/pallas_call | solution.py:476
  153.5 0.0 copy-done.5
  153.5 0.4 bitcast_subtract_fusion
  154.0 1.3 copy.18
  (7 shorter events, 0.1 us)
Async XLA Ops:
  0.0 6.4 %slice-start = ((f32[9,4,1440]{2,1,0:T(4,128)}), f32[9,1,1440]{2,1,0:T(1,128)S(1)}, s32[]{:S(2)}) async-start(f32[9,4,1440]{2,1,0:T(4,128)} %mer_ref.1), calls=%async_computation | async-start | bytes 110592 | tf_op jit(solution)/shard_map/slice | solution.py:436
  0.0 14.3 %collective-permute-start.2 = (f32[288,288]{1,0:T(8,128)}, f32[288,288]{1,0:T(8,128)S(1)}, u32[]{:S(2)}, u32[]{:S(2)}) collective-permute-start(f32[288,288]{1,0:T(8,128)} %bitcast.17), channel_id=1, source_target_pairs={{0,16},{8,24},{16,0},{24,8},{32,48},{40,56},{48,32},{56,40},{64,80... | collective-permute-start | bytes 995336 | tf_op jit(solution)/shard_map/ppermute | solution.py:431
  5.4 8.9 %copy-start.1 = (f32[1,1,288,288]{3,2,1,0:T(8,128)S(1)}, f32[1,1,288,288]{3,2,1,0:T(8,128)}, u32[]{:S(2)}) copy-start(f32[1,1,288,288]{3,2,1,0:T(8,128)} %param.11) | copy-start | bytes 995332
  6.4 23.0 %copy-start.6 = (s32[4,180,1]{1,2,0:T(1,128)S(1)}, s32[4,180,1]{1,2,0:T(1,128)}, u32[]{:S(2)}) copy-start(s32[4,180,1]{1,2,0:T(1,128)} %param.10) | copy-start | bytes 8644
  6.4 61.5 %copy-start.2 = (f32[9,4,1440]{2,1,0:T(4,128)S(1)}, f32[9,4,1440]{2,1,0:T(4,128)}, u32[]{:S(2)}) copy-start(f32[9,4,1440]{2,1,0:T(4,128)} %mer_ref.1) | copy-start | bytes 622084
  7.5 60.5 %collective-permute-start.1 = (f32[30,4,1440]{2,1,0:T(4,128)}, f32[30,4,1440]{2,1,0:T(4,128)S(1)}, u32[]{:S(2)}, u32[]{:S(2)}) collective-permute-start(f32[30,4,1440]{2,1,0:T(4,128)} %pad_maximum_fusion), channel_id=1, source_target_pairs={{8,0},{16,8},{24,16},{32,24},{40,32},{48,40},{56,48},{64,56},{72,6... | collective-permute-start | bytes 2073608 | tf_op jit(solution)/shard_map/ppermute | solution.py:437
  16.3 94.6 %collective-permute-start.5 = (f32[2,648,128]{2,1,0:T(8,128)S(1)}, f32[2,648,128]{2,1,0:T(8,128)}, u32[]{:S(2)}, u32[]{:S(2)}) collective-permute-start(f32[2,648,128]{2,1,0:T(8,128)S(1)} %shard_map.64.n0), channel_id=1, source_target_pairs={{0,96},{8,104},{16,112},{24,120},{32,0},{40,8},{48,16},{56,24},{64... | collective-permute-start | bytes 1990664 | tf_op jit(solution)/shard_map/ppermute | solution.py:447
  24.4 86.5 %collective-permute-start.4 = (f32[2,648,128]{2,1,0:T(8,128)S(1)}, f32[2,648,128]{2,1,0:T(8,128)}, u32[]{:S(2)}, u32[]{:S(2)}) collective-permute-start(f32[2,648,128]{2,1,0:T(8,128)S(1)} %shard_map.64.n0), channel_id=1, source_target_pairs={{0,64},{8,72},{16,80},{24,88},{32,96},{40,104},{48,112},{56,120},{... | collective-permute-start | bytes 1990664 | tf_op jit(solution)/shard_map/ppermute | solution.py:447
  25.4 85.6 %collective-permute-start.3 = (f32[2,648,128]{2,1,0:T(8,128)S(1)}, f32[2,648,128]{2,1,0:T(8,128)}, u32[]{:S(2)}, u32[]{:S(2)}) collective-permute-start(f32[2,648,128]{2,1,0:T(8,128)S(1)} %shard_map.64.n0), channel_id=1, source_target_pairs={{0,32},{8,40},{16,48},{24,56},{32,64},{40,72},{48,80},{56,88},{64,... | collective-permute-start | bytes 1990664 | tf_op jit(solution)/shard_map/ppermute | solution.py:447
  27.5 40.4 %collective-permute-start = (f32[3,9,4,1440]{3,2,1,0:T(4,128)}, f32[3,9,4,1440]{3,2,1,0:T(4,128)S(1)}, u32[]{:S(2)}, u32[]{:S(2)}) collective-permute-start(f32[3,9,4,1440]{3,2,1,0:T(4,128)} %get-tuple-element.24), channel_id=1, source_target_pairs={{0,8},{8,16},{16,24},{24,32},{32,40},{40,48},{48,56},{56,64},{64,7... | collective-permute-start | bytes 1866248 | tf_op jit(solution)/shard_map/ppermute | solution.py:435
  67.9 43.7 %collective-permute-start.6 = (f32[2,648,128]{2,1,0:T(8,128)S(1)}, f32[2,648,128]{2,1,0:T(8,128)S(1)}, u32[]{:S(2)}, u32[]{:S(2)}) collective-permute-start(f32[2,648,128]{2,1,0:T(8,128)S(1)} %shard_map.64.n0), channel_id=1, source_target_pairs={{0,8},{8,0},{16,24},{24,16},{32,40},{40,32},{48,56},{56,48},{64,72... | collective-permute-start | bytes 1990664 | tf_op jit(solution)/shard_map/ppermute | solution.py:449
  68.0 1.0 copy-start.3
  68.9 0.9 copy-start.4
  109.5 1.4 copy-start
  110.9 2.4 %collective-permute-start.7 = (f32[2,648,128]{2,1,0:T(8,128)}, f32[2,648,128]{2,1,0:T(8,128)S(1)}, u32[]{:S(2)}, u32[]{:S(2)}) collective-permute-start(f32[2,648,128]{2,1,0:T(8,128)} %collective-permute-done.3.n1), channel_id=1, source_target_pairs={{0,8},{8,0},{16,24},{24,16},{32,40},{40,32},{48,56},{56,48},{64,72... | collective-permute-start | bytes 1990664 | tf_op jit(solution)/shard_map/ppermute | solution.py:475
  111.0 3.3 %collective-permute-start.8 = (f32[2,648,128]{2,1,0:T(8,128)}, f32[2,648,128]{2,1,0:T(8,128)S(1)}, u32[]{:S(2)}, u32[]{:S(2)}) collective-permute-start(f32[2,648,128]{2,1,0:T(8,128)} %collective-permute-done.4.n2), channel_id=1, source_target_pairs={{0,8},{8,0},{16,24},{24,16},{32,40},{40,32},{48,56},{56,48},{64,72... | collective-permute-start | bytes 1990664 | tf_op jit(solution)/shard_map/ppermute | solution.py:475
  111.5 3.7 %collective-permute-start.9 = (f32[2,648,128]{2,1,0:T(8,128)}, f32[2,648,128]{2,1,0:T(8,128)S(1)}, u32[]{:S(2)}, u32[]{:S(2)}) collective-permute-start(f32[2,648,128]{2,1,0:T(8,128)} %collective-permute-done.5.n3), channel_id=1, source_target_pairs={{0,8},{8,0},{16,24},{24,16},{32,40},{40,32},{48,56},{56,48},{64,72... | collective-permute-start | bytes 1990664 | tf_op jit(solution)/shard_map/ppermute | solution.py:475
  115.2 38.3 %copy-start.5 = (f32[4,9,4,1440]{3,2,1,0:T(4,128)S(1)}, f32[4,9,4,1440]{3,2,1,0:T(4,128)}, u32[]{:S(2)}) copy-start(f32[4,9,4,1440]{3,2,1,0:T(4,128)} %param.6) | copy-start | bytes 2488324

commit v5 on v4

--- a/solution.py
+++ b/solution.py
@@ -158,12 +158,7 @@
         if k + 1 < levels:
             nxt = e_at(k + 2)
             s1, k1 = nxt - right, 6.0 * q(k + 1) - 3.0 * (right + nxt)
-            v = c_ref[k + 1]
-            c0 = jnp.where(sub[:, : 128 + rest], v[0:1], v[1:2])
-            c1 = jnp.where(sub[:, : 128 + rest], v[2:3], v[3:4])
-            c = jnp.concatenate(
-                [c0[:, :128], c1[:, :128], c0[:, 128:], c1[:, 128:], zero[:, : 128 - 2 * rest]], axis=1
-            )
+            c = jnp.where(sub, c_ref[k + 1, 0:1, :], c_ref[k + 1, 1:2, :])
             f_next = flux(c, right, s, s1, kk, k1)
             right, s, kk = nxt, s1, k1
         else:
@@ -331,15 +326,49 @@
 
 def back_kernel(
     rest, levs, order, r_ref, n0, n1, n2, n3, f0, f1, f2, f3, slot_ref,
-    o_ref, y_ref, v_ref, w_ref, z_ref, s1, r1, lsem,
+    o_ref, y_ref, v_ref, w_ref, z_ref, m_ref, move_ref, s1, r1, s2, r2, lsem, msem,
 ):
     lat, lev = lax.axis_index("lat"), lax.axis_index("lev")
     size = r_ref.shape[1] // CHUNKS
     greet(lat, lev, levs)
 
-    def back_copy(j, i):
+    fetches = []
+    for n, ref in enumerate((n0, f0, n1, f1, n2, f2, n3, f3)):
+        fetches.append(pltpu.make_async_copy(ref, m_ref.at[n], msem.at[n]))
+        fetches[n].start()
+
+    def base(d):
+        return lax.rem(lat // 4 - d + 4, 4) * size
+
+    def chunk_copy(d, i):
         to = lax.rem(lev + i, levs)
-        return send(y_ref.at[j, :, to, 0:3], v_ref.at[j, lev, :, 0:3], s1.at[j, i], r1.at[j, i], lat, to)
+        part = pl.ds(base(d), size)
+        return send(y_ref.at[:, part, to, 0:3], v_ref.at[:, lev, part, 0:3], s1.at[d, i], r1.at[d, i], lat, to)
+
+    def tile_copy(j, i):
+        to = lax.rem(lev + i, levs)
+        part = pl.ds(base(CHUNKS - 1), size)
+        return send(y_ref.at[j, part, to, 0:3], v_ref.at[j, lev, part, 0:3], s2.at[j, i], r2.at[j, i], lat, to)
+
+    def own_copy(d):
+        part = pl.ds(base(d), size)
+        return pltpu.make_async_copy(y_ref.at[:, part, lev, 0:3], v_ref.at[:, lev, part, 0:3], lsem.at[d])
+
+    to_lane = lax.broadcasted_iota(jnp.int32, (256, 1024), 1)
+    from_lane = lax.broadcasted_iota(jnp.int32, (256, 1024), 0) & 127
+    wanted = ((to_lane >> 2) & 3) * 32 + (to_lane >> 7) * 4 + (to_lane & 3)
+    move_ref[...] = (from_lane == wanted).astype(F32).astype(BF16)
+
+    def place_last(d):
+        many = 4 * size
+        hi, lo = split(z_ref[:, pl.ds(base(d), size)].reshape(8 * many, 128))
+        moved = dot(jnp.concatenate([hi, lo], axis=1), move_ref[...])
+        group = (lax.broadcasted_iota(jnp.int32, (many, 1024), 1) >> 4) & 7
+        x = moved[:many]
+        for g in range(1, 8):
+            x = jnp.where(group == g, moved[many * g : many * (g + 1)], x)
+        for l in range(8):
+            y_ref[8, pl.ds(base(d), size), l] = x[:, 128 * l : 128 * l + 128].reshape(size, 4, 128)
 
     def mix(n, at):
         tiles = [r_ref[j, n].reshape(4 * levs, 128) for j in range(9)]
@@ -366,43 +395,40 @@
         z = jnp.concatenate([y[r * many : (r + 1) * many, 256:] for r in range(4)], axis=1)
         z_ref[:, n] = z.reshape(8, 4, 128)
 
-    for d, refs in enumerate(((n0, f0), (n1, f1), (n2, f2), (n3, f3))):
-        base = lax.rem(lat // 4 - d + 4, 4) * size
+    arrivals = [8] + list(range(8))
+    for d in range(CHUNKS):
+        fetches[2 * d].wait()
+        fetches[2 * d + 1].wait()
         for at in range(4):
-            hi, lo = split(unpacked(refs[at % 2][at // 2]))
+            hi, lo = split(unpacked(m_ref[2 * d + at % 2, at // 2]))
             w_ref[0, at] = hi
             w_ref[1, at] = lo
 
         @pl.loop(0, size)
         def _(at):
-            mix(base + lax.rem(lat // 2 + at // 2, 2) * 2 + lax.rem(lat + at, 2), at)
-
-    lats = r_ref.shape[1]
-    to_lane = lax.broadcasted_iota(jnp.int32, (256, 1024), 1)
-    from_lane = lax.broadcasted_iota(jnp.int32, (256, 1024), 0) & 127
-    wanted = ((to_lane >> 2) & 3) * 32 + (to_lane >> 7) * 4 + (to_lane & 3)
-    move = (from_lane == wanted).astype(F32).astype(BF16)
-    hi, lo = split(z_ref[...].reshape(8 * 4 * lats, 128))
-    moved = dot(jnp.concatenate([hi, lo], axis=1), move)
-    group = (lax.broadcasted_iota(jnp.int32, (4 * lats, 1024), 1) >> 4) & 7
-    x = moved[: 4 * lats]
-    for g in range(1, 8):
-        x = jnp.where(group == g, moved[4 * lats * g : 4 * lats * (g + 1)], x)
-    for l in range(8):
-        y_ref[8, :, l] = x[:, 128 * l : 128 * l + 128].reshape(lats, 4, 128)
-
-    own = pltpu.make_async_copy(y_ref.at[:, :, lev, 0:3], v_ref.at[:, lev, :, 0:3], lsem.at[0])
-    own.start()
-    greeted(levs)
-    arrivals = [8] + list(range(8))
-    for j in arrivals:
+            mix(base(d) + lax.rem(lat // 2 + at // 2, 2) * 2 + lax.rem(lat + at, 2), at)
+
+        place_last(d)
+        own_copy(d).start()
+        if d == 0:
+            greeted(levs)
+        if d < CHUNKS - 1:
+            for i in range(1, levs):
+                chunk_copy(d, i).start()
+        else:
+            for j in arrivals:
+                for i in range(1, levs):
+                    tile_copy(j, i).start()
+
+    for d in range(CHUNKS):
+        own_copy(d).wait()
+    for d in range(CHUNKS - 1):
         for i in range(1, levs):
-            back_copy(j, i).start()
-    own.wait()
+            chunk_copy(d, i).wait()
     last = None
     for j in arrivals:
         for i in range(1, levs):
-            back_copy(j, i).wait()
+            tile_copy(j, i).wait()
         tile = turned_tile(v_ref, j)
         if j == 8:
             last = tile
@@ -410,11 +436,11 @@
             unselect(128 + rest, j, tile, last, slot_ref, o_ref)
 
 
-def call(kernel, shape, count, scratch=(), limit=48, extra=None, **params):
+def call(kernel, shape, count, scratch=(), limit=48, extra=None, large=(), **params):
     return pl.pallas_call(
         kernel,
         out_shape=jax.ShapeDtypeStruct(shape, F32) if extra is None else (jax.ShapeDtypeStruct(shape, F32), extra),
-        in_specs=[VMEM] * count,
+        in_specs=[pl.BlockSpec(memory_space=pl.ANY) if n in large else VMEM for n in range(count)],
         out_specs=VMEM if extra is None else (VMEM, VMEM),
         scratch_shapes=list(scratch),
         compiler_params=pltpu.CompilerParams(vmem_limit_bytes=limit << 20, **params),
@@ -444,10 +470,13 @@
     place = (targets % groups) * lats + targets // groups
     slots = place * 4 + jnp.sum(same.astype(jnp.int32), axis=1)
     slots = jnp.pad(slots, ((0, 0), (0, 256 - lon)), constant_values=-1)
+    v = vertical.reshape(levels, 2, 2, lon)
+    courant = jnp.concatenate(
+        [v[:, 0, :, :128], v[:, 1, :, :128], v[:, 0, :, 128:], v[:, 1, :, 128:], jnp.zeros((levels, 2, 128 - 2 * rest), F32)],
+        axis=-1,
+    )
     shifted = [lax.ppermute(pair, "lat", [(i, (i + 4 * d) % lats) for i in range(lats)]) for d in range(1, 4)]
     other = [(i, i ^ 1) for i in range(lats)]
-    far = [lax.ppermute(pair, "lat", other)]
-    south, north, pair = lax.optimization_barrier((south, north, pair))
     dma = pltpu.SemaphoreType.DMA
     levels_of = pltpu.VMEM((groups, levs_here, 8, 384), F32)
     received, all_slots = call(
@@ -470,9 +499,9 @@
         extra=jax.ShapeDtypeStruct((groups, 4, 256), jnp.int32),
         collective_id=0,
         has_side_effects=True,
-    )(turned, south, north, zonal, meridional, vertical, slots)
-    received, shifted = lax.optimization_barrier((received, shifted))
-    far += [lax.ppermute(x, "lat", other) for x in shifted]
+    )(turned, south, north, zonal, meridional, courant, slots)
+    received, pair, shifted = lax.optimization_barrier((received, pair, shifted))
+    far = [lax.ppermute(x, "lat", other) for x in [pair] + shifted]
     whole = call(
         functools.partial(back_kernel, rest, groups, order),
         (4, levs_here, trac, width),
@@ -482,10 +511,16 @@
             pltpu.VMEM((9, groups, lats, 4, 128), F32),
             pltpu.VMEM((2, lats // CHUNKS, order, order), BF16),
             pltpu.VMEM((groups, lats, 4, 128), F32),
+            pltpu.VMEM((8,) + pair.shape, F32),
+            pltpu.VMEM((256, 1024), BF16),
+            dma((CHUNKS - 1, groups)),
+            dma((CHUNKS - 1, groups)),
             dma((9, groups)),
             dma((9, groups)),
-            dma((1,)),
+            dma((CHUNKS,)),
+            dma((8,)),
         ],
+        large=range(1, 9),
         collective_id=1,
         has_side_effects=True,
     )(received, pair, *shifted, *far, all_slots)

time: 155 us -> 115 us (0.74)
  the two profiles are of different devices: /device:TPU:24 before, /device:TPU:64 now
where the time goes in v5:
time: 115 us
  Pallas kernels  78 us (68%)
  starting transfers between devices  15.3 us (13%)
  local copies, waits for them, and re-layouts  12.9 us (11%)
  waiting for transfers between devices  6.42 us (6%)
  other arithmetic  1.88 us (2%)
    pallas_call x1, Pallas kernels, body(): call(functools.partial(forth_kernel, rest, groups), (9, lats, groups, 4,...  42.3 us
    pallas_call x1, Pallas kernels, body(): call(functools.partial(back_kernel, rest, groups, order), (4, levs_here,...  33.7 us
    unnamed x20, local copies, waits for them, and re-layouts  7.74 us
    ppermute x3, starting transfers between devices, body(): lax.ppermute(pair, 'lat', [(i, (i + 4 * d) % lats) for i in range(lats)])  7.08 us
    ppermute x1, starting transfers between devices, body(): lax.ppermute(jnp.concatenate([turned[:3].reshape(3 * levs_here, trac, wid...  5.27 us
    ppermute x4, waiting for transfers between devices, body(): far = [lax.ppermute(x, 'lat', other) for x in [pair] + shifted]  4.14 us
  transfers between devices with their start and end apart: 10, of which 5 were waited for; matrix products, arithmetic and copies ran while one was open for 7% of the time, Pallas kernels for 39%

profile of v5, /device:TPU:64, one launch (start us, length us, event | category | flops | bytes accessed | tf_op | source)
XLA Modules:
  0.0 114.8 jit_solution(14286758906389918147)
XLA Ops:
  0.0 0.0 slice-start
  0.0 0.0 collective-permute-start.2
  0.0 1.5 %copy.45 = f32[4,9,4,1440]{3,0,1,2:T(4,128)S(1)} copy(f32[4,9,4,1440]{3,2,1,0:T(4,128)} %param.6) | data formatting | bytes 1658880 | tf_op args[0]
  1.5 0.0 copy-start.7
  1.5 1.0 fusion.6
  2.6 1.9 %collective-permute-start = (f32[3,9,4,1440]{3,2,1,0:T(4,128)}, f32[3,9,4,1440]{3,2,1,0:T(4,128)S(1)}, u32[]{:S(2)}, u32[]{:S(2)}) collective-permute-start(f32[3,9,4,1440]{3,2,1,0:T(4,128)} %get-tuple-element.20), channel_id=1, source_target_pairs={{0,8},{8,16},{16,24},{24,32},{32,40},{40,48},{48,56},{56,64},{64,7... | collective-permute-start | bytes 1866248 | tf_op jit(solution)/shard_map/ppermute | solution.py:461
  4.5 0.0 slice-done
  4.6 1.0 pad_maximum_fusion
  5.6 0.0 copy-start.4
  5.6 5.3 %collective-permute-start.1 = (f32[30,4,1440]{2,1,0:T(4,128)}, f32[30,4,1440]{2,1,0:T(4,128)S(1)}, u32[]{:S(2)}, u32[]{:S(2)}) collective-permute-start(f32[30,4,1440]{2,1,0:T(4,128)} %pad_maximum_fusion), channel_id=1, source_target_pairs={{8,0},{16,8},{24,16},{32,24},{40,32},{48,40},{56,48},{64,56},{72,6... | collective-permute-start | bytes 2073608 | tf_op jit(solution)/shard_map/ppermute | solution.py:463
  10.9 0.0 copy-done.7
  10.9 0.1 copy.26
  11.0 0.4 convert_reduce_fusion
  11.5 1.0 copy.21
  12.5 2.3 %collective-permute-done.2.n_ref = f32[288,288]{1,0:T(8,128)S(1)} collective-permute-done((f32[288,288]{1,0:T(8,128)}, f32[288,288]{1,0:T(8,128)S(1)}, u32[]{:S(2)}, u32[]{:S(2)}) %collective-permute-start.2) | collective-permute-done | bytes 331808 | tf_op jit(solution)/shard_map/ppermute | solution.py:457
  14.8 0.8 copy-done.2
  15.6 1.0 copy-done.1
  16.6 1.0 copy-done.3
  17.6 2.1 %shard_map.65.n0 = f32[2,648,128]{2,1,0:T(8,128)S(1)} custom-call(f32[288,288]{1,0:T(8,128)S(1)} %bitcast.27, f32[288,288]{1,0:T(8,128)S(1)} %copy-done.3), custom_call_target="tpu_custom_call" | custom-call | tf_op jit(solution)/shard_map/pallas_call | solution.py:466
  19.7 5.5 %collective-permute-start.5 = (f32[2,648,128]{2,1,0:T(8,128)S(1)}, f32[2,648,128]{2,1,0:T(8,128)}, u32[]{:S(2)}, u32[]{:S(2)}) collective-permute-start(f32[2,648,128]{2,1,0:T(8,128)S(1)} %shard_map.65.n0), channel_id=1, source_target_pairs={{0,96},{8,104},{16,112},{24,120},{32,0},{40,8},{48,16},{56,24},{64... | collective-permute-start | bytes 1990664 | tf_op jit(solution)/shard_map/ppermute | solution.py:478
  25.1 0.6 collective-permute-start.4
  25.8 1.0 collective-permute-start.3
  26.7 0.7 copy_bitcast_fusion.4
  27.5 0.7 copy_bitcast_fusion.2
  28.2 1.3 %concatenate.7.c_ref = f32[72,2,384]{2,1,0:T(2,128)S(1)} concatenate(f32[72,2,128]{2,1,0:T(2,128)} %get-tuple-element.26, f32[72,2,128]{2,1,0:T(2,128)S(1)} %get-tuple-element.25, f32[72,2,52]{2,1,0:T(2,128)} %get-tuple-element.28, f32[72,2,52]{2,1,0:T(2,128)} %get-tuple-element.27, f32[72,2,24]{2,1,0:T(2,128)S(1)} %broadcast_in_dim.2), dimensions={2} | concatenate | bytes 442368 | tf_op jit(solution)/shard_map/concatenate | solution.py:474
  29.5 0.0 collective-permute-done.south_ref
  29.5 0.0 collective-permute-done.1.north_ref
  29.5 0.0 copy-done.4
  29.5 0.0 copy-start.5
  29.6 0.9 copy-done.5
  30.5 42.3 %shard_map.64 = (f32[9,16,8,4,128]{4,3,2,1,0:T(4,128)S(1)}, s32[8,4,256]{2,1,0:T(4,128)S(1)}) custom-call(f32[4,9,4,1440]{3,2,1,0:T(4,128)S(1)} %bitcast.25, f32[3,9,4,1440]{3,2,1,0:T(4,128)S(1)} %collective-permute-done.south_ref, f32[30,4,1440]{2,1,0:T(4,128)S(1)} %collective-permute-done.1.north_ref, f32[9,4,1440]{2,1,0:T(4,128)S(1)} %copy-done.5, ...), custom_call_target="tpu_custom_call" | custom-call | tf_op jit(solution)/shard_map/pallas_call | solution.py:482
  72.8 0.0 copy-start
  72.8 1.4 %copy-done = f32[9,16,8,4,128]{4,3,2,1,0:T(4,128)} copy-done((f32[9,16,8,4,128]{4,3,2,1,0:T(4,128)}, f32[9,16,8,4,128]{4,3,2,1,0:T(4,128)S(1)}, u32[]{:S(2)}) %copy-start) | copy-done | bytes 2359320
  74.2 0.0 collective-permute-done.5.n3
  74.2 0.0 collective-permute-done.4.n2
  74.2 0.0 collective-permute-done.3.n1
  74.2 0.1 collective-permute-start.6
  74.3 0.5 collective-permute-start.7
  74.8 0.1 collective-permute-start.8
  74.9 0.4 collective-permute-start.9
  75.3 1.1 collective-permute-done.6.f0
  76.4 1.1 collective-permute-done.7.f1
  77.6 0.9 collective-permute-done.8.f2
  78.5 0.9 collective-permute-done.9.f3
  79.5 33.7 %shard_map.66 = f32[4,9,4,1440]{3,2,1,0:T(4,128)S(1)} custom-call(f32[9,16,8,4,128]{4,3,2,1,0:T(4,128)} %copy-done, f32[2,648,128]{2,1,0:T(8,128)S(1)} %shard_map.65.n0, f32[2,648,128]{2,1,0:T(8,128)} %collective-permute-done.3.n1, f32[2,648,128]{2,1,0:T(8,128)} %collective-permute-done.4.n2, f32[2,648,128]{2,1,0:T(8,128)} %collective-permute-done.5.n3, ...), custom_call_target="tpu_custom_call" | custom-call | tf_op jit(solution)/shard_map/pallas_call | solution.py:505
  113.1 0.0 copy-done.6
  113.1 0.4 bitcast_subtract_fusion
  113.6 1.3 %copy.28 = f32[4,9,4,1440]{3,2,1,0:T(4,128)} copy(f32[4,9,4,1440]{3,0,1,2:T(4,128)S(1)} %bitcast_subtract_fusion) | data formatting | bytes 1658880 | tf_op jit(solution)/shard_map/sub | solution.py:527
  (14 shorter events, 0.1 us)
Async XLA Ops:
  0.0 4.5 %slice-start = ((f32[9,4,1440]{2,1,0:T(4,128)}), f32[9,1,1440]{2,1,0:T(1,128)S(1)}, s32[]{:S(2)}) async-start(f32[9,4,1440]{2,1,0:T(4,128)} %mer_ref.1), calls=%async_computation | async-start | bytes 110592 | tf_op jit(solution)/shard_map/slice | solution.py:462
  0.0 14.8 %collective-permute-start.2 = (f32[288,288]{1,0:T(8,128)}, f32[288,288]{1,0:T(8,128)S(1)}, u32[]{:S(2)}, u32[]{:S(2)}) collective-permute-start(f32[288,288]{1,0:T(8,128)} %bitcast.26), channel_id=1, source_target_pairs={{0,16},{8,24},{16,0},{24,8},{32,48},{40,56},{48,32},{56,40},{64,80... | collective-permute-start | bytes 995336 | tf_op jit(solution)/shard_map/ppermute | solution.py:457
  1.5 9.4 %copy-start.7 = (s32[4,180,1]{1,2,0:T(1,128)S(1)}, s32[4,180,1]{1,2,0:T(1,128)}, u32[]{:S(2)}) copy-start(s32[4,180,1]{1,2,0:T(1,128)} %param.10) | copy-start | bytes 8644
  2.6 27.0 %collective-permute-start = (f32[3,9,4,1440]{3,2,1,0:T(4,128)}, f32[3,9,4,1440]{3,2,1,0:T(4,128)S(1)}, u32[]{:S(2)}, u32[]{:S(2)}) collective-permute-start(f32[3,9,4,1440]{3,2,1,0:T(4,128)} %get-tuple-element.20), channel_id=1, source_target_pairs={{0,8},{8,16},{16,24},{24,32},{32,40},{40,48},{48,56},{56,64},{64,7... | collective-permute-start | bytes 1866248 | tf_op jit(solution)/shard_map/ppermute | solution.py:461
  5.6 24.0 %copy-start.4 = (f32[9,4,1440]{2,1,0:T(4,128)S(1)}, f32[9,4,1440]{2,1,0:T(4,128)}, u32[]{:S(2)}) copy-start(f32[9,4,1440]{2,1,0:T(4,128)} %mer_ref.1) | copy-start | bytes 622084
  5.6 23.9 %collective-permute-start.1 = (f32[30,4,1440]{2,1,0:T(4,128)}, f32[30,4,1440]{2,1,0:T(4,128)S(1)}, u32[]{:S(2)}, u32[]{:S(2)}) collective-permute-start(f32[30,4,1440]{2,1,0:T(4,128)} %pad_maximum_fusion), channel_id=1, source_target_pairs={{8,0},{16,8},{24,16},{32,24},{40,32},{48,40},{56,48},{64,56},{72,6... | collective-permute-start | bytes 2073608 | tf_op jit(solution)/shard_map/ppermute | solution.py:463
  14.8 0.8 copy-start.2
  15.6 1.0 copy-start.1
  16.6 1.0 copy-start.3
  19.7 54.5 %collective-permute-start.5 = (f32[2,648,128]{2,1,0:T(8,128)S(1)}, f32[2,648,128]{2,1,0:T(8,128)}, u32[]{:S(2)}, u32[]{:S(2)}) collective-permute-start(f32[2,648,128]{2,1,0:T(8,128)S(1)} %shard_map.65.n0), channel_id=1, source_target_pairs={{0,96},{8,104},{16,112},{24,120},{32,0},{40,8},{48,16},{56,24},{64... | collective-permute-start | bytes 1990664 | tf_op jit(solution)/shard_map/ppermute | solution.py:478
  25.1 49.1 %collective-permute-start.4 = (f32[2,648,128]{2,1,0:T(8,128)S(1)}, f32[2,648,128]{2,1,0:T(8,128)}, u32[]{:S(2)}, u32[]{:S(2)}) collective-permute-start(f32[2,648,128]{2,1,0:T(8,128)S(1)} %shard_map.65.n0), channel_id=1, source_target_pairs={{0,64},{8,72},{16,80},{24,88},{32,96},{40,104},{48,112},{56,120},{... | collective-permute-start | bytes 1990664 | tf_op jit(solution)/shard_map/ppermute | solution.py:478
  25.8 48.4 %collective-permute-start.3 = (f32[2,648,128]{2,1,0:T(8,128)S(1)}, f32[2,648,128]{2,1,0:T(8,128)}, u32[]{:S(2)}, u32[]{:S(2)}) collective-permute-start(f32[2,648,128]{2,1,0:T(8,128)S(1)} %shard_map.65.n0), channel_id=1, source_target_pairs={{0,32},{8,40},{16,48},{24,56},{32,64},{40,72},{48,80},{56,88},{64,... | collective-permute-start | bytes 1990664 | tf_op jit(solution)/shard_map/ppermute | solution.py:478
  29.5 0.9 copy-start.5
  72.8 1.4 %copy-start = (f32[9,16,8,4,128]{4,3,2,1,0:T(4,128)}, f32[9,16,8,4,128]{4,3,2,1,0:T(4,128)S(1)}, u32[]{:S(2)}) copy-start(f32[9,16,8,4,128]{4,3,2,1,0:T(4,128)S(1)} %get-tuple-element.13.r_ref) | copy-start | bytes 7077892
  74.2 2.2 %collective-permute-start.6 = (f32[2,648,128]{2,1,0:T(8,128)S(1)}, f32[2,648,128]{2,1,0:T(8,128)S(1)}, u32[]{:S(2)}, u32[]{:S(2)}) collective-permute-start(f32[2,648,128]{2,1,0:T(8,128)S(1)} %shard_map.65.n0), channel_id=1, source_target_pairs={{0,8},{8,0},{16,24},{24,16},{32,40},{40,32},{48,56},{56,48},{64,72... | collective-permute-start | bytes 1990664 | tf_op jit(solution)/shard_map/ppermute | solution.py:504
  74.3 3.3 %collective-permute-start.7 = (f32[2,648,128]{2,1,0:T(8,128)}, f32[2,648,128]{2,1,0:T(8,128)S(1)}, u32[]{:S(2)}, u32[]{:S(2)}) collective-permute-start(f32[2,648,128]{2,1,0:T(8,128)} %collective-permute-done.3.n1), channel_id=1, source_target_pairs={{0,8},{8,0},{16,24},{24,16},{32,40},{40,32},{48,56},{56,48},{64,72... | collective-permute-start | bytes 1990664 | tf_op jit(solution)/shard_map/ppermute | solution.py:504
  74.8 3.7 %collective-permute-start.8 = (f32[2,648,128]{2,1,0:T(8,128)}, f32[2,648,128]{2,1,0:T(8,128)S(1)}, u32[]{:S(2)}, u32[]{:S(2)}) collective-permute-start(f32[2,648,128]{2,1,0:T(8,128)} %collective-permute-done.4.n2), channel_id=1, source_target_pairs={{0,8},{8,0},{16,24},{24,16},{32,40},{40,32},{48,56},{56,48},{64,72... | collective-permute-start | bytes 1990664 | tf_op jit(solution)/shard_map/ppermute | solution.py:504
  74.9 4.6 %collective-permute-start.9 = (f32[2,648,128]{2,1,0:T(8,128)}, f32[2,648,128]{2,1,0:T(8,128)S(1)}, u32[]{:S(2)}, u32[]{:S(2)}) collective-permute-start(f32[2,648,128]{2,1,0:T(8,128)} %collective-permute-done.5.n3), channel_id=1, source_target_pairs={{0,8},{8,0},{16,24},{24,16},{32,40},{40,32},{48,56},{56,48},{64,72... | collective-permute-start | bytes 1990664 | tf_op jit(solution)/shard_map/ppermute | solution.py:504
  79.5 33.7 %copy-start.6 = (f32[4,9,4,1440]{3,2,1,0:T(4,128)S(1)}, f32[4,9,4,1440]{3,2,1,0:T(4,128)}, u32[]{:S(2)}) copy-start(f32[4,9,4,1440]{3,2,1,0:T(4,128)} %param.6) | copy-start | bytes 2488324

commit v6 on v5

--- a/solution.py
+++ b/solution.py
@@ -245,7 +245,7 @@
         o_ref[r, 8, :, at] = out[32 + 4 * r : 36 + 4 * r, :lon]
 
 
-CHUNKS = 4
+PIECES = ((0, 0, 2), (0, 1, 2), (1, None, 4), (2, None, 4), (3, None, 4))
 
 
 def greet(lat, lev, levs):
@@ -266,12 +266,14 @@
 
 
 def forth_kernel(
-    rest, levs, tr_ref, south_ref, north_ref, zon_ref, mer_ref, c_ref, slot_ref,
-    r_ref, all_ref, g_ref, col_ref, p_ref, a_ref, s1, r1, s2, r2, s3, r3, lsem,
+    rest, levs, tr_ref, south_ref, north_ref, zonal_ref, mer_ref, c_ref, slot_ref,
+    r_ref, all_ref, zon_ref, g_ref, col_ref, p_ref, a_ref, s1, r1, s2, r2, s3, r3, lsem,
 ):
     lat, lev = lax.axis_index("lat"), lax.axis_index("lev")
     block = tr_ref.shape[1]
     greet(lat, lev, levs)
+    fetch = pltpu.make_async_copy(zonal_ref, zon_ref, lsem.at[3])
+    fetch.start()
     greeted(levs)
 
     def slot_copy(i):
@@ -291,6 +293,7 @@
         for i in range(1, levs):
             level_copy(k, i).start()
 
+    fetch.wait()
     horizontal(tr_ref, south_ref, north_ref, zon_ref, mer_ref, g_ref, level_ready)
     own = pltpu.make_async_copy(g_ref.at[lev], col_ref.at[lev], lsem.at[0])
     own.start()
@@ -329,7 +332,6 @@
     o_ref, y_ref, v_ref, w_ref, z_ref, m_ref, move_ref, s1, r1, s2, r2, lsem, msem,
 ):
     lat, lev = lax.axis_index("lat"), lax.axis_index("lev")
-    size = r_ref.shape[1] // CHUNKS
     greet(lat, lev, levs)
 
     fetches = []
@@ -337,38 +339,42 @@
         fetches.append(pltpu.make_async_copy(ref, m_ref.at[n], msem.at[n]))
         fetches[n].start()
 
-    def base(d):
-        return lax.rem(lat // 4 - d + 4, 4) * size
-
-    def chunk_copy(d, i):
+    def begin(n):
+        d, turn, _ = PIECES[n]
+        at = lax.rem(lat // 4 - d + 4, 4) * 4
+        return at if turn is None else at + lax.rem(lat // 2 + turn, 2) * 2
+
+    def part(n):
+        return pl.ds(begin(n), PIECES[n][2])
+
+    def piece_copy(n, i):
         to = lax.rem(lev + i, levs)
-        part = pl.ds(base(d), size)
-        return send(y_ref.at[:, part, to, 0:3], v_ref.at[:, lev, part, 0:3], s1.at[d, i], r1.at[d, i], lat, to)
+        return send(y_ref.at[:, part(n), to, 0:3], v_ref.at[:, lev, part(n), 0:3], s1.at[n, i], r1.at[n, i], lat, to)
 
     def tile_copy(j, i):
         to = lax.rem(lev + i, levs)
-        part = pl.ds(base(CHUNKS - 1), size)
-        return send(y_ref.at[j, part, to, 0:3], v_ref.at[j, lev, part, 0:3], s2.at[j, i], r2.at[j, i], lat, to)
-
-    def own_copy(d):
-        part = pl.ds(base(d), size)
-        return pltpu.make_async_copy(y_ref.at[:, part, lev, 0:3], v_ref.at[:, lev, part, 0:3], lsem.at[d])
+        at = part(len(PIECES) - 1)
+        return send(y_ref.at[j, at, to, 0:3], v_ref.at[j, lev, at, 0:3], s2.at[j, i], r2.at[j, i], lat, to)
+
+    def own_copy(n):
+        return pltpu.make_async_copy(y_ref.at[:, part(n), lev, 0:3], v_ref.at[:, lev, part(n), 0:3], lsem.at[n])
 
     to_lane = lax.broadcasted_iota(jnp.int32, (256, 1024), 1)
     from_lane = lax.broadcasted_iota(jnp.int32, (256, 1024), 0) & 127
     wanted = ((to_lane >> 2) & 3) * 32 + (to_lane >> 7) * 4 + (to_lane & 3)
     move_ref[...] = (from_lane == wanted).astype(F32).astype(BF16)
 
-    def place_last(d):
+    def place_last(n):
+        size = PIECES[n][2]
         many = 4 * size
-        hi, lo = split(z_ref[:, pl.ds(base(d), size)].reshape(8 * many, 128))
+        hi, lo = split(z_ref[:, part(n)].reshape(8 * many, 128))
         moved = dot(jnp.concatenate([hi, lo], axis=1), move_ref[...])
         group = (lax.broadcasted_iota(jnp.int32, (many, 1024), 1) >> 4) & 7
         x = moved[:many]
         for g in range(1, 8):
             x = jnp.where(group == g, moved[many * g : many * (g + 1)], x)
         for l in range(8):
-            y_ref[8, pl.ds(base(d), size), l] = x[:, 128 * l : 128 * l + 128].reshape(size, 4, 128)
+            y_ref[8, part(n), l] = x[:, 128 * l : 128 * l + 128].reshape(size, 4, 128)
 
     def mix(n, at):
         tiles = [r_ref[j, n].reshape(4 * levs, 128) for j in range(9)]
@@ -396,35 +402,38 @@
         z_ref[:, n] = z.reshape(8, 4, 128)
 
     arrivals = [8] + list(range(8))
-    for d in range(CHUNKS):
-        fetches[2 * d].wait()
-        fetches[2 * d + 1].wait()
-        for at in range(4):
-            hi, lo = split(unpacked(m_ref[2 * d + at % 2, at // 2]))
+    for n, (d, turn, size) in enumerate(PIECES):
+        if turn != 1:
+            fetches[2 * d].wait()
+            fetches[2 * d + 1].wait()
+        for at in range(size):
+            hi, lo = split(unpacked(m_ref[2 * d + at % 2, at // 2 + (turn or 0)]))
             w_ref[0, at] = hi
             w_ref[1, at] = lo
+        first = lax.rem(lat // 4 - d + 4, 4) * 4
 
         @pl.loop(0, size)
         def _(at):
-            mix(base(d) + lax.rem(lat // 2 + at // 2, 2) * 2 + lax.rem(lat + at, 2), at)
-
-        place_last(d)
-        own_copy(d).start()
-        if d == 0:
+            steps = at // 2 if turn is None else turn
+            mix(first + lax.rem(lat // 2 + steps, 2) * 2 + lax.rem(lat + at, 2), at)
+
+        place_last(n)
+        own_copy(n).start()
+        if n == 0:
             greeted(levs)
-        if d < CHUNKS - 1:
+        if n < len(PIECES) - 1:
             for i in range(1, levs):
-                chunk_copy(d, i).start()
+                piece_copy(n, i).start()
         else:
             for j in arrivals:
                 for i in range(1, levs):
                     tile_copy(j, i).start()
 
-    for d in range(CHUNKS):
-        own_copy(d).wait()
-    for d in range(CHUNKS - 1):
+    for n in range(len(PIECES)):
+        own_copy(n).wait()
+    for n in range(len(PIECES) - 1):
         for i in range(1, levs):
-            chunk_copy(d, i).wait()
+            piece_copy(n, i).wait()
     last = None
     for j in arrivals:
         for i in range(1, levs):
@@ -463,7 +472,7 @@
     north = lax.ppermute(
         jnp.concatenate([turned[:3].reshape(3 * levs_here, trac, width), edge], axis=0), "lat", down
     )
-    pair = call(functools.partial(reorder_kernel, groups), (2, order * order // 128, 128), 2)(own, across)
+    pair = call(functools.partial(reorder_kernel, groups), (2, order * order // 128, 128), 2, limit=12)(own, across)
     targets = route[:, :, 0]
     before = jnp.arange(lon)[:, None] < jnp.arange(lon)[None, :]
     same = jnp.logical_and(targets[:, :, None] == targets[:, None, :], before[None])
@@ -484,6 +493,7 @@
         (9, lats, groups, 4, 128),
         7,
         [
+            pltpu.VMEM(zonal.shape, F32),
             levels_of,
             levels_of,
             pltpu.VMEM((9, groups, lats, 4, 128), F32),
@@ -494,9 +504,11 @@
             dma((4, groups)),
             dma((groups,)),
             dma((groups,)),
-            dma((3,)),
+            dma((4,)),
         ],
         extra=jax.ShapeDtypeStruct((groups, 4, 256), jnp.int32),
+        limit=24,
+        large=(3,),
         collective_id=0,
         has_side_effects=True,
     )(turned, south, north, zonal, meridional, courant, slots)
@@ -509,18 +521,19 @@
         [
             pltpu.VMEM((9, lats, groups, 4, 128), F32),
             pltpu.VMEM((9, groups, lats, 4, 128), F32),
-            pltpu.VMEM((2, lats // CHUNKS, order, order), BF16),
+            pltpu.VMEM((2, 4, order, order), BF16),
             pltpu.VMEM((groups, lats, 4, 128), F32),
             pltpu.VMEM((8,) + pair.shape, F32),
             pltpu.VMEM((256, 1024), BF16),
-            dma((CHUNKS - 1, groups)),
-            dma((CHUNKS - 1, groups)),
+            dma((len(PIECES) - 1, groups)),
+            dma((len(PIECES) - 1, groups)),
             dma((9, groups)),
             dma((9, groups)),
-            dma((CHUNKS,)),
+            dma((len(PIECES),)),
             dma((8,)),
         ],
         large=range(1, 9),
+        limit=28,
         collective_id=1,
         has_side_effects=True,
     )(received, pair, *shifted, *far, all_slots)

time: 115 us -> 111 us (0.965)
  Pallas kernels: 78 us -> 74.9 us
  local copies, waits for them, and re-layouts: 12.9 us -> 11.5 us
    pallas_call x1, Pallas kernels: 33.7 us -> 30.6 us  [body(): call(functools.partial(back_kernel, rest, groups, order), (4, levs_here,...]
    unnamed x20 -> x18, local copies, waits for them, and re-layouts: 7.74 us -> 6.31 us
  transfers between devices with their start and end apart: 10 -> 10, of which waited for: 5 -> 5; matrix products, arithmetic and copies ran while one was open for 7% -> 7% of each run, Pallas kernels for 39% -> 40%
where the time goes in v6:
time: 111 us; the launch traced here: 110 us
  Pallas kernels  74.9 us (67%)
  starting transfers between devices  15.3 us (14%)
  local copies, waits for them, and re-layouts  11.5 us (10%)
  waiting for transfers between devices  6.41 us (6%)
  other arithmetic  1.88 us (2%)
    pallas_call x1, Pallas kernels, body(): call(functools.partial(forth_kernel, rest, groups), (9, lats, groups, 4,...  42.3 us
    pallas_call x1, Pallas kernels, body(): call(functools.partial(back_kernel, rest, groups, order), (4, levs_here,...  30.6 us
    ppermute x3, starting transfers between devices, body(): lax.ppermute(pair, 'lat', [(i, (i + 4 * d) % lats) for i in range(lats)])  7.08 us
    unnamed x18, local copies, waits for them, and re-layouts  6.31 us
    ppermute x1, starting transfers between devices, body(): lax.ppermute(jnp.concatenate([turned[:3].reshape(3 * levs_here, trac, wid...  5.27 us
    ppermute x4, waiting for transfers between devices, body(): far = [lax.ppermute(x, 'lat', other) for x in [pair] + shifted]  4.14 us
    ppermute x1, waiting for transfers between devices, body(): across = lax.ppermute(own, 'lat', [(i, i ^ 2) for i in range(lats)])  2.26 us
  transfers between devices with their start and end apart: 10, of which 5 were waited for; matrix products, arithmetic and copies ran while one was open for 7% of the time, Pallas kernels for 40%

profile of v6, /device:TPU:64, one launch (start us, length us, event | category | flops | bytes accessed | tf_op | source)
XLA Modules:
  0.0 110.3 jit_solution(3876744429283226180)
XLA Ops:
  0.0 0.0 slice-start
  0.0 0.0 collective-permute-start.2
  0.0 1.5 %copy.45 = f32[4,9,4,1440]{3,0,1,2:T(4,128)S(1)} copy(f32[4,9,4,1440]{3,2,1,0:T(4,128)} %param.6) | data formatting | bytes 1658880 | tf_op args[0]
  1.5 0.0 copy-start.6
  1.5 1.0 fusion.6
  2.6 1.9 %collective-permute-start = (f32[3,9,4,1440]{3,2,1,0:T(4,128)}, f32[3,9,4,1440]{3,2,1,0:T(4,128)S(1)}, u32[]{:S(2)}, u32[]{:S(2)}) collective-permute-start(f32[3,9,4,1440]{3,2,1,0:T(4,128)} %get-tuple-element.20), channel_id=1, source_target_pairs={{0,8},{8,16},{16,24},{24,32},{32,40},{40,48},{48,56},{56,64},{64,7... | collective-permute-start | bytes 1866248 | tf_op jit(solution)/shard_map/ppermute | solution.py:470
  4.5 0.0 slice-done
  4.6 1.0 pad_maximum_fusion
  5.6 0.0 copy-start.3
  5.6 5.3 %collective-permute-start.1 = (f32[30,4,1440]{2,1,0:T(4,128)}, f32[30,4,1440]{2,1,0:T(4,128)S(1)}, u32[]{:S(2)}, u32[]{:S(2)}) collective-permute-start(f32[30,4,1440]{2,1,0:T(4,128)} %pad_maximum_fusion), channel_id=1, source_target_pairs={{8,0},{16,8},{24,16},{32,24},{40,32},{48,40},{56,48},{64,56},{72,6... | collective-permute-start | bytes 2073608 | tf_op jit(solution)/shard_map/ppermute | solution.py:472
  10.9 0.0 copy-done.6
  10.9 0.1 copy.26
  11.0 0.4 convert_reduce_fusion
  11.5 1.0 copy.21
  12.5 2.3 %collective-permute-done.2.n_ref = f32[288,288]{1,0:T(8,128)S(1)} collective-permute-done((f32[288,288]{1,0:T(8,128)}, f32[288,288]{1,0:T(8,128)S(1)}, u32[]{:S(2)}, u32[]{:S(2)}) %collective-permute-start.2) | collective-permute-done | bytes 331808 | tf_op jit(solution)/shard_map/ppermute | solution.py:466
  14.8 0.0 copy-start.1
  14.8 0.8 copy-done.1
  15.6 0.0 copy-start
  15.6 1.0 copy-done
  16.6 1.0 copy-done.2
  17.6 2.1 %shard_map.65.n0 = f32[2,648,128]{2,1,0:T(8,128)S(1)} custom-call(f32[288,288]{1,0:T(8,128)S(1)} %bitcast.27, f32[288,288]{1,0:T(8,128)S(1)} %copy-done.2), custom_call_target="tpu_custom_call" | custom-call | tf_op jit(solution)/shard_map/pallas_call | solution.py:475
  19.7 5.5 %collective-permute-start.5 = (f32[2,648,128]{2,1,0:T(8,128)S(1)}, f32[2,648,128]{2,1,0:T(8,128)}, u32[]{:S(2)}, u32[]{:S(2)}) collective-permute-start(f32[2,648,128]{2,1,0:T(8,128)S(1)} %shard_map.65.n0), channel_id=1, source_target_pairs={{0,96},{8,104},{16,112},{24,120},{32,0},{40,8},{48,16},{56,24},{64... | collective-permute-start | bytes 1990664 | tf_op jit(solution)/shard_map/ppermute | solution.py:487
  25.1 0.6 collective-permute-start.4
  25.8 1.0 collective-permute-start.3
  26.7 0.7 copy_bitcast_fusion.4
  27.5 0.7 copy_bitcast_fusion.2
  28.2 1.3 %concatenate.7.c_ref = f32[72,2,384]{2,1,0:T(2,128)S(1)} concatenate(f32[72,2,128]{2,1,0:T(2,128)} %get-tuple-element.26, f32[72,2,128]{2,1,0:T(2,128)S(1)} %get-tuple-element.25, f32[72,2,52]{2,1,0:T(2,128)} %get-tuple-element.28, f32[72,2,52]{2,1,0:T(2,128)} %get-tuple-element.27, f32[72,2,24]{2,1,0:T(2,128)S(1)} %broadcast_in_dim.2), dimensions={2} | concatenate | bytes 442368 | tf_op jit(solution)/shard_map/concatenate | solution.py:483
  29.5 0.0 collective-permute-done.south_ref
  29.5 0.0 collective-permute-done.1.north_ref
  29.5 0.0 copy-done.3
  29.6 0.0 copy-start.4
  29.6 0.9 copy-done.4
  30.5 42.3 %shard_map.64 = (f32[9,16,8,4,128]{4,3,2,1,0:T(4,128)S(1)}, s32[8,4,256]{2,1,0:T(4,128)S(1)}) custom-call(f32[4,9,4,1440]{3,2,1,0:T(4,128)S(1)} %bitcast.25, f32[3,9,4,1440]{3,2,1,0:T(4,128)S(1)} %collective-permute-done.south_ref, f32[30,4,1440]{2,1,0:T(4,128)S(1)} %collective-permute-done.1.north_ref, f32[9,4,1440]{2,1,0:T(4,128)S(1)} %copy-done.4, ...), custom_call_target="tpu_custom_call" | custom-call | tf_op jit(solution)/shard_map/pallas_call | solution.py:491
  72.8 0.0 collective-permute-done.5.n3
  72.8 0.0 collective-permute-done.4.n2
  72.8 0.0 collective-permute-done.3.n1
  72.8 0.1 collective-permute-start.6
  72.9 0.5 collective-permute-start.7
  73.4 0.1 collective-permute-start.8
  73.5 0.4 collective-permute-start.9
  73.9 1.1 collective-permute-done.6.f0
  75.0 1.1 %collective-permute-done.7.f1 = f32[2,648,128]{2,1,0:T(8,128)S(1)} collective-permute-done((f32[2,648,128]{2,1,0:T(8,128)}, f32[2,648,128]{2,1,0:T(8,128)S(1)}, u32[]{:S(2)}, u32[]{:S(2)}) %collective-permute-start.7) | collective-permute-done | bytes 663584 | tf_op jit(solution)/shard_map/ppermute | solution.py:516
  76.1 0.9 collective-permute-done.8.f2
  77.1 0.9 collective-permute-done.9.f3
  78.0 30.6 %shard_map.66 = f32[4,9,4,1440]{3,2,1,0:T(4,128)S(1)} custom-call(f32[9,16,8,4,128]{4,3,2,1,0:T(4,128)S(1)} %get-tuple-element.13.r_ref, f32[2,648,128]{2,1,0:T(8,128)S(1)} %shard_map.65.n0, f32[2,648,128]{2,1,0:T(8,128)} %collective-permute-done.3.n1, f32[2,648,128]{2,1,0:T(8,128)} %collective-permute-done.4.n2, f32[2,648,128]{2,1,0:T(8,128)} %collective-permute-done.5.n3, ...), custom_call_target="tpu_custom_call" | custom-call | tf_op jit(solution)/shard_map/pallas_call | solution.py:517
  108.6 0.0 copy-done.5
  108.6 0.4 bitcast_subtract_fusion
  109.1 1.3 %copy.28 = f32[4,9,4,1440]{3,2,1,0:T(4,128)} copy(f32[4,9,4,1440]{3,0,1,2:T(4,128)S(1)} %bitcast_subtract_fusion) | data formatting | bytes 1658880 | tf_op jit(solution)/shard_map/sub | solution.py:540
  (12 shorter events, 0.1 us)
Async XLA Ops:
  0.0 4.5 %slice-start = ((f32[9,4,1440]{2,1,0:T(4,128)}), f32[9,1,1440]{2,1,0:T(1,128)S(1)}, s32[]{:S(2)}) async-start(f32[9,4,1440]{2,1,0:T(4,128)} %mer_ref.1), calls=%async_computation | async-start | bytes 110592 | tf_op jit(solution)/shard_map/slice | solution.py:471
  0.0 14.8 %collective-permute-start.2 = (f32[288,288]{1,0:T(8,128)}, f32[288,288]{1,0:T(8,128)S(1)}, u32[]{:S(2)}, u32[]{:S(2)}) collective-permute-start(f32[288,288]{1,0:T(8,128)} %bitcast.26), channel_id=1, source_target_pairs={{0,16},{8,24},{16,0},{24,8},{32,48},{40,56},{48,32},{56,40},{64,80... | collective-permute-start | bytes 995336 | tf_op jit(solution)/shard_map/ppermute | solution.py:466
  1.5 9.4 %copy-start.6 = (s32[4,180,1]{1,2,0:T(1,128)S(1)}, s32[4,180,1]{1,2,0:T(1,128)}, u32[]{:S(2)}) copy-start(s32[4,180,1]{1,2,0:T(1,128)} %param.10) | copy-start | bytes 8644
  2.6 27.0 %collective-permute-start = (f32[3,9,4,1440]{3,2,1,0:T(4,128)}, f32[3,9,4,1440]{3,2,1,0:T(4,128)S(1)}, u32[]{:S(2)}, u32[]{:S(2)}) collective-permute-start(f32[3,9,4,1440]{3,2,1,0:T(4,128)} %get-tuple-element.20), channel_id=1, source_target_pairs={{0,8},{8,16},{16,24},{24,32},{32,40},{40,48},{48,56},{56,64},{64,7... | collective-permute-start | bytes 1866248 | tf_op jit(solution)/shard_map/ppermute | solution.py:470
  5.6 24.0 %copy-start.3 = (f32[9,4,1440]{2,1,0:T(4,128)S(1)}, f32[9,4,1440]{2,1,0:T(4,128)}, u32[]{:S(2)}) copy-start(f32[9,4,1440]{2,1,0:T(4,128)} %mer_ref.1) | copy-start | bytes 622084
  5.6 23.9 %collective-permute-start.1 = (f32[30,4,1440]{2,1,0:T(4,128)}, f32[30,4,1440]{2,1,0:T(4,128)S(1)}, u32[]{:S(2)}, u32[]{:S(2)}) collective-permute-start(f32[30,4,1440]{2,1,0:T(4,128)} %pad_maximum_fusion), channel_id=1, source_target_pairs={{8,0},{16,8},{24,16},{32,24},{40,32},{48,40},{56,48},{64,56},{72,6... | collective-permute-start | bytes 2073608 | tf_op jit(solution)/shard_map/ppermute | solution.py:472
  14.8 0.8 copy-start.1
  15.6 1.0 copy-start
  16.6 1.0 copy-start.2
  19.7 53.1 %collective-permute-start.5 = (f32[2,648,128]{2,1,0:T(8,128)S(1)}, f32[2,648,128]{2,1,0:T(8,128)}, u32[]{:S(2)}, u32[]{:S(2)}) collective-permute-start(f32[2,648,128]{2,1,0:T(8,128)S(1)} %shard_map.65.n0), channel_id=1, source_target_pairs={{0,96},{8,104},{16,112},{24,120},{32,0},{40,8},{48,16},{56,24},{64... | collective-permute-start | bytes 1990664 | tf_op jit(solution)/shard_map/ppermute | solution.py:487
  25.1 47.6 %collective-permute-start.4 = (f32[2,648,128]{2,1,0:T(8,128)S(1)}, f32[2,648,128]{2,1,0:T(8,128)}, u32[]{:S(2)}, u32[]{:S(2)}) collective-permute-start(f32[2,648,128]{2,1,0:T(8,128)S(1)} %shard_map.65.n0), channel_id=1, source_target_pairs={{0,64},{8,72},{16,80},{24,88},{32,96},{40,104},{48,112},{56,120},{... | collective-permute-start | bytes 1990664 | tf_op jit(solution)/shard_map/ppermute | solution.py:487
  25.8 47.0 %collective-permute-start.3 = (f32[2,648,128]{2,1,0:T(8,128)S(1)}, f32[2,648,128]{2,1,0:T(8,128)}, u32[]{:S(2)}, u32[]{:S(2)}) collective-permute-start(f32[2,648,128]{2,1,0:T(8,128)S(1)} %shard_map.65.n0), channel_id=1, source_target_pairs={{0,32},{8,40},{16,48},{24,56},{32,64},{40,72},{48,80},{56,88},{64,... | collective-permute-start | bytes 1990664 | tf_op jit(solution)/shard_map/ppermute | solution.py:487
  29.6 0.9 copy-start.4
  72.8 2.2 %collective-permute-start.6 = (f32[2,648,128]{2,1,0:T(8,128)S(1)}, f32[2,648,128]{2,1,0:T(8,128)S(1)}, u32[]{:S(2)}, u32[]{:S(2)}) collective-permute-start(f32[2,648,128]{2,1,0:T(8,128)S(1)} %shard_map.65.n0), channel_id=1, source_target_pairs={{0,8},{8,0},{16,24},{24,16},{32,40},{40,32},{48,56},{56,48},{64,72... | collective-permute-start | bytes 1990664 | tf_op jit(solution)/shard_map/ppermute | solution.py:516
  72.9 3.3 %collective-permute-start.7 = (f32[2,648,128]{2,1,0:T(8,128)}, f32[2,648,128]{2,1,0:T(8,128)S(1)}, u32[]{:S(2)}, u32[]{:S(2)}) collective-permute-start(f32[2,648,128]{2,1,0:T(8,128)} %collective-permute-done.3.n1), channel_id=1, source_target_pairs={{0,8},{8,0},{16,24},{24,16},{32,40},{40,32},{48,56},{56,48},{64,72... | collective-permute-start | bytes 1990664 | tf_op jit(solution)/shard_map/ppermute | solution.py:516
  73.4 3.7 %collective-permute-start.8 = (f32[2,648,128]{2,1,0:T(8,128)}, f32[2,648,128]{2,1,0:T(8,128)S(1)}, u32[]{:S(2)}, u32[]{:S(2)}) collective-permute-start(f32[2,648,128]{2,1,0:T(8,128)} %collective-permute-done.4.n2), channel_id=1, source_target_pairs={{0,8},{8,0},{16,24},{24,16},{32,40},{40,32},{48,56},{56,48},{64,72... | collective-permute-start | bytes 1990664 | tf_op jit(solution)/shard_map/ppermute | solution.py:516
  73.5 4.6 %collective-permute-start.9 = (f32[2,648,128]{2,1,0:T(8,128)}, f32[2,648,128]{2,1,0:T(8,128)S(1)}, u32[]{:S(2)}, u32[]{:S(2)}) collective-permute-start(f32[2,648,128]{2,1,0:T(8,128)} %collective-permute-done.5.n3), channel_id=1, source_target_pairs={{0,8},{8,0},{16,24},{24,16},{32,40},{40,32},{48,56},{56,48},{64,72... | collective-permute-start | bytes 1990664 | tf_op jit(solution)/shard_map/ppermute | solution.py:516
  78.0 30.6 %copy-start.5 = (f32[4,9,4,1440]{3,2,1,0:T(4,128)S(1)}, f32[4,9,4,1440]{3,2,1,0:T(4,128)}, u32[]{:S(2)}) copy-start(f32[4,9,4,1440]{3,2,1,0:T(4,128)} %param.6) | copy-start | bytes 2488324

commit v7 on v6

--- a/solution.py
+++ b/solution.py
@@ -36,7 +36,7 @@
     return (7.0 / 12.0) * (q_m1 + q_0) - (1.0 / 12.0) * (q_m2 + q_p1)
 
 
-def horizontal(tr_ref, south_ref, north_ref, zon_ref, mer_ref, g_ref, ready):
+def horizontal(tr_ref, south_ref, north_ref, both_ref, g_ref, ready):
     lat = lax.axis_index("lat")
     last = lax.axis_size("lat") - 1
     width = tr_ref.shape[3]
@@ -81,7 +81,7 @@
             kk.append(6.0 * q[p + 1] - 3.0 * (e[p] + right))
         ss = [swap(x) for x in s]
         sk = [swap(x) for x in kk]
-        m = mer_ref[k]
+        m = both_ref[1, k]
         zero = jnp.zeros((8, width), F32)
         m0 = jnp.where(sub, m[0:1] * ksouth, m[1:2])
         m1 = jnp.where(sub, m[2:3], m[3:4])
@@ -93,7 +93,7 @@
                 flux(c, e[p], jnp.where(sub, ss[p - 1], ss[p]), s[p], jnp.where(sub, sk[p - 1], sk[p]), kk[p])
             )
         sf = [swap(x) for x in f]
-        z = zon_ref[k]
+        z = both_ref[0, k]
         out = []
         for p in range(2):
             lat_change = f[p] - jnp.where(sub, sf[p], sf[p + 1])
@@ -198,8 +198,8 @@
         ready(r)
 
 
-def reorder_kernel(levs, m_ref, n_ref, o_ref):
-    order = m_ref.shape[0]
+def reorder_kernel(levs, m_ref, o_ref):
+    order = m_ref.shape[1]
     levels = order // 4
     block = levels // levs
     x = lax.broadcasted_iota(jnp.int32, (order, order), 0)
@@ -209,9 +209,9 @@
     last = (x & 3) * levels + block * ((x - 256) >> 2) + block - 1
     put = (jnp.where(x < 256, main, last) == o).astype(F32).astype(BF16)
     part = order // 4
-    for n, ref in enumerate((m_ref, n_ref)):
-        hi, lo = split(ref[...])
-        rest = (ref[...] - hi.astype(F32) - lo.astype(F32)).astype(BF16)
+    for n in range(2):
+        hi, lo = split(m_ref[n])
+        rest = (m_ref[n] - hi.astype(F32) - lo.astype(F32)).astype(BF16)
         out = None
         for piece in (hi, lo, rest):
             term = dot(dot(put, piece).astype(BF16), pick, NT)
@@ -266,14 +266,12 @@
 
 
 def forth_kernel(
-    rest, levs, tr_ref, south_ref, north_ref, zonal_ref, mer_ref, c_ref, slot_ref,
-    r_ref, all_ref, zon_ref, g_ref, col_ref, p_ref, a_ref, s1, r1, s2, r2, s3, r3, lsem,
+    rest, levs, tr_ref, south_ref, north_ref, both_ref, c_ref, slot_ref,
+    r_ref, all_ref, g_ref, col_ref, p_ref, a_ref, s1, r1, s2, r2, s3, r3, lsem,
 ):
     lat, lev = lax.axis_index("lat"), lax.axis_index("lev")
     block = tr_ref.shape[1]
     greet(lat, lev, levs)
-    fetch = pltpu.make_async_copy(zonal_ref, zon_ref, lsem.at[3])
-    fetch.start()
     greeted(levs)
 
     def slot_copy(i):
@@ -293,8 +291,7 @@
         for i in range(1, levs):
             level_copy(k, i).start()
 
-    fetch.wait()
-    horizontal(tr_ref, south_ref, north_ref, zon_ref, mer_ref, g_ref, level_ready)
+    horizontal(tr_ref, south_ref, north_ref, both_ref, g_ref, level_ready)
     own = pltpu.make_async_copy(g_ref.at[lev], col_ref.at[lev], lsem.at[0])
     own.start()
     own.wait()
@@ -472,7 +469,7 @@
     north = lax.ppermute(
         jnp.concatenate([turned[:3].reshape(3 * levs_here, trac, width), edge], axis=0), "lat", down
     )
-    pair = call(functools.partial(reorder_kernel, groups), (2, order * order // 128, 128), 2, limit=12)(own, across)
+    pair = call(functools.partial(reorder_kernel, groups), (2, order * order // 128, 128), 1, limit=12)(jnp.stack([own, across]))
     targets = route[:, :, 0]
     before = jnp.arange(lon)[:, None] < jnp.arange(lon)[None, :]
     same = jnp.logical_and(targets[:, :, None] == targets[:, None, :], before[None])
@@ -491,9 +488,8 @@
     received, all_slots = call(
         functools.partial(forth_kernel, rest, groups),
         (9, lats, groups, 4, 128),
-        7,
+        6,
         [
-            pltpu.VMEM(zonal.shape, F32),
             levels_of,
             levels_of,
             pltpu.VMEM((9, groups, lats, 4, 128), F32),
@@ -504,14 +500,13 @@
             dma((4, groups)),
             dma((groups,)),
             dma((groups,)),
-            dma((4,)),
+            dma((3,)),
         ],
         extra=jax.ShapeDtypeStruct((groups, 4, 256), jnp.int32),
         limit=24,
-        large=(3,),
         collective_id=0,
         has_side_effects=True,
-    )(turned, south, north, zonal, meridional, courant, slots)
+    )(turned, south, north, jnp.stack([zonal, meridional]), courant, slots)
     received, pair, shifted = lax.optimization_barrier((received, pair, shifted))
     far = [lax.ppermute(x, "lat", other) for x in [pair] + shifted]
     whole = call(

time: 111 us -> 113 us (1.018)
  the two profiles are of different devices: /device:TPU:64 before, /device:TPU:24 now
where the time goes in v7:
time: 113 us; the launch traced here: 112 us
  Pallas kernels  74.7 us (66%)
  starting transfers between devices  17 us (15%)
  waiting for transfers between devices  11.7 us (10%)
  local copies, waits for them, and re-layouts  5.71 us (5%)
  other arithmetic  3.08 us (3%)
    pallas_call x1, Pallas kernels, body(): call(functools.partial(forth_kernel, rest, groups), (9, lats, groups, 4,...  41.1 us
    pallas_call x1, Pallas kernels, body(): call(functools.partial(back_kernel, rest, groups, order), (4, levs_here,...  31.5 us
    ppermute x1, starting transfers between devices, body(): lax.ppermute(jnp.concatenate([turned[:3].reshape(3 * levs_here, trac, wid...  6.03 us
    ppermute x4, waiting for transfers between devices, body(): far = [lax.ppermute(x, 'lat', other) for x in [pair] + shifted]  4.14 us
    ppermute x1, waiting for transfers between devices, body(): across = lax.ppermute(own, 'lat', [(i, i ^ 2) for i in range(lats)])  4.02 us
    ppermute x3, starting transfers between devices, body(): lax.ppermute(pair, 'lat', [(i, (i + 4 * d) % lats) for i in range(lats)])  3.93 us
    ppermute x1, starting transfers between devices, body(): across = lax.ppermute(own, 'lat', [(i, i ^ 2) for i in range(lats)])  3.88 us
    ppermute x1, waiting for transfers between devices, body(): lax.ppermute(jnp.concatenate([turned[:3].reshape(3 * levs_here, trac, wid...  3.52 us
  transfers between devices with their start and end apart: 10, of which 6 were waited for; matrix products, arithmetic and copies ran while one was open for 6% of the time, Pallas kernels for 38%

profile of v7, /device:TPU:24, one launch (start us, length us, event | category | flops | bytes accessed | tf_op | source)
XLA Modules:
  0.0 112.4 jit_solution(7469907947972450766)
XLA Ops:
  0.0 0.0 slice-start
  0.0 3.9 %collective-permute-start.2 = (f32[288,288]{1,0:T(8,128)}, f32[288,288]{1,0:T(8,128)S(1)}, u32[]{:S(2)}, u32[]{:S(2)}) collective-permute-start(f32[288,288]{1,0:T(8,128)} %bitcast.33), channel_id=1, source_target_pairs={{0,16},{8,24},{16,0},{24,8},{32,48},{40,56},{48,32},{56,40},{64,80... | collective-permute-start | bytes 995336 | tf_op jit(solution)/shard_map/ppermute | solution.py:463
  3.9 1.5 %copy.45 = f32[4,9,4,1440]{3,0,1,2:T(4,128)S(1)} copy(f32[4,9,4,1440]{3,2,1,0:T(4,128)} %param.6) | data formatting | bytes 1658880 | tf_op args[0]
  5.4 0.0 copy-start.2
  5.4 1.0 fusion.6
  6.4 0.0 copy-start.1
  6.4 2.0 %collective-permute-start = (f32[3,9,4,1440]{3,2,1,0:T(4,128)}, f32[3,9,4,1440]{3,2,1,0:T(4,128)S(1)}, u32[]{:S(2)}, u32[]{:S(2)}) collective-permute-start(f32[3,9,4,1440]{3,2,1,0:T(4,128)} %get-tuple-element.20), channel_id=1, source_target_pairs={{0,8},{8,16},{16,24},{24,32},{32,40},{40,48},{48,56},{56,64},{64,7... | collective-permute-start | bytes 1866248 | tf_op jit(solution)/shard_map/ppermute | solution.py:467
  8.5 0.0 slice-done
  8.5 1.0 pad_maximum_fusion.1
  9.6 6.0 %collective-permute-start.1 = (f32[30,4,1440]{2,1,0:T(4,128)}, f32[30,4,1440]{2,1,0:T(4,128)S(1)}, u32[]{:S(2)}, u32[]{:S(2)}) collective-permute-start(f32[30,4,1440]{2,1,0:T(4,128)} %pad_maximum_fusion.1), channel_id=1, source_target_pairs={{8,0},{16,8},{24,16},{32,24},{40,32},{48,40},{56,48},{64,56},{72,6... | collective-permute-start | bytes 2073608 | tf_op jit(solution)/shard_map/ppermute | solution.py:469
  15.6 0.0 copy-done.2
  15.7 0.1 copy.26
  15.8 1.0 copy.21
  16.8 0.4 convert_reduce_fusion
  17.3 0.1 copy_bitcast_fusion.4
  17.3 4.0 %collective-permute-done.2 = f32[288,288]{1,0:T(8,128)S(1)} collective-permute-done((f32[288,288]{1,0:T(8,128)}, f32[288,288]{1,0:T(8,128)S(1)}, u32[]{:S(2)}, u32[]{:S(2)}) %collective-permute-start.2) | collective-permute-done | bytes 331808 | tf_op jit(solution)/shard_map/ppermute | solution.py:463
  21.4 0.0 copy-done.1
  21.4 0.1 pad_maximum_fusion.m_ref
  21.4 2.1 %shard_map.65.n0 = f32[2,648,128]{2,1,0:T(8,128)S(1)} custom-call(f32[2,288,288]{2,1,0:T(8,128)S(1)} %pad_maximum_fusion.m_ref), custom_call_target="tpu_custom_call" | custom-call | tf_op jit(solution)/shard_map/pallas_call | solution.py:472
  23.5 0.8 collective-permute-start.5
  24.3 0.6 collective-permute-start.4
  24.9 2.5 %collective-permute-start.3 = (f32[2,648,128]{2,1,0:T(8,128)S(1)}, f32[2,648,128]{2,1,0:T(8,128)}, u32[]{:S(2)}, u32[]{:S(2)}) collective-permute-start(f32[2,648,128]{2,1,0:T(8,128)S(1)} %shard_map.65.n0), channel_id=1, source_target_pairs={{0,32},{8,40},{16,48},{24,56},{32,64},{40,72},{48,80},{56,88},{64,... | collective-permute-start | bytes 1990664 | tf_op jit(solution)/shard_map/ppermute | solution.py:484
  27.5 0.1 copy_bitcast_fusion.2
  27.6 0.5 concatenate.7.c_ref
  28.1 1.1 %pad_maximum_fusion.2.both_ref = f32[2,9,4,1440]{3,2,1,0:T(4,128)S(1)} fusion(f32[1,9,4,1440]{3,2,1,0:T(4,128)} %bitcast.37, f32[1,9,4,1440]{3,2,1,0:T(4,128)} %bitcast.38), kind=kLoop, calls=%fused_computation.5 | loop fusion | flops 103680 | bytes 829440 | tf_op jit(solution)/shard_map/stack | solution.py:509
  29.2 0.0 collective-permute-done.south_ref
  29.3 3.5 %collective-permute-done.1.north_ref = f32[30,4,1440]{2,1,0:T(4,128)S(1)} collective-permute-done((f32[30,4,1440]{2,1,0:T(4,128)}, f32[30,4,1440]{2,1,0:T(4,128)S(1)}, u32[]{:S(2)}, u32[]{:S(2)}) %collective-permute-start.1) | collective-permute-done | bytes 691232 | tf_op jit(solution)/shard_map/ppermute | solution.py:469
  32.8 41.1 %shard_map.64 = (f32[9,16,8,4,128]{4,3,2,1,0:T(4,128)S(1)}, s32[8,4,256]{2,1,0:T(4,128)S(1)}) custom-call(f32[4,9,4,1440]{3,2,1,0:T(4,128)S(1)} %bitcast.29, f32[3,9,4,1440]{3,2,1,0:T(4,128)S(1)} %collective-permute-done.south_ref, f32[30,4,1440]{2,1,0:T(4,128)S(1)} %collective-permute-done.1.north_ref, f32[2,9,4,1440]{3,2,1,0:T(4,128)S(1)} %pad_maximum_fusion.2.both_ref, ...), custom_call_target="tpu_custom_call" | custom-call | tf_op jit(solution)/shard_map/pallas_call | solution.py:488
  73.9 0.0 collective-permute-done.5.n3
  73.9 0.0 collective-permute-done.4.n2
  73.9 0.0 collective-permute-done.3.n1
  73.9 0.3 collective-permute-start.6
  74.3 0.3 collective-permute-start.7
  74.5 0.3 collective-permute-start.8
  74.8 0.3 collective-permute-start.9
  75.0 1.1 collective-permute-done.6.f0
  76.1 1.2 %collective-permute-done.7.f1 = f32[2,648,128]{2,1,0:T(8,128)S(1)} collective-permute-done((f32[2,648,128]{2,1,0:T(8,128)}, f32[2,648,128]{2,1,0:T(8,128)S(1)}, u32[]{:S(2)}, u32[]{:S(2)}) %collective-permute-start.7) | collective-permute-done | bytes 663584 | tf_op jit(solution)/shard_map/ppermute | solution.py:511
  77.3 0.9 collective-permute-done.8.f2
  78.2 0.9 collective-permute-done.9.f3
  79.2 0.0 copy-start
  79.2 31.5 %shard_map.66 = f32[4,9,4,1440]{3,2,1,0:T(4,128)S(1)} custom-call(f32[9,16,8,4,128]{4,3,2,1,0:T(4,128)S(1)} %get-tuple-element.13.r_ref, f32[2,648,128]{2,1,0:T(8,128)S(1)} %shard_map.65.n0, f32[2,648,128]{2,1,0:T(8,128)} %collective-permute-done.3.n1, f32[2,648,128]{2,1,0:T(8,128)} %collective-permute-done.4.n2, f32[2,648,128]{2,1,0:T(8,128)} %collective-permute-done.5.n3, ...), custom_call_target="tpu_custom_call" | custom-call | tf_op jit(solution)/shard_map/pallas_call | solution.py:512
  110.7 0.0 copy-done
  110.7 0.4 bitcast_subtract_fusion
  111.2 1.3 %copy.28 = f32[4,9,4,1440]{3,2,1,0:T(4,128)} copy(f32[4,9,4,1440]{3,0,1,2:T(4,128)S(1)} %bitcast_subtract_fusion) | data formatting | bytes 1658880 | tf_op jit(solution)/shard_map/sub | solution.py:535
  (10 shorter events, 0.1 us)
Async XLA Ops:
  0.0 8.5 %slice-start = ((f32[9,4,1440]{2,1,0:T(4,128)}), f32[9,1,1440]{2,1,0:T(1,128)S(1)}, s32[]{:S(2)}) async-start(f32[9,4,1440]{2,1,0:T(4,128)} %param.8), calls=%async_computation | async-start | bytes 110592 | tf_op jit(solution)/shard_map/slice | solution.py:468
  0.0 21.4 %collective-permute-start.2 = (f32[288,288]{1,0:T(8,128)}, f32[288,288]{1,0:T(8,128)S(1)}, u32[]{:S(2)}, u32[]{:S(2)}) collective-permute-start(f32[288,288]{1,0:T(8,128)} %bitcast.33), channel_id=1, source_target_pairs={{0,16},{8,24},{16,0},{24,8},{32,48},{40,56},{48,32},{56,40},{64,80... | collective-permute-start | bytes 995336 | tf_op jit(solution)/shard_map/ppermute | solution.py:463
  5.4 10.2 %copy-start.2 = (s32[4,180,1]{1,2,0:T(1,128)S(1)}, s32[4,180,1]{1,2,0:T(1,128)}, u32[]{:S(2)}) copy-start(s32[4,180,1]{1,2,0:T(1,128)} %param.10) | copy-start | bytes 8644
  6.4 15.0 %copy-start.1 = (f32[1,1,288,288]{3,2,1,0:T(8,128)S(1)}, f32[1,1,288,288]{3,2,1,0:T(8,128)}, u32[]{:S(2)}) copy-start(f32[1,1,288,288]{3,2,1,0:T(8,128)} %param.11) | copy-start | bytes 995332
  6.4 22.8 %collective-permute-start = (f32[3,9,4,1440]{3,2,1,0:T(4,128)}, f32[3,9,4,1440]{3,2,1,0:T(4,128)S(1)}, u32[]{:S(2)}, u32[]{:S(2)}) collective-permute-start(f32[3,9,4,1440]{3,2,1,0:T(4,128)} %get-tuple-element.20), channel_id=1, source_target_pairs={{0,8},{8,16},{16,24},{24,32},{32,40},{40,48},{48,56},{56,64},{64,7... | collective-permute-start | bytes 1866248 | tf_op jit(solution)/shard_map/ppermute | solution.py:467
  9.6 23.2 %collective-permute-start.1 = (f32[30,4,1440]{2,1,0:T(4,128)}, f32[30,4,1440]{2,1,0:T(4,128)S(1)}, u32[]{:S(2)}, u32[]{:S(2)}) collective-permute-start(f32[30,4,1440]{2,1,0:T(4,128)} %pad_maximum_fusion.1), channel_id=1, source_target_pairs={{8,0},{16,8},{24,16},{32,24},{40,32},{48,40},{56,48},{64,56},{72,6... | collective-permute-start | bytes 2073608 | tf_op jit(solution)/shard_map/ppermute | solution.py:469
  23.5 50.4 %collective-permute-start.5 = (f32[2,648,128]{2,1,0:T(8,128)S(1)}, f32[2,648,128]{2,1,0:T(8,128)}, u32[]{:S(2)}, u32[]{:S(2)}) collective-permute-start(f32[2,648,128]{2,1,0:T(8,128)S(1)} %shard_map.65.n0), channel_id=1, source_target_pairs={{0,96},{8,104},{16,112},{24,120},{32,0},{40,8},{48,16},{56,24},{64... | collective-permute-start | bytes 1990664 | tf_op jit(solution)/shard_map/ppermute | solution.py:484
  24.3 49.6 %collective-permute-start.4 = (f32[2,648,128]{2,1,0:T(8,128)S(1)}, f32[2,648,128]{2,1,0:T(8,128)}, u32[]{:S(2)}, u32[]{:S(2)}) collective-permute-start(f32[2,648,128]{2,1,0:T(8,128)S(1)} %shard_map.65.n0), channel_id=1, source_target_pairs={{0,64},{8,72},{16,80},{24,88},{32,96},{40,104},{48,112},{56,120},{... | collective-permute-start | bytes 1990664 | tf_op jit(solution)/shard_map/ppermute | solution.py:484
  24.9 49.0 %collective-permute-start.3 = (f32[2,648,128]{2,1,0:T(8,128)S(1)}, f32[2,648,128]{2,1,0:T(8,128)}, u32[]{:S(2)}, u32[]{:S(2)}) collective-permute-start(f32[2,648,128]{2,1,0:T(8,128)S(1)} %shard_map.65.n0), channel_id=1, source_target_pairs={{0,32},{8,40},{16,48},{24,56},{32,64},{40,72},{48,80},{56,88},{64,... | collective-permute-start | bytes 1990664 | tf_op jit(solution)/shard_map/ppermute | solution.py:484
  73.9 2.2 %collective-permute-start.6 = (f32[2,648,128]{2,1,0:T(8,128)S(1)}, f32[2,648,128]{2,1,0:T(8,128)S(1)}, u32[]{:S(2)}, u32[]{:S(2)}) collective-permute-start(f32[2,648,128]{2,1,0:T(8,128)S(1)} %shard_map.65.n0), channel_id=1, source_target_pairs={{0,8},{8,0},{16,24},{24,16},{32,40},{40,32},{48,56},{56,48},{64,72... | collective-permute-start | bytes 1990664 | tf_op jit(solution)/shard_map/ppermute | solution.py:511
  74.3 3.0 %collective-permute-start.7 = (f32[2,648,128]{2,1,0:T(8,128)}, f32[2,648,128]{2,1,0:T(8,128)S(1)}, u32[]{:S(2)}, u32[]{:S(2)}) collective-permute-start(f32[2,648,128]{2,1,0:T(8,128)} %collective-permute-done.3.n1), channel_id=1, source_target_pairs={{0,8},{8,0},{16,24},{24,16},{32,40},{40,32},{48,56},{56,48},{64,72... | collective-permute-start | bytes 1990664 | tf_op jit(solution)/shard_map/ppermute | solution.py:511
  74.5 3.7 %collective-permute-start.8 = (f32[2,648,128]{2,1,0:T(8,128)}, f32[2,648,128]{2,1,0:T(8,128)S(1)}, u32[]{:S(2)}, u32[]{:S(2)}) collective-permute-start(f32[2,648,128]{2,1,0:T(8,128)} %collective-permute-done.4.n2), channel_id=1, source_target_pairs={{0,8},{8,0},{16,24},{24,16},{32,40},{40,32},{48,56},{56,48},{64,72... | collective-permute-start | bytes 1990664 | tf_op jit(solution)/shard_map/ppermute | solution.py:511
  74.8 4.4 %collective-permute-start.9 = (f32[2,648,128]{2,1,0:T(8,128)}, f32[2,648,128]{2,1,0:T(8,128)S(1)}, u32[]{:S(2)}, u32[]{:S(2)}) collective-permute-start(f32[2,648,128]{2,1,0:T(8,128)} %collective-permute-done.5.n3), channel_id=1, source_target_pairs={{0,8},{8,0},{16,24},{24,16},{32,40},{40,32},{48,56},{56,48},{64,72... | collective-permute-start | bytes 1990664 | tf_op jit(solution)/shard_map/ppermute | solution.py:511
  79.2 31.5 %copy-start = (f32[4,9,4,1440]{3,2,1,0:T(4,128)S(1)}, f32[4,9,4,1440]{3,2,1,0:T(4,128)}, u32[]{:S(2)}) copy-start(f32[4,9,4,1440]{3,2,1,0:T(4,128)} %param.6) | copy-start | bytes 2488324

commit v8 on v7

--- a/solution.py
+++ b/solution.py
@@ -481,6 +481,7 @@
         [v[:, 0, :, :128], v[:, 1, :, :128], v[:, 0, :, 128:], v[:, 1, :, 128:], jnp.zeros((levels, 2, 128 - 2 * rest), F32)],
         axis=-1,
     )
+    south, north, pair, courant = lax.optimization_barrier((south, north, pair, courant))
     shifted = [lax.ppermute(pair, "lat", [(i, (i + 4 * d) % lats) for i in range(lats)]) for d in range(1, 4)]
     other = [(i, i ^ 1) for i in range(lats)]
     dma = pltpu.SemaphoreType.DMA

time: 113 us -> 109 us (0.965)
  Pallas kernels: 74.7 us -> 70.7 us
  waiting for transfers between devices: 11.7 us -> 8.09 us
  starting transfers between devices: 17 us -> 18.5 us
    ppermute x1, waiting for transfers between devices: 3.52 us -> 0.24 us  [body(): lax.ppermute(jnp.concatenate([turned[:3].reshape(3 * levs_here, trac, wid...]
    pallas_call x1, Pallas kernels: 41.1 us -> 38.8 us  [body(): call(functools.partial(forth_kernel, rest, groups), (9, lats, groups, 4,...]
    pallas_call x1, Pallas kernels: 31.5 us -> 29.8 us  [body(): call(functools.partial(back_kernel, rest, groups, order), (4, levs_here,...]
    ppermute x4, starting transfers between devices: 1.1 us -> 2.67 us  [body(): far = [lax.ppermute(x, 'lat', other) for x in [pair] + shifted]]
    unnamed x10 -> x14, local copies, waits for them, and re-layouts: 2.56 us -> 1.61 us
  transfers between devices with their start and end apart: 10 -> 10, of which waited for: 6 -> 6; matrix products, arithmetic and copies ran while one was open for 6% -> 8% of each run, Pallas kernels for 38% -> 38%
where the time goes in v8:
time: 109 us; the launch traced here: 108 us
  Pallas kernels  70.7 us (65%)
  starting transfers between devices  18.5 us (17%)
  waiting for transfers between devices  8.09 us (7%)
  local copies, waits for them, and re-layouts  6.1 us (6%)
  other arithmetic  4.05 us (4%)
    pallas_call x1, Pallas kernels, body(): call(functools.partial(forth_kernel, rest, groups), (9, lats, groups, 4,...  38.8 us
    pallas_call x1, Pallas kernels, body(): call(functools.partial(back_kernel, rest, groups, order), (4, levs_here,...  29.8 us
    ppermute x1, starting transfers between devices, body(): lax.ppermute(jnp.concatenate([turned[:3].reshape(3 * levs_here, trac, wid...  6.03 us
    ppermute x4, waiting for transfers between devices, body(): far = [lax.ppermute(x, 'lat', other) for x in [pair] + shifted]  4.19 us
    ppermute x1, starting transfers between devices, body(): across = lax.ppermute(own, 'lat', [(i, i ^ 2) for i in range(lats)])  3.88 us
    ppermute x3, starting transfers between devices, body(): lax.ppermute(pair, 'lat', [(i, (i + 4 * d) % lats) for i in range(lats)])  3.86 us
    ppermute x1, waiting for transfers between devices, body(): across = lax.ppermute(own, 'lat', [(i, i ^ 2) for i in range(lats)])  3.66 us
    ppermute x4, starting transfers between devices, body(): far = [lax.ppermute(x, 'lat', other) for x in [pair] + shifted]  2.67 us
  transfers between devices with their start and end apart: 10, of which 6 were waited for; matrix products, arithmetic and copies ran while one was open for 8% of the time, Pallas kernels for 38%

profile of v8, /device:TPU:24, one launch (start us, length us, event | category | flops | bytes accessed | tf_op | source)
XLA Modules:
  0.0 107.7 jit_solution(7890190193363984860)
XLA Ops:
  0.0 0.0 slice-start
  0.0 3.9 %collective-permute-start.2 = (f32[288,288]{1,0:T(8,128)}, f32[288,288]{1,0:T(8,128)}, u32[]{:S(2)}, u32[]{:S(2)}) collective-permute-start(f32[288,288]{1,0:T(8,128)} %bitcast.33), channel_id=1, source_target_pairs={{0,16},{8,24},{16,0},{24,8},{32,48},{40,56},{48,32},{56,40},{64,80... | collective-permute-start | bytes 995336 | tf_op jit(solution)/shard_map/ppermute | solution.py:463
  3.9 1.5 %copy.45 = f32[4,9,4,1440]{3,0,1,2:T(4,128)S(1)} copy(f32[4,9,4,1440]{3,2,1,0:T(4,128)} %param.6) | data formatting | bytes 1658880 | tf_op args[0]
  5.4 0.0 copy-start.3
  5.4 1.0 fusion.6
  6.4 0.0 copy-start.1
  6.4 2.0 %collective-permute-start = (f32[3,9,4,1440]{3,2,1,0:T(4,128)}, f32[3,9,4,1440]{3,2,1,0:T(4,128)S(1)}, u32[]{:S(2)}, u32[]{:S(2)}) collective-permute-start(f32[3,9,4,1440]{3,2,1,0:T(4,128)} %get-tuple-element.28), channel_id=1, source_target_pairs={{0,8},{8,16},{16,24},{24,32},{32,40},{40,48},{48,56},{56,64},{64,7... | collective-permute-start | bytes 1866248 | tf_op jit(solution)/shard_map/ppermute | solution.py:467
  8.4 0.0 slice-done
  8.5 1.0 pad_maximum_fusion.1
  9.6 6.0 %collective-permute-start.1 = (f32[30,4,1440]{2,1,0:T(4,128)}, f32[30,4,1440]{2,1,0:T(4,128)S(1)}, u32[]{:S(2)}, u32[]{:S(2)}) collective-permute-start(f32[30,4,1440]{2,1,0:T(4,128)} %pad_maximum_fusion.1), channel_id=1, source_target_pairs={{8,0},{16,8},{24,16},{32,24},{40,32},{48,40},{56,48},{64,56},{72,6... | collective-permute-start | bytes 2073608 | tf_op jit(solution)/shard_map/ppermute | solution.py:469
  15.6 0.0 copy-done.3
  15.6 0.1 copy.21
  15.7 0.1 copy_bitcast_fusion.4
  15.8 0.0 copy-start.4
  15.8 0.0 copy-start.2
  15.8 0.7 copy_bitcast_fusion.2
  16.6 1.3 %concatenate.7.c_ref = f32[72,2,384]{2,1,0:T(2,128)S(1)} concatenate(f32[72,2,128]{2,1,0:T(2,128)S(1)} %get-tuple-element.34, f32[72,2,128]{2,1,0:T(2,128)S(1)} %get-tuple-element.33, f32[72,2,52]{2,1,0:T(2,128)} %get-tuple-element.36, f32[72,2,52]{2,1,0:T(2,128)S(1)} %get-tuple-element.35, f32[72,2,24]{2,1,0:T(2,128)S(1)} %broadcast_in_dim.2), dimensions={2} | concatenate | bytes 442368 | tf_op jit(solution)/shard_map/concatenate | solution.py:480
  17.8 3.7 %collective-permute-done.2 = f32[288,288]{1,0:T(8,128)} collective-permute-done((f32[288,288]{1,0:T(8,128)}, f32[288,288]{1,0:T(8,128)}, u32[]{:S(2)}, u32[]{:S(2)}) %collective-permute-start.2) | collective-permute-done | bytes 331808 | tf_op jit(solution)/shard_map/ppermute | solution.py:463
  21.5 0.0 copy-done.1
  21.5 1.1 %pad_maximum_fusion.m_ref = f32[2,288,288]{2,1,0:T(8,128)S(1)} fusion(f32[1,288,288]{2,1,0:T(8,128)} %bitcast.5, f32[1,288,288]{2,1,0:T(8,128)S(1)} %bitcast.34), kind=kLoop, calls=%fused_computation | loop fusion | flops 165888 | bytes 1327104 | tf_op jit(solution)/shard_map/stack | solution.py:472
  22.6 2.1 %shard_map.64.n0 = f32[2,648,128]{2,1,0:T(8,128)S(1)} custom-call(f32[2,288,288]{2,1,0:T(8,128)S(1)} %pad_maximum_fusion.m_ref), custom_call_target="tpu_custom_call" | custom-call | tf_op jit(solution)/shard_map/pallas_call | solution.py:472
  24.7 0.0 collective-permute-done.south_ref
  24.7 0.2 collective-permute-done.1.north_ref
  24.9 0.7 collective-permute-start.5
  25.7 0.5 collective-permute-start.4
  26.2 2.6 %collective-permute-start.3 = (f32[2,648,128]{2,1,0:T(8,128)S(1)}, f32[2,648,128]{2,1,0:T(8,128)}, u32[]{:S(2)}, u32[]{:S(2)}) collective-permute-start(f32[2,648,128]{2,1,0:T(8,128)S(1)} %shard_map.64.n0), channel_id=1, source_target_pairs={{0,32},{8,40},{16,48},{24,56},{32,64},{40,72},{48,80},{56,88},{64,... | collective-permute-start | bytes 1990664 | tf_op jit(solution)/shard_map/ppermute | solution.py:485
  28.8 0.0 copy-done.4
  28.8 0.1 copy.26
  28.9 0.4 convert_reduce_fusion
  29.4 0.0 copy-done.2
  29.4 1.0 pad_maximum_fusion.2.both_ref
  30.4 38.8 %shard_map.65 = (f32[9,16,8,4,128]{4,3,2,1,0:T(4,128)S(1)}, s32[8,4,256]{2,1,0:T(4,128)S(1)}) custom-call(f32[4,9,4,1440]{3,2,1,0:T(4,128)S(1)} %bitcast.29, f32[3,9,4,1440]{3,2,1,0:T(4,128)S(1)} %collective-permute-done.south_ref, f32[30,4,1440]{2,1,0:T(4,128)S(1)} %collective-permute-done.1.north_ref, f32[2,9,4,1440]{3,2,1,0:T(4,128)S(1)} %pad_maximum_fusion.2.both_ref, ...), custom_call_target="tpu_custom_call" | custom-call | tf_op jit(solution)/shard_map/pallas_call | solution.py:489
  69.3 0.0 collective-permute-done.5.n3
  69.3 0.0 collective-permute-done.4.n2
  69.3 0.0 collective-permute-done.3.n1
  69.3 2.1 %collective-permute-start.6 = (f32[2,648,128]{2,1,0:T(8,128)S(1)}, f32[2,648,128]{2,1,0:T(8,128)S(1)}, u32[]{:S(2)}, u32[]{:S(2)}) collective-permute-start(f32[2,648,128]{2,1,0:T(8,128)S(1)} %shard_map.64.n0), channel_id=1, source_target_pairs={{0,8},{8,0},{16,24},{24,16},{32,40},{40,32},{48,56},{56,48},{64,72... | collective-permute-start | bytes 1990664 | tf_op jit(solution)/shard_map/ppermute | solution.py:512
  71.4 0.1 collective-permute-start.7
  71.5 0.4 collective-permute-start.8
  71.9 0.1 collective-permute-start.9
  72.0 1.1 %collective-permute-done.6.f0 = f32[2,648,128]{2,1,0:T(8,128)S(1)} collective-permute-done((f32[2,648,128]{2,1,0:T(8,128)S(1)}, f32[2,648,128]{2,1,0:T(8,128)S(1)}, u32[]{:S(2)}, u32[]{:S(2)}) %collective-permute-start.6) | collective-permute-done | bytes 663584 | tf_op jit(solution)/shard_map/ppermute | solution.py:512
  73.1 1.1 %collective-permute-done.7.f1 = f32[2,648,128]{2,1,0:T(8,128)S(1)} collective-permute-done((f32[2,648,128]{2,1,0:T(8,128)}, f32[2,648,128]{2,1,0:T(8,128)S(1)}, u32[]{:S(2)}, u32[]{:S(2)}) %collective-permute-start.7) | collective-permute-done | bytes 663584 | tf_op jit(solution)/shard_map/ppermute | solution.py:512
  74.3 0.9 collective-permute-done.8.f2
  75.2 0.9 collective-permute-done.9.f3
  76.2 0.0 copy-start
  76.2 29.8 %shard_map.66 = f32[4,9,4,1440]{3,2,1,0:T(4,128)S(1)} custom-call(f32[9,16,8,4,128]{4,3,2,1,0:T(4,128)S(1)} %get-tuple-element.21.r_ref, f32[2,648,128]{2,1,0:T(8,128)S(1)} %shard_map.64.n0, f32[2,648,128]{2,1,0:T(8,128)} %collective-permute-done.3.n1, f32[2,648,128]{2,1,0:T(8,128)} %collective-permute-done.4.n2, f32[2,648,128]{2,1,0:T(8,128)} %collective-permute-done.5.n3, ...), custom_call_target="tpu_custom_call" | custom-call | tf_op jit(solution)/shard_map/pallas_call | solution.py:513
  106.0 0.0 copy-done
  106.0 0.4 bitcast_subtract_fusion
  106.4 1.3 %copy.28 = f32[4,9,4,1440]{3,2,1,0:T(4,128)} copy(f32[4,9,4,1440]{3,0,1,2:T(4,128)S(1)} %bitcast_subtract_fusion) | data formatting | bytes 1658880 | tf_op jit(solution)/shard_map/sub | solution.py:536
  (10 shorter events, 0.1 us)
Async XLA Ops:
  0.0 8.4 %slice-start = ((f32[9,4,1440]{2,1,0:T(4,128)}), f32[9,1,1440]{2,1,0:T(1,128)S(1)}, s32[]{:S(2)}) async-start(f32[9,4,1440]{2,1,0:T(4,128)} %param.8), calls=%async_computation | async-start | bytes 110592 | tf_op jit(solution)/shard_map/slice | solution.py:468
  0.0 21.5 %collective-permute-start.2 = (f32[288,288]{1,0:T(8,128)}, f32[288,288]{1,0:T(8,128)}, u32[]{:S(2)}, u32[]{:S(2)}) collective-permute-start(f32[288,288]{1,0:T(8,128)} %bitcast.33), channel_id=1, source_target_pairs={{0,16},{8,24},{16,0},{24,8},{32,48},{40,56},{48,32},{56,40},{64,80... | collective-permute-start | bytes 995336 | tf_op jit(solution)/shard_map/ppermute | solution.py:463
  5.4 10.2 %copy-start.3 = (f32[72,4,180]{2,1,0:T(4,128)S(1)}, f32[72,4,180]{2,1,0:T(4,128)}, u32[]{:S(2)}) copy-start(f32[72,4,180]{2,1,0:T(4,128)} %param.9) | copy-start | bytes 622084
  6.4 15.1 %copy-start.1 = (f32[1,1,288,288]{3,2,1,0:T(8,128)S(1)}, f32[1,1,288,288]{3,2,1,0:T(8,128)}, u32[]{:S(2)}) copy-start(f32[1,1,288,288]{3,2,1,0:T(8,128)} %param.11) | copy-start | bytes 995332
  6.4 18.3 %collective-permute-start = (f32[3,9,4,1440]{3,2,1,0:T(4,128)}, f32[3,9,4,1440]{3,2,1,0:T(4,128)S(1)}, u32[]{:S(2)}, u32[]{:S(2)}) collective-permute-start(f32[3,9,4,1440]{3,2,1,0:T(4,128)} %get-tuple-element.28), channel_id=1, source_target_pairs={{0,8},{8,16},{16,24},{24,32},{32,40},{40,48},{48,56},{56,64},{64,7... | collective-permute-start | bytes 1866248 | tf_op jit(solution)/shard_map/ppermute | solution.py:467
  9.6 15.4 %collective-permute-start.1 = (f32[30,4,1440]{2,1,0:T(4,128)}, f32[30,4,1440]{2,1,0:T(4,128)S(1)}, u32[]{:S(2)}, u32[]{:S(2)}) collective-permute-start(f32[30,4,1440]{2,1,0:T(4,128)} %pad_maximum_fusion.1), channel_id=1, source_target_pairs={{8,0},{16,8},{24,16},{32,24},{40,32},{48,40},{56,48},{64,56},{72,6... | collective-permute-start | bytes 2073608 | tf_op jit(solution)/shard_map/ppermute | solution.py:469
  15.8 13.0 %copy-start.4 = (s32[4,180,1]{1,2,0:T(1,128)S(1)}, s32[4,180,1]{1,2,0:T(1,128)}, u32[]{:S(2)}) copy-start(s32[4,180,1]{1,2,0:T(1,128)} %param.10) | copy-start | bytes 8644
  15.8 13.6 %copy-start.2 = (f32[9,4,1440]{2,1,0:T(4,128)S(1)}, f32[9,4,1440]{2,1,0:T(4,128)}, u32[]{:S(2)}) copy-start(f32[9,4,1440]{2,1,0:T(4,128)} %param.8) | copy-start | bytes 622084
  24.9 44.4 %collective-permute-start.5 = (f32[2,648,128]{2,1,0:T(8,128)S(1)}, f32[2,648,128]{2,1,0:T(8,128)}, u32[]{:S(2)}, u32[]{:S(2)}) collective-permute-start(f32[2,648,128]{2,1,0:T(8,128)S(1)} %shard_map.64.n0), channel_id=1, source_target_pairs={{0,96},{8,104},{16,112},{24,120},{32,0},{40,8},{48,16},{56,24},{64... | collective-permute-start | bytes 1990664 | tf_op jit(solution)/shard_map/ppermute | solution.py:485
  25.7 43.6 %collective-permute-start.4 = (f32[2,648,128]{2,1,0:T(8,128)S(1)}, f32[2,648,128]{2,1,0:T(8,128)}, u32[]{:S(2)}, u32[]{:S(2)}) collective-permute-start(f32[2,648,128]{2,1,0:T(8,128)S(1)} %shard_map.64.n0), channel_id=1, source_target_pairs={{0,64},{8,72},{16,80},{24,88},{32,96},{40,104},{48,112},{56,120},{... | collective-permute-start | bytes 1990664 | tf_op jit(solution)/shard_map/ppermute | solution.py:485
  26.2 43.1 %collective-permute-start.3 = (f32[2,648,128]{2,1,0:T(8,128)S(1)}, f32[2,648,128]{2,1,0:T(8,128)}, u32[]{:S(2)}, u32[]{:S(2)}) collective-permute-start(f32[2,648,128]{2,1,0:T(8,128)S(1)} %shard_map.64.n0), channel_id=1, source_target_pairs={{0,32},{8,40},{16,48},{24,56},{32,64},{40,72},{48,80},{56,88},{64,... | collective-permute-start | bytes 1990664 | tf_op jit(solution)/shard_map/ppermute | solution.py:485
  69.3 3.8 %collective-permute-start.6 = (f32[2,648,128]{2,1,0:T(8,128)S(1)}, f32[2,648,128]{2,1,0:T(8,128)S(1)}, u32[]{:S(2)}, u32[]{:S(2)}) collective-permute-start(f32[2,648,128]{2,1,0:T(8,128)S(1)} %shard_map.64.n0), channel_id=1, source_target_pairs={{0,8},{8,0},{16,24},{24,16},{32,40},{40,32},{48,56},{56,48},{64,72... | collective-permute-start | bytes 1990664 | tf_op jit(solution)/shard_map/ppermute | solution.py:512
  71.4 2.9 %collective-permute-start.7 = (f32[2,648,128]{2,1,0:T(8,128)}, f32[2,648,128]{2,1,0:T(8,128)S(1)}, u32[]{:S(2)}, u32[]{:S(2)}) collective-permute-start(f32[2,648,128]{2,1,0:T(8,128)} %collective-permute-done.3.n1), channel_id=1, source_target_pairs={{0,8},{8,0},{16,24},{24,16},{32,40},{40,32},{48,56},{56,48},{64,72... | collective-permute-start | bytes 1990664 | tf_op jit(solution)/shard_map/ppermute | solution.py:512
  71.5 3.8 %collective-permute-start.8 = (f32[2,648,128]{2,1,0:T(8,128)}, f32[2,648,128]{2,1,0:T(8,128)S(1)}, u32[]{:S(2)}, u32[]{:S(2)}) collective-permute-start(f32[2,648,128]{2,1,0:T(8,128)} %collective-permute-done.4.n2), channel_id=1, source_target_pairs={{0,8},{8,0},{16,24},{24,16},{32,40},{40,32},{48,56},{56,48},{64,72... | collective-permute-start | bytes 1990664 | tf_op jit(solution)/shard_map/ppermute | solution.py:512
  71.9 4.3 %collective-permute-start.9 = (f32[2,648,128]{2,1,0:T(8,128)}, f32[2,648,128]{2,1,0:T(8,128)S(1)}, u32[]{:S(2)}, u32[]{:S(2)}) collective-permute-start(f32[2,648,128]{2,1,0:T(8,128)} %collective-permute-done.5.n3), channel_id=1, source_target_pairs={{0,8},{8,0},{16,24},{24,16},{32,40},{40,32},{48,56},{56,48},{64,72... | collective-permute-start | bytes 1990664 | tf_op jit(solution)/shard_map/ppermute | solution.py:512
  76.2 29.8 %copy-start = (f32[4,9,4,1440]{3,2,1,0:T(4,128)S(1)}, f32[4,9,4,1440]{3,2,1,0:T(4,128)}, u32[]{:S(2)}) copy-start(f32[4,9,4,1440]{3,2,1,0:T(4,128)} %param.6) | copy-start | bytes 2488324

commit v9 on v7

--- a/solution.py
+++ b/solution.py
@@ -241,8 +241,10 @@
         one = selector(slot_ref[g, r : r + 1, :])
         out = dot(jnp.concatenate([hi, lo], axis=1), jnp.concatenate([one, one], axis=0))
         at = slice(lon * g, lon * g + lon)
-        o_ref[r, 0:8, :, at] = out[0:32, :lon].reshape(8, 4, lon)
-        o_ref[r, 8, :, at] = out[32 + 4 * r : 36 + 4 * r, :lon]
+        for t in range(4):
+            for k in range(8):
+                o_ref[t, k, r : r + 1, at] = out[4 * k + t : 4 * k + t + 1, :lon]
+            o_ref[t, 8, r : r + 1, at] = out[32 + 4 * r + t : 33 + 4 * r + t, :lon]
 
 
 PIECES = ((0, 0, 2), (0, 1, 2), (1, None, 4), (2, None, 4), (3, None, 4))
@@ -481,6 +483,8 @@
         [v[:, 0, :, :128], v[:, 1, :, :128], v[:, 0, :, 128:], v[:, 1, :, 128:], jnp.zeros((levels, 2, 128 - 2 * rest), F32)],
         axis=-1,
     )
+    both = jnp.stack([zonal, meridional])
+    south, north, pair, courant, both = lax.optimization_barrier((south, north, pair, courant, both))
     shifted = [lax.ppermute(pair, "lat", [(i, (i + 4 * d) % lats) for i in range(lats)]) for d in range(1, 4)]
     other = [(i, i ^ 1) for i in range(lats)]
     dma = pltpu.SemaphoreType.DMA
@@ -506,12 +510,12 @@
         limit=24,
         collective_id=0,
         has_side_effects=True,
-    )(turned, south, north, jnp.stack([zonal, meridional]), courant, slots)
+    )(turned, south, north, both, courant, slots)
     received, pair, shifted = lax.optimization_barrier((received, pair, shifted))
     far = [lax.ppermute(x, "lat", other) for x in [pair] + shifted]
     whole = call(
         functools.partial(back_kernel, rest, groups, order),
-        (4, levs_here, trac, width),
+        (trac, levs_here, rows, width),
         10,
         [
             pltpu.VMEM((9, lats, groups, 4, 128), F32),
@@ -532,7 +536,7 @@
         collective_id=1,
         has_side_effects=True,
     )(received, pair, *shifted, *far, all_slots)
-    return jnp.transpose(whole, (2, 1, 0, 3)) - tracers
+    return whole - tracers
 
 
 def solution(mesh):

time: 113 us -> 109 us (0.965)
  Pallas kernels: 74.7 us -> 72 us
  waiting for transfers between devices: 11.7 us -> 9.34 us
  local copies, waits for them, and re-layouts: 5.71 us -> 3.49 us
  starting transfers between devices: 17 us -> 18.6 us
    ppermute x1, waiting for transfers between devices: 3.52 us -> 0.3 us  [body(): lax.ppermute(jnp.concatenate([turned[:3].reshape(3 * levs_here, trac, wid...]
    ppermute x4, starting transfers between devices: 1.1 us -> 2.77 us  [body(): far = [lax.ppermute(x, 'lat', other) for x in [pair] + shifted]]
    pallas_call x1, Pallas kernels: 41.1 us -> 39.7 us  [body(): call(functools.partial(forth_kernel, rest, groups), (9, lats, groups, 4,...]
    pallas_call x1, Pallas kernels: 31.5 us -> 30.2 us  [body(): call(functools.partial(back_kernel, rest, groups, order), (trac, levs_her...]
    sub x1 -> x0, local copies, waits for them, and re-layouts: 1.25 us -> none  [body(): return jnp.transpose(whole, (2, 1, 0, 3)) - tracers]
    unnamed x10 -> x16, local copies, waits for them, and re-layouts: 2.56 us -> 1.61 us
  transfers between devices with their start and end apart: 10 -> 10, of which waited for: 6 -> 6; matrix products, arithmetic and copies ran while one was open for 6% -> 6% of each run, Pallas kernels for 38% -> 39%
where the time goes in v9:
time: 109 us; the launch traced here: 108 us
  Pallas kernels  72 us (66%)
  starting transfers between devices  18.6 us (17%)
  waiting for transfers between devices  9.34 us (9%)
  other arithmetic  3.8 us (3%)
  local copies, waits for them, and re-layouts  3.49 us (3%)
    pallas_call x1, Pallas kernels, body(): call(functools.partial(forth_kernel, rest, groups), (9, lats, groups, 4,...  39.7 us
    pallas_call x1, Pallas kernels, body(): call(functools.partial(back_kernel, rest, groups, order), (trac, levs_her...  30.2 us
    ppermute x1, starting transfers between devices, body(): lax.ppermute(jnp.concatenate([turned[:3].reshape(3 * levs_here, trac, wid...  6.03 us
    ppermute x1, waiting for transfers between devices, body(): across = lax.ppermute(own, 'lat', [(i, i ^ 2) for i in range(lats)])  4.85 us
    ppermute x4, waiting for transfers between devices, body(): far = [lax.ppermute(x, 'lat', other) for x in [pair] + shifted]  4.19 us
    ppermute x1, starting transfers between devices, body(): across = lax.ppermute(own, 'lat', [(i, i ^ 2) for i in range(lats)])  3.88 us
    ppermute x3, starting transfers between devices, body(): lax.ppermute(pair, 'lat', [(i, (i + 4 * d) % lats) for i in range(lats)])  3.86 us
    ppermute x4, starting transfers between devices, body(): far = [lax.ppermute(x, 'lat', other) for x in [pair] + shifted]  2.77 us
  transfers between devices with their start and end apart: 10, of which 6 were waited for; matrix products, arithmetic and copies ran while one was open for 6% of the time, Pallas kernels for 39%

profile of v9, /device:TPU:24, one launch (start us, length us, event | category | flops | bytes accessed | tf_op | source)
XLA Modules:
  0.0 107.5 jit_solution(423535533083229876)
XLA Ops:
  0.0 0.0 slice-start
  0.0 3.9 %collective-permute-start.2 = (f32[288,288]{1,0:T(8,128)}, f32[288,288]{1,0:T(8,128)}, u32[]{:S(2)}, u32[]{:S(2)}) collective-permute-start(f32[288,288]{1,0:T(8,128)} %bitcast.31), channel_id=1, source_target_pairs={{0,16},{8,24},{16,0},{24,8},{32,48},{40,56},{48,32},{56,40},{64,80... | collective-permute-start | bytes 995336 | tf_op jit(solution)/shard_map/ppermute | solution.py:465
  3.9 1.5 %copy.38 = f32[4,9,4,1440]{3,0,1,2:T(4,128)S(1)} copy(f32[4,9,4,1440]{3,2,1,0:T(4,128)} %param.6) | data formatting | bytes 1658880 | tf_op args[0]
  5.4 0.0 copy-start.3
  5.4 1.0 fusion.6
  6.4 0.0 copy-start.2
  6.4 0.0 copy-start.4
  6.4 2.0 %collective-permute-start = (f32[3,9,4,1440]{3,2,1,0:T(4,128)}, f32[3,9,4,1440]{3,2,1,0:T(4,128)}, u32[]{:S(2)}, u32[]{:S(2)}) collective-permute-start(f32[3,9,4,1440]{3,2,1,0:T(4,128)} %get-tuple-element.30), channel_id=1, source_target_pairs={{0,8},{8,16},{16,24},{24,32},{32,40},{40,48},{48,56},{56,64},{64,7... | collective-permute-start | bytes 1866248 | tf_op jit(solution)/shard_map/ppermute | solution.py:469
  8.4 0.0 slice-done
  8.5 0.0 copy-start.1
  8.5 1.0 pad_maximum_fusion.1
  9.6 6.0 %collective-permute-start.1 = (f32[30,4,1440]{2,1,0:T(4,128)}, f32[30,4,1440]{2,1,0:T(4,128)S(1)}, u32[]{:S(2)}, u32[]{:S(2)}) collective-permute-start(f32[30,4,1440]{2,1,0:T(4,128)} %pad_maximum_fusion.1), channel_id=1, source_target_pairs={{8,0},{16,8},{24,16},{32,24},{40,32},{48,40},{56,48},{64,56},{72,6... | collective-permute-start | bytes 2073608 | tf_op jit(solution)/shard_map/ppermute | solution.py:471
  15.6 0.0 copy-done.3
  15.6 0.1 copy.17
  15.7 0.1 copy_bitcast_fusion.4
  15.8 0.1 copy_bitcast_fusion.2
  15.9 0.0 copy-start.5
  15.9 0.5 concatenate.7.c_ref
  16.5 0.0 copy-done.2
  16.5 0.0 copy-done.4
  16.5 0.1 pad_maximum_fusion.2.both_ref
  16.6 4.9 %collective-permute-done.2 = f32[288,288]{1,0:T(8,128)} collective-permute-done((f32[288,288]{1,0:T(8,128)}, f32[288,288]{1,0:T(8,128)}, u32[]{:S(2)}, u32[]{:S(2)}) %collective-permute-start.2) | collective-permute-done | bytes 331808 | tf_op jit(solution)/shard_map/ppermute | solution.py:465
  21.5 0.0 copy-done.1
  21.5 1.1 pad_maximum_fusion.m_ref
  22.5 2.1 %shard_map.64.n0 = f32[2,648,128]{2,1,0:T(8,128)S(1)} custom-call(f32[2,288,288]{2,1,0:T(8,128)S(1)} %pad_maximum_fusion.m_ref), custom_call_target="tpu_custom_call" | custom-call | tf_op jit(solution)/shard_map/pallas_call | solution.py:474
  24.6 0.0 collective-permute-done.south_ref
  24.6 0.3 collective-permute-done.1.north_ref
  24.9 0.7 collective-permute-start.5
  25.7 0.5 collective-permute-start.4
  26.2 2.6 %collective-permute-start.3 = (f32[2,648,128]{2,1,0:T(8,128)S(1)}, f32[2,648,128]{2,1,0:T(8,128)}, u32[]{:S(2)}, u32[]{:S(2)}) collective-permute-start(f32[2,648,128]{2,1,0:T(8,128)S(1)} %shard_map.64.n0), channel_id=1, source_target_pairs={{0,32},{8,40},{16,48},{24,56},{32,64},{40,72},{48,80},{56,88},{64,... | collective-permute-start | bytes 1990664 | tf_op jit(solution)/shard_map/ppermute | solution.py:488
  28.8 0.0 copy-done.5
  28.8 0.1 copy.22
  29.0 0.4 convert_reduce_fusion
  29.4 39.7 %shard_map.65 = (f32[9,16,8,4,128]{4,3,2,1,0:T(4,128)S(1)}, s32[8,4,256]{2,1,0:T(4,128)S(1)}) custom-call(f32[4,9,4,1440]{3,2,1,0:T(4,128)S(1)} %bitcast.27, f32[3,9,4,1440]{3,2,1,0:T(4,128)} %collective-permute-done.south_ref, f32[30,4,1440]{2,1,0:T(4,128)S(1)} %collective-permute-done.1.north_ref, f32[2,9,4,1440]{3,2,1,0:T(4,128)S(1)} %pad_maximum_fusion.2.both_ref, ...), custom_call_target="tpu_custom_call" | custom-call | tf_op jit(solution)/shard_map/pallas_call | solution.py:492
  69.1 0.0 collective-permute-done.5.n3
  69.1 0.0 collective-permute-done.4.n2
  69.1 0.0 collective-permute-done.3.n1
  69.1 2.2 %collective-permute-start.6 = (f32[2,648,128]{2,1,0:T(8,128)S(1)}, f32[2,648,128]{2,1,0:T(8,128)S(1)}, u32[]{:S(2)}, u32[]{:S(2)}) collective-permute-start(f32[2,648,128]{2,1,0:T(8,128)S(1)} %shard_map.64.n0), channel_id=1, source_target_pairs={{0,8},{8,0},{16,24},{24,16},{32,40},{40,32},{48,56},{56,48},{64,72... | collective-permute-start | bytes 1990664 | tf_op jit(solution)/shard_map/ppermute | solution.py:515
  71.3 0.1 collective-permute-start.7
  71.4 0.4 collective-permute-start.8
  71.8 0.1 collective-permute-start.9
  71.9 1.1 %collective-permute-done.6.f0 = f32[2,648,128]{2,1,0:T(8,128)S(1)} collective-permute-done((f32[2,648,128]{2,1,0:T(8,128)S(1)}, f32[2,648,128]{2,1,0:T(8,128)S(1)}, u32[]{:S(2)}, u32[]{:S(2)}) %collective-permute-start.6) | collective-permute-done | bytes 663584 | tf_op jit(solution)/shard_map/ppermute | solution.py:515
  73.1 1.1 %collective-permute-done.7.f1 = f32[2,648,128]{2,1,0:T(8,128)S(1)} collective-permute-done((f32[2,648,128]{2,1,0:T(8,128)}, f32[2,648,128]{2,1,0:T(8,128)S(1)}, u32[]{:S(2)}, u32[]{:S(2)}) %collective-permute-start.7) | collective-permute-done | bytes 663584 | tf_op jit(solution)/shard_map/ppermute | solution.py:515
  74.2 0.9 collective-permute-done.8.f2
  75.2 0.9 collective-permute-done.9.f3
  76.1 30.2 %shard_map.66 = f32[4,9,4,1440]{3,2,1,0:T(4,128)S(1)} custom-call(f32[9,16,8,4,128]{4,3,2,1,0:T(4,128)S(1)} %get-tuple-element.23.r_ref, f32[2,648,128]{2,1,0:T(8,128)S(1)} %shard_map.64.n0, f32[2,648,128]{2,1,0:T(8,128)} %collective-permute-done.3.n1, f32[2,648,128]{2,1,0:T(8,128)} %collective-permute-done.4.n2, f32[2,648,128]{2,1,0:T(8,128)} %collective-permute-done.5.n3, ...), custom_call_target="tpu_custom_call" | custom-call | tf_op jit(solution)/shard_map/pallas_call | solution.py:516
  106.4 0.0 copy-done
  106.4 1.1 %sub.10 = f32[4,9,4,1440]{3,2,1,0:T(4,128)} subtract(f32[4,9,4,1440]{3,2,1,0:T(4,128)S(1)} %shard_map.66, f32[4,9,4,1440]{3,2,1,0:T(4,128)S(1)} %copy-done) | non-fusion elementwise | flops 207360 | bytes 2488320 | tf_op jit(solution)/shard_map/sub | solution.py:539
  (11 shorter events, 0.1 us)
Async XLA Ops:
  0.0 8.4 %slice-start = ((f32[9,4,1440]{2,1,0:T(4,128)}), f32[9,1,1440]{2,1,0:T(1,128)S(1)}, s32[]{:S(2)}) async-start(f32[9,4,1440]{2,1,0:T(4,128)} %param.8), calls=%async_computation | async-start | bytes 110592 | tf_op jit(solution)/shard_map/slice | solution.py:470
  0.0 21.5 %collective-permute-start.2 = (f32[288,288]{1,0:T(8,128)}, f32[288,288]{1,0:T(8,128)}, u32[]{:S(2)}, u32[]{:S(2)}) collective-permute-start(f32[288,288]{1,0:T(8,128)} %bitcast.31), channel_id=1, source_target_pairs={{0,16},{8,24},{16,0},{24,8},{32,48},{40,56},{48,32},{56,40},{64,80... | collective-permute-start | bytes 995336 | tf_op jit(solution)/shard_map/ppermute | solution.py:465
  5.4 10.2 %copy-start.3 = (f32[72,4,180]{2,1,0:T(4,128)S(1)}, f32[72,4,180]{2,1,0:T(4,128)}, u32[]{:S(2)}) copy-start(f32[72,4,180]{2,1,0:T(4,128)} %param.9) | copy-start | bytes 622084
  6.4 10.1 %copy-start.2 = (f32[9,4,1440]{2,1,0:T(4,128)S(1)}, f32[9,4,1440]{2,1,0:T(4,128)}, u32[]{:S(2)}) copy-start(f32[9,4,1440]{2,1,0:T(4,128)} %param.8) | copy-start | bytes 622084
  6.4 10.1 %copy-start.4 = (f32[9,4,1440]{2,1,0:T(4,128)S(1)}, f32[9,4,1440]{2,1,0:T(4,128)}, u32[]{:S(2)}) copy-start(f32[9,4,1440]{2,1,0:T(4,128)} %param.7) | copy-start | bytes 622084
  6.4 18.2 %collective-permute-start = (f32[3,9,4,1440]{3,2,1,0:T(4,128)}, f32[3,9,4,1440]{3,2,1,0:T(4,128)}, u32[]{:S(2)}, u32[]{:S(2)}) collective-permute-start(f32[3,9,4,1440]{3,2,1,0:T(4,128)} %get-tuple-element.30), channel_id=1, source_target_pairs={{0,8},{8,16},{16,24},{24,32},{32,40},{40,48},{48,56},{56,64},{64,7... | collective-permute-start | bytes 1866248 | tf_op jit(solution)/shard_map/ppermute | solution.py:469
  8.5 12.9 %copy-start.1 = (f32[1,1,288,288]{3,2,1,0:T(8,128)S(1)}, f32[1,1,288,288]{3,2,1,0:T(8,128)}, u32[]{:S(2)}) copy-start(f32[1,1,288,288]{3,2,1,0:T(8,128)} %param.11) | copy-start | bytes 995332
  9.6 15.4 %collective-permute-start.1 = (f32[30,4,1440]{2,1,0:T(4,128)}, f32[30,4,1440]{2,1,0:T(4,128)S(1)}, u32[]{:S(2)}, u32[]{:S(2)}) collective-permute-start(f32[30,4,1440]{2,1,0:T(4,128)} %pad_maximum_fusion.1), channel_id=1, source_target_pairs={{8,0},{16,8},{24,16},{32,24},{40,32},{48,40},{56,48},{64,56},{72,6... | collective-permute-start | bytes 2073608 | tf_op jit(solution)/shard_map/ppermute | solution.py:471
  15.9 12.9 %copy-start.5 = (s32[4,180,1]{1,2,0:T(1,128)S(1)}, s32[4,180,1]{1,2,0:T(1,128)}, u32[]{:S(2)}) copy-start(s32[4,180,1]{1,2,0:T(1,128)} %param.10) | copy-start | bytes 8644
  24.9 44.2 %collective-permute-start.5 = (f32[2,648,128]{2,1,0:T(8,128)S(1)}, f32[2,648,128]{2,1,0:T(8,128)}, u32[]{:S(2)}, u32[]{:S(2)}) collective-permute-start(f32[2,648,128]{2,1,0:T(8,128)S(1)} %shard_map.64.n0), channel_id=1, source_target_pairs={{0,96},{8,104},{16,112},{24,120},{32,0},{40,8},{48,16},{56,24},{64... | collective-permute-start | bytes 1990664 | tf_op jit(solution)/shard_map/ppermute | solution.py:488
  25.7 43.5 %collective-permute-start.4 = (f32[2,648,128]{2,1,0:T(8,128)S(1)}, f32[2,648,128]{2,1,0:T(8,128)}, u32[]{:S(2)}, u32[]{:S(2)}) collective-permute-start(f32[2,648,128]{2,1,0:T(8,128)S(1)} %shard_map.64.n0), channel_id=1, source_target_pairs={{0,64},{8,72},{16,80},{24,88},{32,96},{40,104},{48,112},{56,120},{... | collective-permute-start | bytes 1990664 | tf_op jit(solution)/shard_map/ppermute | solution.py:488
  26.2 43.0 %collective-permute-start.3 = (f32[2,648,128]{2,1,0:T(8,128)S(1)}, f32[2,648,128]{2,1,0:T(8,128)}, u32[]{:S(2)}, u32[]{:S(2)}) collective-permute-start(f32[2,648,128]{2,1,0:T(8,128)S(1)} %shard_map.64.n0), channel_id=1, source_target_pairs={{0,32},{8,40},{16,48},{24,56},{32,64},{40,72},{48,80},{56,88},{64,... | collective-permute-start | bytes 1990664 | tf_op jit(solution)/shard_map/ppermute | solution.py:488
  69.1 3.9 %collective-permute-start.6 = (f32[2,648,128]{2,1,0:T(8,128)S(1)}, f32[2,648,128]{2,1,0:T(8,128)S(1)}, u32[]{:S(2)}, u32[]{:S(2)}) collective-permute-start(f32[2,648,128]{2,1,0:T(8,128)S(1)} %shard_map.64.n0), channel_id=1, source_target_pairs={{0,8},{8,0},{16,24},{24,16},{32,40},{40,32},{48,56},{56,48},{64,72... | collective-permute-start | bytes 1990664 | tf_op jit(solution)/shard_map/ppermute | solution.py:515
  71.3 2.9 %collective-permute-start.7 = (f32[2,648,128]{2,1,0:T(8,128)}, f32[2,648,128]{2,1,0:T(8,128)S(1)}, u32[]{:S(2)}, u32[]{:S(2)}) collective-permute-start(f32[2,648,128]{2,1,0:T(8,128)} %collective-permute-done.3.n1), channel_id=1, source_target_pairs={{0,8},{8,0},{16,24},{24,16},{32,40},{40,32},{48,56},{56,48},{64,72... | collective-permute-start | bytes 1990664 | tf_op jit(solution)/shard_map/ppermute | solution.py:515
  71.4 3.8 %collective-permute-start.8 = (f32[2,648,128]{2,1,0:T(8,128)}, f32[2,648,128]{2,1,0:T(8,128)S(1)}, u32[]{:S(2)}, u32[]{:S(2)}) collective-permute-start(f32[2,648,128]{2,1,0:T(8,128)} %collective-permute-done.4.n2), channel_id=1, source_target_pairs={{0,8},{8,0},{16,24},{24,16},{32,40},{40,32},{48,56},{56,48},{64,72... | collective-permute-start | bytes 1990664 | tf_op jit(solution)/shard_map/ppermute | solution.py:515
  71.8 4.3 %collective-permute-start.9 = (f32[2,648,128]{2,1,0:T(8,128)}, f32[2,648,128]{2,1,0:T(8,128)S(1)}, u32[]{:S(2)}, u32[]{:S(2)}) collective-permute-start(f32[2,648,128]{2,1,0:T(8,128)} %collective-permute-done.5.n3), channel_id=1, source_target_pairs={{0,8},{8,0},{16,24},{24,16},{32,40},{40,32},{48,56},{56,48},{64,72... | collective-permute-start | bytes 1990664 | tf_op jit(solution)/shard_map/ppermute | solution.py:515
  76.1 30.3 %copy-start = (f32[4,9,4,1440]{3,2,1,0:T(4,128)S(1)}, f32[4,9,4,1440]{3,2,1,0:T(4,128)}, u32[]{:S(2)}) copy-start(f32[4,9,4,1440]{3,2,1,0:T(4,128)} %param.6) | copy-start | bytes 2488324

commit v10 on v9

--- a/solution.py
+++ b/solution.py
@@ -247,7 +247,7 @@
             o_ref[t, 8, r : r + 1, at] = out[32 + 4 * r + t : 33 + 4 * r + t, :lon]
 
 
-PIECES = ((0, 0, 2), (0, 1, 2), (1, None, 4), (2, None, 4), (3, None, 4))
+PIECES = ((0, 0, 0, 1), (0, 0, 1, 1), (0, 1, None, 2), (1, None, None, 4), (2, None, None, 4), (3, None, None, 4))
 
 
 def greet(lat, lev, levs):
@@ -339,12 +339,14 @@
         fetches[n].start()
 
     def begin(n):
-        d, turn, _ = PIECES[n]
+        d, turn, core, _ = PIECES[n]
         at = lax.rem(lat // 4 - d + 4, 4) * 4
-        return at if turn is None else at + lax.rem(lat // 2 + turn, 2) * 2
+        if turn is not None:
+            at = at + lax.rem(lat // 2 + turn, 2) * 2
+        return at if core is None else at + lax.rem(lat + core, 2)
 
     def part(n):
-        return pl.ds(begin(n), PIECES[n][2])
+        return pl.ds(begin(n), PIECES[n][3])
 
     def piece_copy(n, i):
         to = lax.rem(lev + i, levs)
@@ -364,7 +366,7 @@
     move_ref[...] = (from_lane == wanted).astype(F32).astype(BF16)
 
     def place_last(n):
-        size = PIECES[n][2]
+        size = PIECES[n][3]
         many = 4 * size
         hi, lo = split(z_ref[:, part(n)].reshape(8 * many, 128))
         moved = dot(jnp.concatenate([hi, lo], axis=1), move_ref[...])
@@ -401,12 +403,14 @@
         z_ref[:, n] = z.reshape(8, 4, 128)
 
     arrivals = [8] + list(range(8))
-    for n, (d, turn, size) in enumerate(PIECES):
-        if turn != 1:
-            fetches[2 * d].wait()
-            fetches[2 * d + 1].wait()
+    fetched = set()
+    for n, (d, turn, core, size) in enumerate(PIECES):
+        for ref in (2 * d, 2 * d + 1) if core is None else (2 * d + core,):
+            if ref not in fetched:
+                fetched.add(ref)
+                fetches[ref].wait()
         for at in range(size):
-            hi, lo = split(unpacked(m_ref[2 * d + at % 2, at // 2 + (turn or 0)]))
+            hi, lo = split(unpacked(m_ref[2 * d + (at % 2 if core is None else core), at // 2 + (turn or 0)]))
             w_ref[0, at] = hi
             w_ref[1, at] = lo
         first = lax.rem(lat // 4 - d + 4, 4) * 4
@@ -414,7 +418,7 @@
         @pl.loop(0, size)
         def _(at):
             steps = at // 2 if turn is None else turn
-            mix(first + lax.rem(lat // 2 + steps, 2) * 2 + lax.rem(lat + at, 2), at)
+            mix(first + lax.rem(lat // 2 + steps, 2) * 2 + lax.rem(lat + at + (core or 0), 2), at)
 
         place_last(n)
         own_copy(n).start()
@@ -483,8 +487,7 @@
         [v[:, 0, :, :128], v[:, 1, :, :128], v[:, 0, :, 128:], v[:, 1, :, 128:], jnp.zeros((levels, 2, 128 - 2 * rest), F32)],
         axis=-1,
     )
-    both = jnp.stack([zonal, meridional])
-    south, north, pair, courant, both = lax.optimization_barrier((south, north, pair, courant, both))
+    south, north, pair, courant = lax.optimization_barrier((south, north, pair, courant))
     shifted = [lax.ppermute(pair, "lat", [(i, (i + 4 * d) % lats) for i in range(lats)]) for d in range(1, 4)]
     other = [(i, i ^ 1) for i in range(lats)]
     dma = pltpu.SemaphoreType.DMA
@@ -510,7 +513,7 @@
         limit=24,
         collective_id=0,
         has_side_effects=True,
-    )(turned, south, north, both, courant, slots)
+    )(turned, south, north, jnp.stack([zonal, meridional]), courant, slots)
     received, pair, shifted = lax.optimization_barrier((received, pair, shifted))
     far = [lax.ppermute(x, "lat", other) for x in [pair] + shifted]
     whole = call(

time: 109 us -> 109 us (level)
  local copies, waits for them, and re-layouts: 3.49 us -> 4.84 us
  waiting for transfers between devices: 9.34 us -> 8.09 us
  Pallas kernels: 72 us -> 70.9 us
    ppermute x1, waiting for transfers between devices: 4.85 us -> 3.66 us  [body(): across = lax.ppermute(own, 'lat', [(i, i ^ 2) for i in range(lats)])]
  transfers between devices with their start and end apart: 10 -> 10, of which waited for: 6 -> 6; matrix products, arithmetic and copies ran while one was open for 6% -> 8% of each run, Pallas kernels for 39% -> 38%
where the time goes in v10:
time: 109 us; the launch traced here: 107 us
  Pallas kernels  70.9 us (65%)
  starting transfers between devices  18.5 us (17%)
  waiting for transfers between devices  8.09 us (7%)
  local copies, waits for them, and re-layouts  4.84 us (4%)
  other arithmetic  4.77 us (4%)
    pallas_call x1, Pallas kernels, body(): call(functools.partial(forth_kernel, rest, groups), (9, lats, groups, 4,...  38.8 us
    pallas_call x1, Pallas kernels, body(): call(functools.partial(back_kernel, rest, groups, order), (trac, levs_her...  30.1 us
    ppermute x1, starting transfers between devices, body(): lax.ppermute(jnp.concatenate([turned[:3].reshape(3 * levs_here, trac, wid...  6.03 us
    ppermute x4, waiting for transfers between devices, body(): far = [lax.ppermute(x, 'lat', other) for x in [pair] + shifted]  4.19 us
    ppermute x1, starting transfers between devices, body(): across = lax.ppermute(own, 'lat', [(i, i ^ 2) for i in range(lats)])  3.88 us
    ppermute x3, starting transfers between devices, body(): lax.ppermute(pair, 'lat', [(i, (i + 4 * d) % lats) for i in range(lats)])  3.86 us
    ppermute x1, waiting for transfers between devices, body(): across = lax.ppermute(own, 'lat', [(i, i ^ 2) for i in range(lats)])  3.66 us
    ppermute x4, starting transfers between devices, body(): far = [lax.ppermute(x, 'lat', other) for x in [pair] + shifted]  2.67 us
  transfers between devices with their start and end apart: 10, of which 6 were waited for; matrix products, arithmetic and copies ran while one was open for 8% of the time, Pallas kernels for 38%

profile of v10, /device:TPU:24, one launch (start us, length us, event | category | flops | bytes accessed | tf_op | source)
XLA Modules:
  0.0 107.4 jit_solution(15989682837831460668)
XLA Ops:
  0.0 0.0 slice-start
  0.0 3.9 %collective-permute-start.2 = (f32[288,288]{1,0:T(8,128)}, f32[288,288]{1,0:T(8,128)}, u32[]{:S(2)}, u32[]{:S(2)}) collective-permute-start(f32[288,288]{1,0:T(8,128)} %bitcast.31), channel_id=1, source_target_pairs={{0,16},{8,24},{16,0},{24,8},{32,48},{40,56},{48,32},{56,40},{64,80... | collective-permute-start | bytes 995336 | tf_op jit(solution)/shard_map/ppermute | solution.py:469
  3.9 1.5 %copy.38 = f32[4,9,4,1440]{3,0,1,2:T(4,128)S(1)} copy(f32[4,9,4,1440]{3,2,1,0:T(4,128)} %param.6) | data formatting | bytes 1658880 | tf_op args[0]
  5.4 0.0 copy-start.3
  5.4 1.0 fusion.6
  6.4 0.0 copy-start.1
  6.4 2.0 %collective-permute-start = (f32[3,9,4,1440]{3,2,1,0:T(4,128)}, f32[3,9,4,1440]{3,2,1,0:T(4,128)S(1)}, u32[]{:S(2)}, u32[]{:S(2)}) collective-permute-start(f32[3,9,4,1440]{3,2,1,0:T(4,128)} %get-tuple-element.28), channel_id=1, source_target_pairs={{0,8},{8,16},{16,24},{24,32},{32,40},{40,48},{48,56},{56,64},{64,7... | collective-permute-start | bytes 1866248 | tf_op jit(solution)/shard_map/ppermute | solution.py:473
  8.4 0.0 slice-done
  8.5 1.0 pad_maximum_fusion.1
  9.6 6.0 %collective-permute-start.1 = (f32[30,4,1440]{2,1,0:T(4,128)}, f32[30,4,1440]{2,1,0:T(4,128)S(1)}, u32[]{:S(2)}, u32[]{:S(2)}) collective-permute-start(f32[30,4,1440]{2,1,0:T(4,128)} %pad_maximum_fusion.1), channel_id=1, source_target_pairs={{8,0},{16,8},{24,16},{32,24},{40,32},{48,40},{56,48},{64,56},{72,6... | collective-permute-start | bytes 2073608 | tf_op jit(solution)/shard_map/ppermute | solution.py:475
  15.6 0.0 copy-done.3
  15.6 0.1 copy.17
  15.7 0.1 copy_bitcast_fusion.4
  15.8 0.0 copy-start.4
  15.8 0.0 copy-start.2
  15.8 0.7 copy_bitcast_fusion.2
  16.6 1.3 %concatenate.7.c_ref = f32[72,2,384]{2,1,0:T(2,128)S(1)} concatenate(f32[72,2,128]{2,1,0:T(2,128)S(1)} %get-tuple-element.34, f32[72,2,128]{2,1,0:T(2,128)S(1)} %get-tuple-element.33, f32[72,2,52]{2,1,0:T(2,128)} %get-tuple-element.36, f32[72,2,52]{2,1,0:T(2,128)S(1)} %get-tuple-element.35, f32[72,2,24]{2,1,0:T(2,128)S(1)} %broadcast_in_dim.2), dimensions={2} | concatenate | bytes 442368 | tf_op jit(solution)/shard_map/concatenate | solution.py:486
  17.8 3.7 %collective-permute-done.2 = f32[288,288]{1,0:T(8,128)} collective-permute-done((f32[288,288]{1,0:T(8,128)}, f32[288,288]{1,0:T(8,128)}, u32[]{:S(2)}, u32[]{:S(2)}) %collective-permute-start.2) | collective-permute-done | bytes 331808 | tf_op jit(solution)/shard_map/ppermute | solution.py:469
  21.5 0.0 copy-done.1
  21.5 1.1 %pad_maximum_fusion.m_ref = f32[2,288,288]{2,1,0:T(8,128)S(1)} fusion(f32[1,288,288]{2,1,0:T(8,128)} %bitcast.5, f32[1,288,288]{2,1,0:T(8,128)S(1)} %bitcast.32), kind=kLoop, calls=%fused_computation | loop fusion | flops 165888 | bytes 1327104 | tf_op jit(solution)/shard_map/stack | solution.py:478
  22.6 2.1 %shard_map.64.n0 = f32[2,648,128]{2,1,0:T(8,128)S(1)} custom-call(f32[2,288,288]{2,1,0:T(8,128)S(1)} %pad_maximum_fusion.m_ref), custom_call_target="tpu_custom_call" | custom-call | tf_op jit(solution)/shard_map/pallas_call | solution.py:478
  24.7 0.0 collective-permute-done.south_ref
  24.7 0.2 collective-permute-done.1.north_ref
  24.9 0.7 collective-permute-start.5
  25.7 0.5 collective-permute-start.4
  26.2 2.6 %collective-permute-start.3 = (f32[2,648,128]{2,1,0:T(8,128)S(1)}, f32[2,648,128]{2,1,0:T(8,128)}, u32[]{:S(2)}, u32[]{:S(2)}) collective-permute-start(f32[2,648,128]{2,1,0:T(8,128)S(1)} %shard_map.64.n0), channel_id=1, source_target_pairs={{0,32},{8,40},{16,48},{24,56},{32,64},{40,72},{48,80},{56,88},{64,... | collective-permute-start | bytes 1990664 | tf_op jit(solution)/shard_map/ppermute | solution.py:491
  28.8 0.0 copy-done.4
  28.8 0.1 copy.22
  28.9 0.4 convert_reduce_fusion
  29.4 0.0 copy-done.2
  29.4 1.0 pad_maximum_fusion.2.both_ref
  30.4 38.8 %shard_map.65 = (f32[9,16,8,4,128]{4,3,2,1,0:T(4,128)S(1)}, s32[8,4,256]{2,1,0:T(4,128)S(1)}) custom-call(f32[4,9,4,1440]{3,2,1,0:T(4,128)S(1)} %bitcast.27, f32[3,9,4,1440]{3,2,1,0:T(4,128)S(1)} %collective-permute-done.south_ref, f32[30,4,1440]{2,1,0:T(4,128)S(1)} %collective-permute-done.1.north_ref, f32[2,9,4,1440]{3,2,1,0:T(4,128)S(1)} %pad_maximum_fusion.2.both_ref, ...), custom_call_target="tpu_custom_call" | custom-call | tf_op jit(solution)/shard_map/pallas_call | solution.py:495
  69.3 0.0 collective-permute-done.5.n3
  69.3 0.0 collective-permute-done.4.n2
  69.3 0.0 collective-permute-done.3.n1
  69.3 2.1 %collective-permute-start.6 = (f32[2,648,128]{2,1,0:T(8,128)S(1)}, f32[2,648,128]{2,1,0:T(8,128)S(1)}, u32[]{:S(2)}, u32[]{:S(2)}) collective-permute-start(f32[2,648,128]{2,1,0:T(8,128)S(1)} %shard_map.64.n0), channel_id=1, source_target_pairs={{0,8},{8,0},{16,24},{24,16},{32,40},{40,32},{48,56},{56,48},{64,72... | collective-permute-start | bytes 1990664 | tf_op jit(solution)/shard_map/ppermute | solution.py:518
  71.4 0.1 collective-permute-start.7
  71.5 0.4 collective-permute-start.8
  71.9 0.1 collective-permute-start.9
  72.0 1.1 %collective-permute-done.6.f0 = f32[2,648,128]{2,1,0:T(8,128)S(1)} collective-permute-done((f32[2,648,128]{2,1,0:T(8,128)S(1)}, f32[2,648,128]{2,1,0:T(8,128)S(1)}, u32[]{:S(2)}, u32[]{:S(2)}) %collective-permute-start.6) | collective-permute-done | bytes 663584 | tf_op jit(solution)/shard_map/ppermute | solution.py:518
  73.1 1.1 %collective-permute-done.7.f1 = f32[2,648,128]{2,1,0:T(8,128)S(1)} collective-permute-done((f32[2,648,128]{2,1,0:T(8,128)}, f32[2,648,128]{2,1,0:T(8,128)S(1)}, u32[]{:S(2)}, u32[]{:S(2)}) %collective-permute-start.7) | collective-permute-done | bytes 663584 | tf_op jit(solution)/shard_map/ppermute | solution.py:518
  74.3 0.9 collective-permute-done.8.f2
  75.2 0.9 collective-permute-done.9.f3
  76.2 0.0 copy-start
  76.2 30.1 %shard_map.66 = f32[4,9,4,1440]{3,2,1,0:T(4,128)S(1)} custom-call(f32[9,16,8,4,128]{4,3,2,1,0:T(4,128)S(1)} %get-tuple-element.21.r_ref, f32[2,648,128]{2,1,0:T(8,128)S(1)} %shard_map.64.n0, f32[2,648,128]{2,1,0:T(8,128)} %collective-permute-done.3.n1, f32[2,648,128]{2,1,0:T(8,128)} %collective-permute-done.4.n2, f32[2,648,128]{2,1,0:T(8,128)} %collective-permute-done.5.n3, ...), custom_call_target="tpu_custom_call" | custom-call | tf_op jit(solution)/shard_map/pallas_call | solution.py:519
  106.2 0.0 copy-done
  106.2 1.1 %sub.10 = f32[4,9,4,1440]{3,2,1,0:T(4,128)} subtract(f32[4,9,4,1440]{3,2,1,0:T(4,128)S(1)} %shard_map.66, f32[4,9,4,1440]{3,2,1,0:T(4,128)S(1)} %copy-done) | non-fusion elementwise | flops 207360 | bytes 2488320 | tf_op jit(solution)/shard_map/sub | solution.py:542
  (10 shorter events, 0.1 us)
Async XLA Ops:
  0.0 8.4 %slice-start = ((f32[9,4,1440]{2,1,0:T(4,128)}), f32[9,1,1440]{2,1,0:T(1,128)S(1)}, s32[]{:S(2)}) async-start(f32[9,4,1440]{2,1,0:T(4,128)} %param.8), calls=%async_computation | async-start | bytes 110592 | tf_op jit(solution)/shard_map/slice | solution.py:474
  0.0 21.5 %collective-permute-start.2 = (f32[288,288]{1,0:T(8,128)}, f32[288,288]{1,0:T(8,128)}, u32[]{:S(2)}, u32[]{:S(2)}) collective-permute-start(f32[288,288]{1,0:T(8,128)} %bitcast.31), channel_id=1, source_target_pairs={{0,16},{8,24},{16,0},{24,8},{32,48},{40,56},{48,32},{56,40},{64,80... | collective-permute-start | bytes 995336 | tf_op jit(solution)/shard_map/ppermute | solution.py:469
  5.4 10.2 %copy-start.3 = (f32[72,4,180]{2,1,0:T(4,128)S(1)}, f32[72,4,180]{2,1,0:T(4,128)}, u32[]{:S(2)}) copy-start(f32[72,4,180]{2,1,0:T(4,128)} %param.9) | copy-start | bytes 622084
  6.4 15.1 %copy-start.1 = (f32[1,1,288,288]{3,2,1,0:T(8,128)S(1)}, f32[1,1,288,288]{3,2,1,0:T(8,128)}, u32[]{:S(2)}) copy-start(f32[1,1,288,288]{3,2,1,0:T(8,128)} %param.11) | copy-start | bytes 995332
  6.4 18.3 %collective-permute-start = (f32[3,9,4,1440]{3,2,1,0:T(4,128)}, f32[3,9,4,1440]{3,2,1,0:T(4,128)S(1)}, u32[]{:S(2)}, u32[]{:S(2)}) collective-permute-start(f32[3,9,4,1440]{3,2,1,0:T(4,128)} %get-tuple-element.28), channel_id=1, source_target_pairs={{0,8},{8,16},{16,24},{24,32},{32,40},{40,48},{48,56},{56,64},{64,7... | collective-permute-start | bytes 1866248 | tf_op jit(solution)/shard_map/ppermute | solution.py:473
  9.6 15.4 %collective-permute-start.1 = (f32[30,4,1440]{2,1,0:T(4,128)}, f32[30,4,1440]{2,1,0:T(4,128)S(1)}, u32[]{:S(2)}, u32[]{:S(2)}) collective-permute-start(f32[30,4,1440]{2,1,0:T(4,128)} %pad_maximum_fusion.1), channel_id=1, source_target_pairs={{8,0},{16,8},{24,16},{32,24},{40,32},{48,40},{56,48},{64,56},{72,6... | collective-permute-start | bytes 2073608 | tf_op jit(solution)/shard_map/ppermute | solution.py:475
  15.8 13.0 %copy-start.4 = (s32[4,180,1]{1,2,0:T(1,128)S(1)}, s32[4,180,1]{1,2,0:T(1,128)}, u32[]{:S(2)}) copy-start(s32[4,180,1]{1,2,0:T(1,128)} %param.10) | copy-start | bytes 8644
  15.8 13.6 %copy-start.2 = (f32[9,4,1440]{2,1,0:T(4,128)S(1)}, f32[9,4,1440]{2,1,0:T(4,128)}, u32[]{:S(2)}) copy-start(f32[9,4,1440]{2,1,0:T(4,128)} %param.8) | copy-start | bytes 622084
  24.9 44.4 %collective-permute-start.5 = (f32[2,648,128]{2,1,0:T(8,128)S(1)}, f32[2,648,128]{2,1,0:T(8,128)}, u32[]{:S(2)}, u32[]{:S(2)}) collective-permute-start(f32[2,648,128]{2,1,0:T(8,128)S(1)} %shard_map.64.n0), channel_id=1, source_target_pairs={{0,96},{8,104},{16,112},{24,120},{32,0},{40,8},{48,16},{56,24},{64... | collective-permute-start | bytes 1990664 | tf_op jit(solution)/shard_map/ppermute | solution.py:491
  25.7 43.6 %collective-permute-start.4 = (f32[2,648,128]{2,1,0:T(8,128)S(1)}, f32[2,648,128]{2,1,0:T(8,128)}, u32[]{:S(2)}, u32[]{:S(2)}) collective-permute-start(f32[2,648,128]{2,1,0:T(8,128)S(1)} %shard_map.64.n0), channel_id=1, source_target_pairs={{0,64},{8,72},{16,80},{24,88},{32,96},{40,104},{48,112},{56,120},{... | collective-permute-start | bytes 1990664 | tf_op jit(solution)/shard_map/ppermute | solution.py:491
  26.2 43.1 %collective-permute-start.3 = (f32[2,648,128]{2,1,0:T(8,128)S(1)}, f32[2,648,128]{2,1,0:T(8,128)}, u32[]{:S(2)}, u32[]{:S(2)}) collective-permute-start(f32[2,648,128]{2,1,0:T(8,128)S(1)} %shard_map.64.n0), channel_id=1, source_target_pairs={{0,32},{8,40},{16,48},{24,56},{32,64},{40,72},{48,80},{56,88},{64,... | collective-permute-start | bytes 1990664 | tf_op jit(solution)/shard_map/ppermute | solution.py:491
  69.3 3.8 %collective-permute-start.6 = (f32[2,648,128]{2,1,0:T(8,128)S(1)}, f32[2,648,128]{2,1,0:T(8,128)S(1)}, u32[]{:S(2)}, u32[]{:S(2)}) collective-permute-start(f32[2,648,128]{2,1,0:T(8,128)S(1)} %shard_map.64.n0), channel_id=1, source_target_pairs={{0,8},{8,0},{16,24},{24,16},{32,40},{40,32},{48,56},{56,48},{64,72... | collective-permute-start | bytes 1990664 | tf_op jit(solution)/shard_map/ppermute | solution.py:518
  71.4 2.9 %collective-permute-start.7 = (f32[2,648,128]{2,1,0:T(8,128)}, f32[2,648,128]{2,1,0:T(8,128)S(1)}, u32[]{:S(2)}, u32[]{:S(2)}) collective-permute-start(f32[2,648,128]{2,1,0:T(8,128)} %collective-permute-done.3.n1), channel_id=1, source_target_pairs={{0,8},{8,0},{16,24},{24,16},{32,40},{40,32},{48,56},{56,48},{64,72... | collective-permute-start | bytes 1990664 | tf_op jit(solution)/shard_map/ppermute | solution.py:518
  71.5 3.8 %collective-permute-start.8 = (f32[2,648,128]{2,1,0:T(8,128)}, f32[2,648,128]{2,1,0:T(8,128)S(1)}, u32[]{:S(2)}, u32[]{:S(2)}) collective-permute-start(f32[2,648,128]{2,1,0:T(8,128)} %collective-permute-done.4.n2), channel_id=1, source_target_pairs={{0,8},{8,0},{16,24},{24,16},{32,40},{40,32},{48,56},{56,48},{64,72... | collective-permute-start | bytes 1990664 | tf_op jit(solution)/shard_map/ppermute | solution.py:518
  71.9 4.3 %collective-permute-start.9 = (f32[2,648,128]{2,1,0:T(8,128)}, f32[2,648,128]{2,1,0:T(8,128)S(1)}, u32[]{:S(2)}, u32[]{:S(2)}) collective-permute-start(f32[2,648,128]{2,1,0:T(8,128)} %collective-permute-done.5.n3), channel_id=1, source_target_pairs={{0,8},{8,0},{16,24},{24,16},{32,40},{40,32},{48,56},{56,48},{64,72... | collective-permute-start | bytes 1990664 | tf_op jit(solution)/shard_map/ppermute | solution.py:518
  76.2 30.1 %copy-start = (f32[4,9,4,1440]{3,2,1,0:T(4,128)S(1)}, f32[4,9,4,1440]{3,2,1,0:T(4,128)}, u32[]{:S(2)}) copy-start(f32[4,9,4,1440]{3,2,1,0:T(4,128)} %param.6) | copy-start | bytes 2488324

commit v11 on v10

--- a/solution.py
+++ b/solution.py
@@ -274,14 +274,11 @@
     lat, lev = lax.axis_index("lat"), lax.axis_index("lev")
     block = tr_ref.shape[1]
     greet(lat, lev, levs)
-    greeted(levs)
 
     def slot_copy(i):
         to = lax.rem(lev + i, levs)
         return send(slot_ref, all_ref.at[lev], s3.at[i], r3.at[i], lat, to)
 
-    for i in range(1, levs):
-        slot_copy(i).start()
     own_slots = pltpu.make_async_copy(slot_ref, all_ref.at[lev], lsem.at[2])
     own_slots.start()
 
@@ -290,10 +287,13 @@
         return send(g_ref.at[to, k], col_ref.at[lev, k], s1.at[k, i], r1.at[k, i], lat, to)
 
     def level_ready(k):
+        pl.when(k == 0)(lambda: greeted(levs))
         for i in range(1, levs):
             level_copy(k, i).start()
 
     horizontal(tr_ref, south_ref, north_ref, both_ref, g_ref, level_ready)
+    for i in range(1, levs):
+        slot_copy(i).start()
     own = pltpu.make_async_copy(g_ref.at[lev], col_ref.at[lev], lsem.at[0])
     own.start()
     own.wait()

time: 109 us -> 108 us (level)
  Pallas kernels: 70.9 us -> 69.6 us
    pallas_call x1, Pallas kernels: 38.8 us -> 37.5 us  [body(): call(functools.partial(forth_kernel, rest, groups), (9, lats, groups, 4,...]
  transfers between devices with their start and end apart: 10 -> 10, of which waited for: 6 -> 6; matrix products, arithmetic and copies ran while one was open for 8% -> 8% of each run, Pallas kernels for 38% -> 37%
where the time goes in v11:
time: 108 us; the launch traced here: 107 us
  Pallas kernels  69.6 us (64%)
  starting transfers between devices  19 us (18%)
  waiting for transfers between devices  8.09 us (7%)
  local copies, waits for them, and re-layouts  4.84 us (4%)
  other arithmetic  4.77 us (4%)
    pallas_call x1, Pallas kernels, body(): call(functools.partial(forth_kernel, rest, groups), (9, lats, groups, 4,...  37.5 us
    pallas_call x1, Pallas kernels, body(): call(functools.partial(back_kernel, rest, groups, order), (trac, levs_her...  30.1 us
    ppermute x1, starting transfers between devices, body(): lax.ppermute(jnp.concatenate([turned[:3].reshape(3 * levs_here, trac, wid...  6.03 us
    ppermute x4, waiting for transfers between devices, body(): far = [lax.ppermute(x, 'lat', other) for x in [pair] + shifted]  4.19 us
    ppermute x1, starting transfers between devices, body(): across = lax.ppermute(own, 'lat', [(i, i ^ 2) for i in range(lats)])  3.88 us
    ppermute x3, starting transfers between devices, body(): lax.ppermute(pair, 'lat', [(i, (i + 4 * d) % lats) for i in range(lats)])  3.86 us
    ppermute x1, waiting for transfers between devices, body(): across = lax.ppermute(own, 'lat', [(i, i ^ 2) for i in range(lats)])  3.66 us
    ppermute x4, starting transfers between devices, body(): far = [lax.ppermute(x, 'lat', other) for x in [pair] + shifted]  3.19 us
  transfers between devices with their start and end apart: 10, of which 6 were waited for; matrix products, arithmetic and copies ran while one was open for 8% of the time, Pallas kernels for 37%

profile of v11, /device:TPU:24, one launch (start us, length us, event | category | flops | bytes accessed | tf_op | source)
XLA Modules:
  0.0 106.6 jit_solution(4794757342810829998)
XLA Ops:
  0.0 0.0 slice-start
  0.0 3.9 %collective-permute-start.2 = (f32[288,288]{1,0:T(8,128)}, f32[288,288]{1,0:T(8,128)}, u32[]{:S(2)}, u32[]{:S(2)}) collective-permute-start(f32[288,288]{1,0:T(8,128)} %bitcast.31), channel_id=1, source_target_pairs={{0,16},{8,24},{16,0},{24,8},{32,48},{40,56},{48,32},{56,40},{64,80... | collective-permute-start | bytes 995336 | tf_op jit(solution)/shard_map/ppermute | solution.py:469
  3.9 1.5 %copy.38 = f32[4,9,4,1440]{3,0,1,2:T(4,128)S(1)} copy(f32[4,9,4,1440]{3,2,1,0:T(4,128)} %param.6) | data formatting | bytes 1658880 | tf_op args[0]
  5.4 0.0 copy-start.3
  5.4 1.0 fusion.6
  6.4 0.0 copy-start.1
  6.4 2.0 %collective-permute-start = (f32[3,9,4,1440]{3,2,1,0:T(4,128)}, f32[3,9,4,1440]{3,2,1,0:T(4,128)S(1)}, u32[]{:S(2)}, u32[]{:S(2)}) collective-permute-start(f32[3,9,4,1440]{3,2,1,0:T(4,128)} %get-tuple-element.28), channel_id=1, source_target_pairs={{0,8},{8,16},{16,24},{24,32},{32,40},{40,48},{48,56},{56,64},{64,7... | collective-permute-start | bytes 1866248 | tf_op jit(solution)/shard_map/ppermute | solution.py:473
  8.4 0.0 slice-done
  8.5 1.0 pad_maximum_fusion.1
  9.6 6.0 %collective-permute-start.1 = (f32[30,4,1440]{2,1,0:T(4,128)}, f32[30,4,1440]{2,1,0:T(4,128)S(1)}, u32[]{:S(2)}, u32[]{:S(2)}) collective-permute-start(f32[30,4,1440]{2,1,0:T(4,128)} %pad_maximum_fusion.1), channel_id=1, source_target_pairs={{8,0},{16,8},{24,16},{32,24},{40,32},{48,40},{56,48},{64,56},{72,6... | collective-permute-start | bytes 2073608 | tf_op jit(solution)/shard_map/ppermute | solution.py:475
  15.6 0.0 copy-done.3
  15.6 0.1 copy.17
  15.7 0.1 copy_bitcast_fusion.4
  15.8 0.0 copy-start.4
  15.8 0.0 copy-start.2
  15.8 0.7 copy_bitcast_fusion.2
  16.6 1.3 %concatenate.7.c_ref = f32[72,2,384]{2,1,0:T(2,128)S(1)} concatenate(f32[72,2,128]{2,1,0:T(2,128)S(1)} %get-tuple-element.34, f32[72,2,128]{2,1,0:T(2,128)S(1)} %get-tuple-element.33, f32[72,2,52]{2,1,0:T(2,128)} %get-tuple-element.36, f32[72,2,52]{2,1,0:T(2,128)S(1)} %get-tuple-element.35, f32[72,2,24]{2,1,0:T(2,128)S(1)} %broadcast_in_dim.2), dimensions={2} | concatenate | bytes 442368 | tf_op jit(solution)/shard_map/concatenate | solution.py:486
  17.8 3.7 %collective-permute-done.2 = f32[288,288]{1,0:T(8,128)} collective-permute-done((f32[288,288]{1,0:T(8,128)}, f32[288,288]{1,0:T(8,128)}, u32[]{:S(2)}, u32[]{:S(2)}) %collective-permute-start.2) | collective-permute-done | bytes 331808 | tf_op jit(solution)/shard_map/ppermute | solution.py:469
  21.5 0.0 copy-done.1
  21.5 1.1 %pad_maximum_fusion.m_ref = f32[2,288,288]{2,1,0:T(8,128)S(1)} fusion(f32[1,288,288]{2,1,0:T(8,128)} %bitcast.5, f32[1,288,288]{2,1,0:T(8,128)S(1)} %bitcast.32), kind=kLoop, calls=%fused_computation | loop fusion | flops 165888 | bytes 1327104 | tf_op jit(solution)/shard_map/stack | solution.py:478
  22.6 2.1 %shard_map.64.n0 = f32[2,648,128]{2,1,0:T(8,128)S(1)} custom-call(f32[2,288,288]{2,1,0:T(8,128)S(1)} %pad_maximum_fusion.m_ref), custom_call_target="tpu_custom_call" | custom-call | tf_op jit(solution)/shard_map/pallas_call | solution.py:478
  24.7 0.0 collective-permute-done.south_ref
  24.7 0.2 collective-permute-done.1.north_ref
  24.9 0.7 collective-permute-start.5
  25.7 0.5 collective-permute-start.4
  26.2 2.6 %collective-permute-start.3 = (f32[2,648,128]{2,1,0:T(8,128)S(1)}, f32[2,648,128]{2,1,0:T(8,128)}, u32[]{:S(2)}, u32[]{:S(2)}) collective-permute-start(f32[2,648,128]{2,1,0:T(8,128)S(1)} %shard_map.64.n0), channel_id=1, source_target_pairs={{0,32},{8,40},{16,48},{24,56},{32,64},{40,72},{48,80},{56,88},{64,... | collective-permute-start | bytes 1990664 | tf_op jit(solution)/shard_map/ppermute | solution.py:491
  28.8 0.0 copy-done.4
  28.8 0.1 copy.22
  28.9 0.4 convert_reduce_fusion
  29.4 0.0 copy-done.2
  29.4 1.0 pad_maximum_fusion.2.both_ref
  30.4 37.5 %shard_map.65 = (f32[9,16,8,4,128]{4,3,2,1,0:T(4,128)S(1)}, s32[8,4,256]{2,1,0:T(4,128)S(1)}) custom-call(f32[4,9,4,1440]{3,2,1,0:T(4,128)S(1)} %bitcast.27, f32[3,9,4,1440]{3,2,1,0:T(4,128)S(1)} %collective-permute-done.south_ref, f32[30,4,1440]{2,1,0:T(4,128)S(1)} %collective-permute-done.1.north_ref, f32[2,9,4,1440]{3,2,1,0:T(4,128)S(1)} %pad_maximum_fusion.2.both_ref, ...), custom_call_target="tpu_custom_call" | custom-call | tf_op jit(solution)/shard_map/pallas_call | solution.py:495
  68.0 0.0 collective-permute-done.5.n3
  68.0 0.0 collective-permute-done.4.n2
  68.0 0.0 collective-permute-done.3.n1
  68.0 2.6 %collective-permute-start.6 = (f32[2,648,128]{2,1,0:T(8,128)S(1)}, f32[2,648,128]{2,1,0:T(8,128)S(1)}, u32[]{:S(2)}, u32[]{:S(2)}) collective-permute-start(f32[2,648,128]{2,1,0:T(8,128)S(1)} %shard_map.64.n0), channel_id=1, source_target_pairs={{0,8},{8,0},{16,24},{24,16},{32,40},{40,32},{48,56},{56,48},{64,72... | collective-permute-start | bytes 1990664 | tf_op jit(solution)/shard_map/ppermute | solution.py:518
  70.6 0.1 collective-permute-start.7
  70.7 0.4 collective-permute-start.8
  71.1 0.1 collective-permute-start.9
  71.2 1.1 %collective-permute-done.6.f0 = f32[2,648,128]{2,1,0:T(8,128)S(1)} collective-permute-done((f32[2,648,128]{2,1,0:T(8,128)S(1)}, f32[2,648,128]{2,1,0:T(8,128)S(1)}, u32[]{:S(2)}, u32[]{:S(2)}) %collective-permute-start.6) | collective-permute-done | bytes 663584 | tf_op jit(solution)/shard_map/ppermute | solution.py:518
  72.3 1.1 %collective-permute-done.7.f1 = f32[2,648,128]{2,1,0:T(8,128)S(1)} collective-permute-done((f32[2,648,128]{2,1,0:T(8,128)}, f32[2,648,128]{2,1,0:T(8,128)S(1)}, u32[]{:S(2)}, u32[]{:S(2)}) %collective-permute-start.7) | collective-permute-done | bytes 663584 | tf_op jit(solution)/shard_map/ppermute | solution.py:518
  73.5 0.9 collective-permute-done.8.f2
  74.4 0.9 collective-permute-done.9.f3
  75.4 0.0 copy-start
  75.4 30.1 %shard_map.66 = f32[4,9,4,1440]{3,2,1,0:T(4,128)S(1)} custom-call(f32[9,16,8,4,128]{4,3,2,1,0:T(4,128)S(1)} %get-tuple-element.21.r_ref, f32[2,648,128]{2,1,0:T(8,128)S(1)} %shard_map.64.n0, f32[2,648,128]{2,1,0:T(8,128)} %collective-permute-done.3.n1, f32[2,648,128]{2,1,0:T(8,128)} %collective-permute-done.4.n2, f32[2,648,128]{2,1,0:T(8,128)} %collective-permute-done.5.n3, ...), custom_call_target="tpu_custom_call" | custom-call | tf_op jit(solution)/shard_map/pallas_call | solution.py:519
  105.4 0.0 copy-done
  105.4 1.1 %sub.10 = f32[4,9,4,1440]{3,2,1,0:T(4,128)} subtract(f32[4,9,4,1440]{3,2,1,0:T(4,128)S(1)} %shard_map.66, f32[4,9,4,1440]{3,2,1,0:T(4,128)S(1)} %copy-done) | non-fusion elementwise | flops 207360 | bytes 2488320 | tf_op jit(solution)/shard_map/sub | solution.py:542
  (10 shorter events, 0.1 us)
Async XLA Ops:
  0.0 8.4 %slice-start = ((f32[9,4,1440]{2,1,0:T(4,128)}), f32[9,1,1440]{2,1,0:T(1,128)S(1)}, s32[]{:S(2)}) async-start(f32[9,4,1440]{2,1,0:T(4,128)} %param.8), calls=%async_computation | async-start | bytes 110592 | tf_op jit(solution)/shard_map/slice | solution.py:474
  0.0 21.5 %collective-permute-start.2 = (f32[288,288]{1,0:T(8,128)}, f32[288,288]{1,0:T(8,128)}, u32[]{:S(2)}, u32[]{:S(2)}) collective-permute-start(f32[288,288]{1,0:T(8,128)} %bitcast.31), channel_id=1, source_target_pairs={{0,16},{8,24},{16,0},{24,8},{32,48},{40,56},{48,32},{56,40},{64,80... | collective-permute-start | bytes 995336 | tf_op jit(solution)/shard_map/ppermute | solution.py:469
  5.4 10.2 %copy-start.3 = (f32[72,4,180]{2,1,0:T(4,128)S(1)}, f32[72,4,180]{2,1,0:T(4,128)}, u32[]{:S(2)}) copy-start(f32[72,4,180]{2,1,0:T(4,128)} %param.9) | copy-start | bytes 622084
  6.4 15.1 %copy-start.1 = (f32[1,1,288,288]{3,2,1,0:T(8,128)S(1)}, f32[1,1,288,288]{3,2,1,0:T(8,128)}, u32[]{:S(2)}) copy-start(f32[1,1,288,288]{3,2,1,0:T(8,128)} %param.11) | copy-start | bytes 995332
  6.4 18.3 %collective-permute-start = (f32[3,9,4,1440]{3,2,1,0:T(4,128)}, f32[3,9,4,1440]{3,2,1,0:T(4,128)S(1)}, u32[]{:S(2)}, u32[]{:S(2)}) collective-permute-start(f32[3,9,4,1440]{3,2,1,0:T(4,128)} %get-tuple-element.28), channel_id=1, source_target_pairs={{0,8},{8,16},{16,24},{24,32},{32,40},{40,48},{48,56},{56,64},{64,7... | collective-permute-start | bytes 1866248 | tf_op jit(solution)/shard_map/ppermute | solution.py:473
  9.6 15.4 %collective-permute-start.1 = (f32[30,4,1440]{2,1,0:T(4,128)}, f32[30,4,1440]{2,1,0:T(4,128)S(1)}, u32[]{:S(2)}, u32[]{:S(2)}) collective-permute-start(f32[30,4,1440]{2,1,0:T(4,128)} %pad_maximum_fusion.1), channel_id=1, source_target_pairs={{8,0},{16,8},{24,16},{32,24},{40,32},{48,40},{56,48},{64,56},{72,6... | collective-permute-start | bytes 2073608 | tf_op jit(solution)/shard_map/ppermute | solution.py:475
  15.8 13.0 %copy-start.4 = (s32[4,180,1]{1,2,0:T(1,128)S(1)}, s32[4,180,1]{1,2,0:T(1,128)}, u32[]{:S(2)}) copy-start(s32[4,180,1]{1,2,0:T(1,128)} %param.10) | copy-start | bytes 8644
  15.8 13.6 %copy-start.2 = (f32[9,4,1440]{2,1,0:T(4,128)S(1)}, f32[9,4,1440]{2,1,0:T(4,128)}, u32[]{:S(2)}) copy-start(f32[9,4,1440]{2,1,0:T(4,128)} %param.8) | copy-start | bytes 622084
  24.9 43.0 %collective-permute-start.5 = (f32[2,648,128]{2,1,0:T(8,128)S(1)}, f32[2,648,128]{2,1,0:T(8,128)}, u32[]{:S(2)}, u32[]{:S(2)}) collective-permute-start(f32[2,648,128]{2,1,0:T(8,128)S(1)} %shard_map.64.n0), channel_id=1, source_target_pairs={{0,96},{8,104},{16,112},{24,120},{32,0},{40,8},{48,16},{56,24},{64... | collective-permute-start | bytes 1990664 | tf_op jit(solution)/shard_map/ppermute | solution.py:491
  25.7 42.3 %collective-permute-start.4 = (f32[2,648,128]{2,1,0:T(8,128)S(1)}, f32[2,648,128]{2,1,0:T(8,128)}, u32[]{:S(2)}, u32[]{:S(2)}) collective-permute-start(f32[2,648,128]{2,1,0:T(8,128)S(1)} %shard_map.64.n0), channel_id=1, source_target_pairs={{0,64},{8,72},{16,80},{24,88},{32,96},{40,104},{48,112},{56,120},{... | collective-permute-start | bytes 1990664 | tf_op jit(solution)/shard_map/ppermute | solution.py:491
  26.2 41.8 %collective-permute-start.3 = (f32[2,648,128]{2,1,0:T(8,128)S(1)}, f32[2,648,128]{2,1,0:T(8,128)}, u32[]{:S(2)}, u32[]{:S(2)}) collective-permute-start(f32[2,648,128]{2,1,0:T(8,128)S(1)} %shard_map.64.n0), channel_id=1, source_target_pairs={{0,32},{8,40},{16,48},{24,56},{32,64},{40,72},{48,80},{56,88},{64,... | collective-permute-start | bytes 1990664 | tf_op jit(solution)/shard_map/ppermute | solution.py:491
  68.0 4.3 %collective-permute-start.6 = (f32[2,648,128]{2,1,0:T(8,128)S(1)}, f32[2,648,128]{2,1,0:T(8,128)S(1)}, u32[]{:S(2)}, u32[]{:S(2)}) collective-permute-start(f32[2,648,128]{2,1,0:T(8,128)S(1)} %shard_map.64.n0), channel_id=1, source_target_pairs={{0,8},{8,0},{16,24},{24,16},{32,40},{40,32},{48,56},{56,48},{64,72... | collective-permute-start | bytes 1990664 | tf_op jit(solution)/shard_map/ppermute | solution.py:518
  70.6 2.9 %collective-permute-start.7 = (f32[2,648,128]{2,1,0:T(8,128)}, f32[2,648,128]{2,1,0:T(8,128)S(1)}, u32[]{:S(2)}, u32[]{:S(2)}) collective-permute-start(f32[2,648,128]{2,1,0:T(8,128)} %collective-permute-done.3.n1), channel_id=1, source_target_pairs={{0,8},{8,0},{16,24},{24,16},{32,40},{40,32},{48,56},{56,48},{64,72... | collective-permute-start | bytes 1990664 | tf_op jit(solution)/shard_map/ppermute | solution.py:518
  70.7 3.8 %collective-permute-start.8 = (f32[2,648,128]{2,1,0:T(8,128)}, f32[2,648,128]{2,1,0:T(8,128)S(1)}, u32[]{:S(2)}, u32[]{:S(2)}) collective-permute-start(f32[2,648,128]{2,1,0:T(8,128)} %collective-permute-done.4.n2), channel_id=1, source_target_pairs={{0,8},{8,0},{16,24},{24,16},{32,40},{40,32},{48,56},{56,48},{64,72... | collective-permute-start | bytes 1990664 | tf_op jit(solution)/shard_map/ppermute | solution.py:518
  71.1 4.3 %collective-permute-start.9 = (f32[2,648,128]{2,1,0:T(8,128)}, f32[2,648,128]{2,1,0:T(8,128)S(1)}, u32[]{:S(2)}, u32[]{:S(2)}) collective-permute-start(f32[2,648,128]{2,1,0:T(8,128)} %collective-permute-done.5.n3), channel_id=1, source_target_pairs={{0,8},{8,0},{16,24},{24,16},{32,40},{40,32},{48,56},{56,48},{64,72... | collective-permute-start | bytes 1990664 | tf_op jit(solution)/shard_map/ppermute | solution.py:518
  75.4 30.1 %copy-start = (f32[4,9,4,1440]{3,2,1,0:T(4,128)S(1)}, f32[4,9,4,1440]{3,2,1,0:T(4,128)}, u32[]{:S(2)}) copy-start(f32[4,9,4,1440]{3,2,1,0:T(4,128)} %param.6) | copy-start | bytes 2488324
